TPU v7x, 128 devices: a whole 4x4x4 slice. The times are simulated.
128 devices in a mesh: gx: 4 (over x), gy: 4 (over y), gz: 8 (over z, core).
Axes of the slice: x: 4, y: 4, z: 4, core: 2. Of those that a mesh axis runs over, the one named last changes fastest.
Arguments:
- right_side: float32 [32, 256, 1024], P('gx', 'gy', 'gz'), may hold values from -40 to 40
- phase: int32 [32, 256, 1024], P('gx', 'gy', 'gz'), may hold values from 0 to 1
- deflation_weights: float32 [32, 256, 1024], P('gx', 'gy', 'gz'), may hold values from -0.1875 to 0.1875
- coarse_inverse: float32 [8192, 8192], P(('gx', 'gy', 'gz')), may hold values from 0 to 16, as said below
Outputs:
- pressure: float32 [32, 256, 1024], P('gx', 'gy', 'gz')
- residual: float32 [32, 256, 1024], P('gx', 'gy', 'gz')
Inputs may be any that keep to these rules, and one draw needn't show every extreme that they name: `coarse_inverse`: symmetric and positive definite, with nonnegative entries.
All inputs are finite; a program needn't handle non-finite values.
Results may differ from a plain program's by a relative error of at most 0.0003.
Values sent between devices are 32-bit elements; how exact they have to be, the bound alone decides.
No kernel may reach another device: no remote copies, remote signals or barrier semaphores. Data moves between devices by JAX's collectives and lax.ppermute only.
A program may use at most 64 MiB of HBM per device.

v0:
```python
import jax
import jax.numpy as jnp
from jax import lax
from jax.sharding import PartitionSpec as P

SBX = 4
SBY = 4
SBZ = 4
ND = 64
DEG = 6
ITERS = 2


spectrum_low = 0.08
spectrum_high = 2.0


def extended(cells, sides, width):
    for axis, dim in sides:
        count = lax.axis_size(axis)
        ends = count - 1
        head = lax.slice_in_dim(cells, 0, width, axis=dim)
        tail = lax.slice_in_dim(cells, cells.shape[dim] - width, cells.shape[dim], axis=dim)
        cells = jnp.concatenate(
            [
                lax.ppermute(tail, axis, [(i, (i + 1) % count) for i in range(ends)]),
                cells,
                lax.ppermute(head, axis, [((i + 1) % count, i) for i in range(ends)]),
            ],
            axis=dim,
        )
    return cells


def recurrence():
    center = 0.5 * (spectrum_high + spectrum_low)
    half_width = 0.5 * (spectrum_high - spectrum_low)
    ratio = center / half_width
    earlier = 1.0 / ratio
    weights = []
    for index in range(DEG - 1):
        later = 1.0 / (2.0 * ratio - earlier)
        weights.append((later * earlier, 2.0 * later / half_width))
        earlier = later
    return (1.0 / center, weights)


def coefficients(density_pad):
    face_x = 2.0 / (density_pad[1:, 1:-1, 1:-1] + density_pad[:-1, 1:-1, 1:-1])
    face_y = 2.0 / (density_pad[1:-1, 1:, 1:-1] + density_pad[1:-1, :-1, 1:-1])
    face_z = 2.0 / (density_pad[1:-1, 1:-1, 1:] + density_pad[1:-1, 1:-1, :-1])
    diagonal = (
        face_x[:-1]
        + face_x[1:]
        + face_y[:, :-1]
        + face_y[:, 1:]
        + face_z[:, :, :-1]
        + face_z[:, :, 1:]
    )
    return ((face_x, face_y, face_z), diagonal)


def stencil(padded, faces):
    flux_x = faces[0] * (padded[1:, 1:-1, 1:-1] - padded[:-1, 1:-1, 1:-1])
    flux_y = faces[1] * (padded[1:-1, 1:, 1:-1] - padded[1:-1, :-1, 1:-1])
    flux_z = faces[2] * (padded[1:-1, 1:-1, 1:] - padded[1:-1, 1:-1, :-1])
    return (
        flux_x[:-1]
        - flux_x[1:]
        + (flux_y[:, :-1] - flux_y[:, 1:])
        + (flux_z[:, :, :-1] - flux_z[:, :, 1:])
    )


def energy_sum(residual, precond):
    return lax.psum(jnp.sum(residual * precond), ("gx", "gy", "gz"))


def local(right_side, phase, deflation_weights, coarse_inverse):
    first_scale, weights = recurrence()
    cells_x, cells_y, cells_z = right_side.shape
    density = jnp.where(phase == 1, 0.001, 1.0).astype(jnp.float32)
    padded = extended(density, (("gx", 0), ("gy", 1), ("gz", 2)), 1)
    padded = jnp.where(padded == 0.0, 1.0, padded)
    faces, diagonal = coefficients(padded)

    def operate(field):
        padded_field = extended(field, (("gx", 0), ("gy", 1), ("gz", 2)), 1)
        return stencil(padded_field, faces)

    def smooth(residual):
        step = residual / diagonal * first_scale
        result = step
        for keep, push in weights:
            step = keep * step + push * ((residual - operate(result)) / diagonal)
            result = result + step
        return result

    inner_x, inner_y, inner_z = (cells_x // SBX, cells_y // SBY, cells_z // SBZ)

    def deflate(residual):
        blocks = (
            (deflation_weights * residual)
            .reshape(SBX, inner_x, SBY, inner_y, SBZ, inner_z)
            .sum(axis=(1, 3, 5))
            .reshape(ND)
        )
        amounts = jnp.dot(
            coarse_inverse,
            lax.all_gather(blocks, ("gx", "gy", "gz"), axis=0, tiled=True),
            precision=lax.Precision.HIGHEST,
        )
        spread = deflation_weights.reshape(
            SBX, inner_x, SBY, inner_y, SBZ, inner_z
        ) * amounts.reshape(SBX, 1, SBY, 1, SBZ, 1)
        return spread.reshape(cells_x, cells_y, cells_z)

    def precondition(residual):
        return smooth(residual) + deflate(residual)

    pressure = jnp.zeros_like(right_side)
    residual = right_side
    precond = precondition(residual)
    energy = energy_sum(residual, precond)
    direction = precond
    for index in range(ITERS):
        image = operate(direction)
        step_size = energy / lax.psum(jnp.sum(direction * image), ("gx", "gy", "gz"))
        pressure = pressure + step_size * direction
        residual = residual - step_size * image
        if index + 1 < ITERS:
            precond = precondition(residual)
            energy_next = energy_sum(residual, precond)
            direction = precond + energy_next / energy * direction
            energy = energy_next
    return (pressure, residual)


def solution(mesh):
    return jax.shard_map(
        local,
        mesh=mesh,
        in_specs=(
            P("gx", "gy", "gz"),
            P("gx", "gy", "gz"),
            P("gx", "gy", "gz"),
            P(("gx", "gy", "gz"), None),
        ),
        out_specs=(P("gx", "gy", "gz"), P("gx", "gy", "gz")),
        check_vma=False,
    )
```

profile of v0, /device:TPU:1, one launch (start us, length us, event | category | flops | bytes accessed | tf_op | source)
XLA Modules:
  0.0 723.9 jit_solution(4280820555265646652)
XLA Ops:
  3.1 4.6 collective-permute-start
  10.0 4.1 collective-permute-start.2
  15.0 4.9 collective-permute-start.5
  30.8 4.6 collective-permute-start.7
  37.7 4.5 collective-permute-start.9
  43.2 6.1 collective-permute-start.11
  53.7 4.4 collective-permute-done.10
  60.0 4.6 collective-permute-start.13
  66.9 4.5 collective-permute-start.15
  80.3 4.4 collective-permute-done.16
  86.6 4.6 collective-permute-start.19
  93.5 4.5 collective-permute-start.21
  106.9 4.4 collective-permute-done.22
  114.6 4.6 collective-permute-start.25
  122.3 4.5 collective-permute-start.27
  136.8 4.4 collective-permute-done.28
  144.6 4.6 collective-permute-start.31
  153.5 68.5 %all-reduce = f32[8192]{0:T(1024)S(1)} all-reduce(f32[8192]{0:T(1024)S(1)} %dynamic-update-slice), channel_id=1, replica_groups=mesh['gx'=4,'gy'=4,'gz'=8] {'gx','gy','gz'}, use_global_device_ids=true, to_apply=%add | all-reduce | flops 8192 | bytes 65536
  228.8 4.0 collective-permute-start.33
  233.8 4.3 collective-permute-start.35
  242.5 4.4 collective-permute-done.34
  248.9 4.0 collective-permute-start.37
  255.2 4.5 collective-permute-start.39
  268.9 4.4 collective-permute-done.40
  275.2 65.5 %all-reduce.2 = (f32[]{:T(128)}, f32[]{:T(128)}) all-reduce(f32[]{:T(128)} %get-tuple-element.3, f32[]{:T(128)} %get-tuple-element.2), channel_id=1, replica_groups=mesh['gx'=4,'gy'=4,'gz'=8] {'gx','gy','gz'}, use_global_device_ids=true, to_apply=%region_2.3 | all-reduce | flops 2 | bytes 16 | tf_op jit(solution)/shard_map/psum | solution.py:76
  345.3 4.0 collective-permute-start.43
  351.6 4.0 collective-permute-start.45
  356.5 6.4 collective-permute-start.47
  367.4 4.4 collective-permute-done.46
  373.7 4.6 collective-permute-start.49
  380.6 4.5 collective-permute-start.51
  394.0 4.4 collective-permute-done.52
  400.3 4.7 collective-permute-start.55
  407.3 4.5 collective-permute-start.57
  421.0 4.4 collective-permute-done.58
  428.7 4.6 collective-permute-start.61
  437.6 67.5 %all-reduce.1 = f32[8192]{0:T(1024)S(1)} all-reduce(f32[8192]{0:T(1024)S(1)} %dynamic-update-slice.1), channel_id=1, replica_groups=mesh['gx'=4,'gy'=4,'gz'=8] {'gx','gy','gz'}, use_global_device_ids=true, to_apply=%add.1 | all-reduce | flops 8192 | bytes 65536
  507.2 4.0 collective-permute-start.63
  521.2 4.4 collective-permute-done.64
  528.9 4.0 collective-permute-start.67
  540.5 4.5 collective-permute-start.69
  554.7 4.4 collective-permute-done.70
  561.1 65.0 %psum.30 = f32[]{:T(128)} all-reduce(f32[]{:T(128)} %get-tuple-element.8), channel_id=1, replica_groups=mesh['gx'=4,'gy'=4,'gz'=8] {'gx','gy','gz'}, use_global_device_ids=true, to_apply=%region_7.8 | all-reduce | flops 1 | bytes 8 | tf_op jit(solution)/shard_map/psum | solution.py:76
  629.7 4.0 collective-permute-start.73
  636.0 4.0 collective-permute-start.75
  641.0 5.2 collective-permute-start.77
  650.7 4.4 collective-permute-done.76
  656.2 64.5 %psum.31 = f32[]{:T(128)} all-reduce(f32[]{:T(128)} %get-tuple-element.6), channel_id=1, replica_groups=mesh['gx'=4,'gy'=4,'gz'=8] {'gx','gy','gz'}, use_global_device_ids=true, to_apply=%region_9.10 | all-reduce | flops 1 | bytes 8 | tf_op jit(solution)/shard_map/psum | solution.py:128
  (289 shorter events, 193.3 us)
Async XLA Ops:
  1.8 5.9 collective-permute-start.1
  15.0 11.7 %collective-permute-start.5 = (f32[10,66,1]{2,1,0:T(8,128)S(1)}, f32[10,66,1]{2,1,0:T(8,128)S(1)}, u32[]{:S(2)}, u32[]{:S(2)}) collective-permute-start(f32[10,66,1]{2,1,0:T(8,128)S(1)} %get-tuple-element.56), channel_id=1, source_target_pairs={{1,0},{2,1},{3,2},{4,3},{5,4},{6,5},{7,6},{9,8},{10,9},{11,10},{12... | collective-permute-start | bytes 7928 | tf_op jit(solution)/shard_map/ppermute | solution.py:28
  20.0 8.0 %collective-permute-start.4 = (f32[10,66,1]{2,1,0:T(8,128)S(1)}, f32[10,66,1]{2,1,0:T(8,128)S(1)}, u32[]{:S(2)}, u32[]{:S(2)}) collective-permute-start(f32[10,66,1]{2,1,0:T(8,128)S(1)} %get-tuple-element.55), channel_id=1, source_target_pairs={{0,1},{1,2},{2,3},{3,4},{4,5},{5,6},{6,7},{8,9},{9,10},{10,11},{11... | collective-permute-start | bytes 7928 | tf_op jit(solution)/shard_map/ppermute | solution.py:26
  29.5 5.9 collective-permute-start.6
  36.4 6.1 collective-permute-start.8
  43.2 10.5 %collective-permute-start.11 = (f32[10,66,1]{2,1,0:T(8,128)S(1)}, f32[10,66,1]{2,1,0:T(8,128)S(1)}, u32[]{:S(2)}, u32[]{:S(2)}) collective-permute-start(f32[10,66,1]{2,1,0:T(8,128)S(1)} %get-tuple-element.54), channel_id=1, source_target_pairs={{0,1},{1,2},{2,3},{3,4},{4,5},{5,6},{6,7},{8,9},{9,10},{10,11},{11... | collective-permute-start | bytes 7928 | tf_op jit(solution)/shard_map/ppermute | solution.py:26
  49.3 8.8 %collective-permute-start.10 = (f32[10,66,1]{2,1,0:T(8,128)S(1)}, f32[10,66,1]{2,1,0:T(8,128)S(1)}, u32[]{:S(2)}, u32[]{:S(2)}) collective-permute-start(f32[10,66,1]{2,1,0:T(8,128)S(1)} %get-tuple-element.53), channel_id=1, source_target_pairs={{1,0},{2,1},{3,2},{4,3},{5,4},{6,5},{7,6},{9,8},{10,9},{11,10},{12... | collective-permute-start | bytes 7928 | tf_op jit(solution)/shard_map/ppermute | solution.py:28
  58.7 5.9 collective-permute-start.12
  65.6 6.1 collective-permute-start.14
  72.4 7.9 %collective-permute-start.17 = (f32[10,66,1]{2,1,0:T(8,128)S(1)}, f32[10,66,1]{2,1,0:T(8,128)S(1)}, u32[]{:S(2)}, u32[]{:S(2)}) collective-permute-start(f32[10,66,1]{2,1,0:T(8,128)S(1)} %get-tuple-element.52), channel_id=1, source_target_pairs={{0,1},{1,2},{2,3},{3,4},{4,5},{5,6},{6,7},{8,9},{9,10},{10,11},{11... | collective-permute-start | bytes 7928 | tf_op jit(solution)/shard_map/ppermute | solution.py:26
  75.8 8.8 %collective-permute-start.16 = (f32[10,66,1]{2,1,0:T(8,128)S(1)}, f32[10,66,1]{2,1,0:T(8,128)S(1)}, u32[]{:S(2)}, u32[]{:S(2)}) collective-permute-start(f32[10,66,1]{2,1,0:T(8,128)S(1)} %get-tuple-element.51), channel_id=1, source_target_pairs={{1,0},{2,1},{3,2},{4,3},{5,4},{6,5},{7,6},{9,8},{10,9},{11,10},{12... | collective-permute-start | bytes 7928 | tf_op jit(solution)/shard_map/ppermute | solution.py:28
  85.3 5.9 collective-permute-start.18
  92.2 6.1 collective-permute-start.20
  99.0 7.9 %collective-permute-start.23 = (f32[10,66,1]{2,1,0:T(8,128)S(1)}, f32[10,66,1]{2,1,0:T(8,128)S(1)}, u32[]{:S(2)}, u32[]{:S(2)}) collective-permute-start(f32[10,66,1]{2,1,0:T(8,128)S(1)} %get-tuple-element.50), channel_id=1, source_target_pairs={{0,1},{1,2},{2,3},{3,4},{4,5},{5,6},{6,7},{8,9},{9,10},{10,11},{11... | collective-permute-start | bytes 7928 | tf_op jit(solution)/shard_map/ppermute | solution.py:26
  102.5 8.8 %collective-permute-start.22 = (f32[10,66,1]{2,1,0:T(8,128)S(1)}, f32[10,66,1]{2,1,0:T(8,128)S(1)}, u32[]{:S(2)}, u32[]{:S(2)}) collective-permute-start(f32[10,66,1]{2,1,0:T(8,128)S(1)} %get-tuple-element.49), channel_id=1, source_target_pairs={{1,0},{2,1},{3,2},{4,3},{5,4},{6,5},{7,6},{9,8},{10,9},{11,10},{12... | collective-permute-start | bytes 7928 | tf_op jit(solution)/shard_map/ppermute | solution.py:28
  113.3 5.9 collective-permute-start.24
  121.0 7.1 collective-permute-start.26
  129.3 7.5 %collective-permute-start.29 = (f32[10,66,1]{2,1,0:T(8,128)S(1)}, f32[10,66,1]{2,1,0:T(8,128)S(1)}, u32[]{:S(2)}, u32[]{:S(2)}) collective-permute-start(f32[10,66,1]{2,1,0:T(8,128)S(1)} %get-tuple-element.48), channel_id=1, source_target_pairs={{0,1},{1,2},{2,3},{3,4},{4,5},{5,6},{6,7},{8,9},{9,10},{10,11},{11... | collective-permute-start | bytes 7928 | tf_op jit(solution)/shard_map/ppermute | solution.py:26
  132.3 8.8 %collective-permute-start.28 = (f32[10,66,1]{2,1,0:T(8,128)S(1)}, f32[10,66,1]{2,1,0:T(8,128)S(1)}, u32[]{:S(2)}, u32[]{:S(2)}) collective-permute-start(f32[10,66,1]{2,1,0:T(8,128)S(1)} %get-tuple-element.47), channel_id=1, source_target_pairs={{1,0},{2,1},{3,2},{4,3},{5,4},{6,5},{7,6},{9,8},{10,9},{11,10},{12... | collective-permute-start | bytes 7928 | tf_op jit(solution)/shard_map/ppermute | solution.py:28
  143.3 84.1 %collective-permute-start.30 = (f32[1,64,128]{2,1,0:T(8,128)S(1)}, f32[1,64,128]{2,1,0:T(8,128)S(1)}, u32[]{:S(2)}, u32[]{:S(2)}) collective-permute-start(f32[1,64,128]{2,1,0:T(8,128)S(1)} %get-tuple-element.99), channel_id=1, source_target_pairs={{32,0},{64,32},{96,64},{33,1},{65,33},{97,65},{34,2},{66,34},{98,6... | collective-permute-start | bytes 98312 | tf_op jit(solution)/shard_map/ppermute | solution.py:28
  144.6 82.8 %collective-permute-start.31 = (f32[1,64,128]{2,1,0:T(8,128)S(1)}, f32[1,64,128]{2,1,0:T(8,128)S(1)}, u32[]{:S(2)}, u32[]{:S(2)}) collective-permute-start(f32[1,64,128]{2,1,0:T(8,128)S(1)} %get-tuple-element.98), channel_id=1, source_target_pairs={{0,32},{32,64},{64,96},{1,33},{33,65},{65,97},{2,34},{34,66},{66,9... | collective-permute-start | bytes 98312 | tf_op jit(solution)/shard_map/ppermute | solution.py:26
  233.8 8.7 %collective-permute-start.35 = (f32[10,66,1]{2,1,0:T(8,128)S(1)}, f32[10,66,1]{2,1,0:T(8,128)S(1)}, u32[]{:S(2)}, u32[]{:S(2)}) collective-permute-start(f32[10,66,1]{2,1,0:T(8,128)S(1)} %get-tuple-element.46), channel_id=1, source_target_pairs={{0,1},{1,2},{2,3},{3,4},{4,5},{5,6},{6,7},{8,9},{9,10},{10,11},{11... | collective-permute-start | bytes 7928 | tf_op jit(solution)/shard_map/ppermute | solution.py:26
  238.1 8.8 %collective-permute-start.34 = (f32[10,66,1]{2,1,0:T(8,128)S(1)}, f32[10,66,1]{2,1,0:T(8,128)S(1)}, u32[]{:S(2)}, u32[]{:S(2)}) collective-permute-start(f32[10,66,1]{2,1,0:T(8,128)S(1)} %get-tuple-element.45), channel_id=1, source_target_pairs={{1,0},{2,1},{3,2},{4,3},{5,4},{6,5},{7,6},{9,8},{10,9},{11,10},{12... | collective-permute-start | bytes 7928 | tf_op jit(solution)/shard_map/ppermute | solution.py:28
  253.9 6.1 collective-permute-start.38
  260.7 8.2 %collective-permute-start.41 = (f32[10,66,1]{2,1,0:T(8,128)S(1)}, f32[10,66,1]{2,1,0:T(8,128)S(1)}, u32[]{:S(2)}, u32[]{:S(2)}) collective-permute-start(f32[10,66,1]{2,1,0:T(8,128)S(1)} %get-tuple-element.44), channel_id=1, source_target_pairs={{0,1},{1,2},{2,3},{3,4},{4,5},{5,6},{6,7},{8,9},{9,10},{10,11},{11... | collective-permute-start | bytes 7928 | tf_op jit(solution)/shard_map/ppermute | solution.py:26
  264.5 8.8 %collective-permute-start.40 = (f32[10,66,1]{2,1,0:T(8,128)S(1)}, f32[10,66,1]{2,1,0:T(8,128)S(1)}, u32[]{:S(2)}, u32[]{:S(2)}) collective-permute-start(f32[10,66,1]{2,1,0:T(8,128)S(1)} %get-tuple-element.43), channel_id=1, source_target_pairs={{1,0},{2,1},{3,2},{4,3},{5,4},{6,5},{7,6},{9,8},{10,9},{11,10},{12... | collective-permute-start | bytes 7928 | tf_op jit(solution)/shard_map/ppermute | solution.py:28
  356.5 10.9 %collective-permute-start.47 = (f32[10,66,1]{2,1,0:T(8,128)S(1)}, f32[10,66,1]{2,1,0:T(8,128)S(1)}, u32[]{:S(2)}, u32[]{:S(2)}) collective-permute-start(f32[10,66,1]{2,1,0:T(8,128)S(1)} %get-tuple-element.42), channel_id=1, source_target_pairs={{0,1},{1,2},{2,3},{3,4},{4,5},{5,6},{6,7},{8,9},{9,10},{10,11},{11... | collective-permute-start | bytes 7928 | tf_op jit(solution)/shard_map/ppermute | solution.py:26
  363.0 8.8 %collective-permute-start.46 = (f32[10,66,1]{2,1,0:T(8,128)S(1)}, f32[10,66,1]{2,1,0:T(8,128)S(1)}, u32[]{:S(2)}, u32[]{:S(2)}) collective-permute-start(f32[10,66,1]{2,1,0:T(8,128)S(1)} %get-tuple-element.41), channel_id=1, source_target_pairs={{1,0},{2,1},{3,2},{4,3},{5,4},{6,5},{7,6},{9,8},{10,9},{11,10},{12... | collective-permute-start | bytes 7928 | tf_op jit(solution)/shard_map/ppermute | solution.py:28
  372.4 5.9 collective-permute-start.48
  379.3 6.1 collective-permute-start.50
  386.1 7.9 %collective-permute-start.53 = (f32[10,66,1]{2,1,0:T(8,128)S(1)}, f32[10,66,1]{2,1,0:T(8,128)S(1)}, u32[]{:S(2)}, u32[]{:S(2)}) collective-permute-start(f32[10,66,1]{2,1,0:T(8,128)S(1)} %get-tuple-element.40), channel_id=1, source_target_pairs={{0,1},{1,2},{2,3},{3,4},{4,5},{5,6},{6,7},{8,9},{9,10},{10,11},{11... | collective-permute-start | bytes 7928 | tf_op jit(solution)/shard_map/ppermute | solution.py:26
  389.6 8.8 %collective-permute-start.52 = (f32[10,66,1]{2,1,0:T(8,128)S(1)}, f32[10,66,1]{2,1,0:T(8,128)S(1)}, u32[]{:S(2)}, u32[]{:S(2)}) collective-permute-start(f32[10,66,1]{2,1,0:T(8,128)S(1)} %get-tuple-element.39), channel_id=1, source_target_pairs={{1,0},{2,1},{3,2},{4,3},{5,4},{6,5},{7,6},{9,8},{10,9},{11,10},{12... | collective-permute-start | bytes 7928 | tf_op jit(solution)/shard_map/ppermute | solution.py:28
  399.0 6.0 collective-permute-start.54
  406.0 6.1 collective-permute-start.56
  412.8 8.1 %collective-permute-start.59 = (f32[10,66,1]{2,1,0:T(8,128)S(1)}, f32[10,66,1]{2,1,0:T(8,128)S(1)}, u32[]{:S(2)}, u32[]{:S(2)}) collective-permute-start(f32[10,66,1]{2,1,0:T(8,128)S(1)} %get-tuple-element.38), channel_id=1, source_target_pairs={{0,1},{1,2},{2,3},{3,4},{4,5},{5,6},{6,7},{8,9},{9,10},{10,11},{11... | collective-permute-start | bytes 7928 | tf_op jit(solution)/shard_map/ppermute | solution.py:26
  416.5 8.8 %collective-permute-start.58 = (f32[10,66,1]{2,1,0:T(8,128)S(1)}, f32[10,66,1]{2,1,0:T(8,128)S(1)}, u32[]{:S(2)}, u32[]{:S(2)}) collective-permute-start(f32[10,66,1]{2,1,0:T(8,128)S(1)} %get-tuple-element.37), channel_id=1, source_target_pairs={{1,0},{2,1},{3,2},{4,3},{5,4},{6,5},{7,6},{9,8},{10,9},{11,10},{12... | collective-permute-start | bytes 7928 | tf_op jit(solution)/shard_map/ppermute | solution.py:28
  427.4 77.7 %collective-permute-start.60 = (f32[1,64,128]{2,1,0:T(8,128)S(1)}, f32[1,64,128]{2,1,0:T(8,128)S(1)}, u32[]{:S(2)}, u32[]{:S(2)}) collective-permute-start(f32[1,64,128]{2,1,0:T(8,128)S(1)} %get-tuple-element.88), channel_id=1, source_target_pairs={{32,0},{64,32},{96,64},{33,1},{65,33},{97,65},{34,2},{66,34},{98,6... | collective-permute-start | bytes 98312 | tf_op jit(solution)/shard_map/ppermute | solution.py:28
  428.7 76.4 %collective-permute-start.61 = (f32[1,64,128]{2,1,0:T(8,128)S(1)}, f32[1,64,128]{2,1,0:T(8,128)S(1)}, u32[]{:S(2)}, u32[]{:S(2)}) collective-permute-start(f32[1,64,128]{2,1,0:T(8,128)S(1)} %get-tuple-element.87), channel_id=1, source_target_pairs={{0,32},{32,64},{64,96},{1,33},{33,65},{65,97},{2,34},{34,66},{66,9... | collective-permute-start | bytes 98312 | tf_op jit(solution)/shard_map/ppermute | solution.py:26
  505.9 6.6 collective-permute-start.62
  513.7 7.5 %collective-permute-start.65 = (f32[10,66,1]{2,1,0:T(8,128)S(1)}, f32[10,66,1]{2,1,0:T(8,128)S(1)}, u32[]{:S(2)}, u32[]{:S(2)}) collective-permute-start(f32[10,66,1]{2,1,0:T(8,128)S(1)} %get-tuple-element.36), channel_id=1, source_target_pairs={{0,1},{1,2},{2,3},{3,4},{4,5},{5,6},{6,7},{8,9},{9,10},{10,11},{11... | collective-permute-start | bytes 7928 | tf_op jit(solution)/shard_map/ppermute | solution.py:26
  516.8 8.8 %collective-permute-start.64 = (f32[10,66,1]{2,1,0:T(8,128)S(1)}, f32[10,66,1]{2,1,0:T(8,128)S(1)}, u32[]{:S(2)}, u32[]{:S(2)}) collective-permute-start(f32[10,66,1]{2,1,0:T(8,128)S(1)} %get-tuple-element.35), channel_id=1, source_target_pairs={{1,0},{2,1},{3,2},{4,3},{5,4},{6,5},{7,6},{9,8},{10,9},{11,10},{12... | collective-permute-start | bytes 7928 | tf_op jit(solution)/shard_map/ppermute | solution.py:28
  527.7 10.7 %collective-permute-start.66 = (f32[1,64,128]{2,1,0:T(8,128)S(1)}, f32[1,64,128]{2,1,0:T(8,128)S(1)}, u32[]{:S(2)}, u32[]{:S(2)}) collective-permute-start(f32[1,64,128]{2,1,0:T(8,128)S(1)} %get-tuple-element.86), channel_id=1, source_target_pairs={{32,0},{64,32},{96,64},{33,1},{65,33},{97,65},{34,2},{66,34},{98,6... | collective-permute-start | bytes 98312 | tf_op jit(solution)/shard_map/ppermute | solution.py:28
  528.9 9.4 %collective-permute-start.67 = (f32[1,64,128]{2,1,0:T(8,128)S(1)}, f32[1,64,128]{2,1,0:T(8,128)S(1)}, u32[]{:S(2)}, u32[]{:S(2)}) collective-permute-start(f32[1,64,128]{2,1,0:T(8,128)S(1)} %get-tuple-element.85), channel_id=1, source_target_pairs={{0,32},{32,64},{64,96},{1,33},{33,65},{65,97},{2,34},{34,66},{66,9... | collective-permute-start | bytes 98312 | tf_op jit(solution)/shard_map/ppermute | solution.py:26
  539.2 7.1 collective-permute-start.68
  547.5 7.2 collective-permute-start.71
  550.3 8.8 %collective-permute-start.70 = (f32[10,66,1]{2,1,0:T(8,128)S(1)}, f32[10,66,1]{2,1,0:T(8,128)S(1)}, u32[]{:S(2)}, u32[]{:S(2)}) collective-permute-start(f32[10,66,1]{2,1,0:T(8,128)S(1)} %get-tuple-element.33), channel_id=1, source_target_pairs={{1,0},{2,1},{3,2},{4,3},{5,4},{6,5},{7,6},{9,8},{10,9},{11,10},{12... | collective-permute-start | bytes 7928 | tf_op jit(solution)/shard_map/ppermute | solution.py:28
  641.0 9.7 %collective-permute-start.77 = (f32[10,66,1]{2,1,0:T(8,128)S(1)}, f32[10,66,1]{2,1,0:T(8,128)S(1)}, u32[]{:S(2)}, u32[]{:S(2)}) collective-permute-start(f32[10,66,1]{2,1,0:T(8,128)S(1)} %get-tuple-element.32), channel_id=1, source_target_pairs={{0,1},{1,2},{2,3},{3,4},{4,5},{5,6},{6,7},{8,9},{9,10},{10,11},{11... | collective-permute-start | bytes 7928 | tf_op jit(solution)/shard_map/ppermute | solution.py:26
  646.3 8.8 %collective-permute-start.76 = (f32[10,66,1]{2,1,0:T(8,128)S(1)}, f32[10,66,1]{2,1,0:T(8,128)S(1)}, u32[]{:S(2)}, u32[]{:S(2)}) collective-permute-start(f32[10,66,1]{2,1,0:T(8,128)S(1)} %get-tuple-element.31), channel_id=1, source_target_pairs={{1,0},{2,1},{3,2},{4,3},{5,4},{6,5},{7,6},{9,8},{10,9},{11,10},{12... | collective-permute-start | bytes 7928 | tf_op jit(solution)/shard_map/ppermute | solution.py:28
  (54 other events, 680.0 us)
where the time goes:
time: 727 us; the launch traced here: 724 us
  blocking collectives  331 us (46%)
  starting transfers between devices  227 us (31%)
  waiting for transfers between devices  99.6 us (14%)
  other arithmetic  37.8 us (5%)
  local copies, waits for them, and re-layouts  18.4 us (3%)
    ppermute x39, starting transfers between devices, extended(): lax.ppermute(tail, axis, [(i, (i + 1) % count) for i in range(ends)])  166 us
    unnamed x2, blocking collectives  136 us
    psum x2, blocking collectives, energy_sum(): return lax.psum(jnp.sum(residual * precond), ('gx', 'gy', 'gz'))  131 us
    psum x1, blocking collectives, local(): lax.psum(jnp.sum(direction * image), ('gx', 'gy', 'gz'))  64.5 us
    ppermute x39, starting transfers between devices, extended(): lax.ppermute(head, axis, [((i + 1) % count, i) for i in range(ends)])  61.5 us
    ppermute x39, waiting for transfers between devices, extended(): lax.ppermute(head, axis, [((i + 1) % count, i) for i in range(ends)])  56.1 us
    ppermute x39, waiting for transfers between devices, extended(): lax.ppermute(tail, axis, [(i, (i + 1) % count) for i in range(ends)])  43.6 us
  transfers between devices with their start and end apart: 78, of which 46 were waited for; matrix products, arithmetic and copies ran while one was open for 4% of the time, Pallas kernels for 0%

commit v1 on v0

v1 whole, which is shorter than its diff:
```python
import functools

import jax
import jax.numpy as jnp
import numpy as np
from jax import lax
from jax.experimental import pallas as pl
from jax.experimental.pallas import tpu as pltpu
from jax.sharding import PartitionSpec as P

AXES = ("gx", "gy", "gz")
SBX = 4
ND = 64
DEG = 6
spectrum_low = 0.08
spectrum_high = 2.0

CX, CY, CZ = 8, 64, 128
HX, HY = 7, 8
PX, PY, PZ = CX + 2 * HX, CY + 2 * HY, 2 * CZ
H_R, H_G, H_V = 5, 7, 1
N_R, N_G, N_V = CX + 2 * H_R, CX + 2 * H_G, CX + 2 * H_V
N_ALL = N_R + N_G + N_V
GROUPS = -(-N_ALL // 16)
GROUPS_P = -(-PX // 16)
NDEV = 128

LIQUID = np.float32(1.0)
GAS = np.float32(0.001)
F_LL = np.float32(2.0) / (LIQUID + LIQUID)
F_LG = np.float32(2.0) / (LIQUID + GAS)
F_GG = np.float32(2.0) / (GAS + GAS)

F32 = jnp.float32
EXACT = lax.Precision.HIGHEST


def recurrence():
    center = 0.5 * (spectrum_high + spectrum_low)
    half_width = 0.5 * (spectrum_high - spectrum_low)
    ratio = center / half_width
    earlier = 1.0 / ratio
    weights = []
    for index in range(DEG - 1):
        later = 1.0 / (2.0 * ratio - earlier)
        weights.append((later * earlier, 2.0 * later / half_width))
        earlier = later
    return (1.0 / center, weights)


def iota(shape, dim):
    return lax.broadcasted_iota(jnp.int32, shape, dim)


def neighbours(ref, i):
    v = ref[i]
    return (
        ref[i - 1],
        ref[i + 1],
        pltpu.roll(v, 1, 0),
        pltpu.roll(v, PY - 1, 0),
        pltpu.roll(v, 1, 1),
        pltpu.roll(v, PZ - 1, 1),
    )


def inside_yz(pos):
    gy, gz = pos[1], pos[2]
    row = iota((PY, PZ), 0) - HY + gy * CY
    lane = iota((PY, PZ), 1)
    near = jnp.where(lane < CZ + CZ // 2, lane, lane - PZ) + gz * CZ
    kept = (lane < CZ + 8) | (lane >= PZ - 8)
    good = (row >= 0) & (row < 4 * CY) & (near >= 0) & (near < 8 * CZ) & kept
    return jnp.where(good, 1.0, 0.0).astype(F32)


def inside_x(pos, rel):
    x = pos[0] * CX + rel
    return jnp.where((x >= 0) & (x < 4 * CX), 1.0, 0.0).astype(F32)


def pair(labels):
    gas = labels > 0.5
    return jnp.where(gas, F_LG, F_LL), jnp.where(gas, F_GG - F_LG, F_LG - F_LL)


def row_sums(parts):
    rows = []
    for part in parts:
        for sy in range(4):
            rows.append(jnp.sum(part[16 * sy : 16 * sy + 16], axis=0, keepdims=True))
    stacked = jnp.concatenate(rows, axis=0)
    pick = jnp.where(iota((128, 128), 0) // 32 == iota((128, 128), 1) % 4, 1.0, 0.0).astype(F32)
    spread = jnp.dot(stacked, pick, precision=EXACT, preferred_element_type=F32)
    keep = (iota((16, 128), 1) // 4) % 16 == iota((16, 128), 0)
    return jnp.sum(jnp.where(keep, spread, 0.0), axis=0, keepdims=True)


def fields(rows):
    count = len(rows)
    keep = (iota((16, 128), 1) // 4 == iota((16, 128), 0)) & (iota((16, 128), 1) < ND)
    tall = jnp.concatenate([jnp.where(keep, jnp.broadcast_to(r, (16, 128)), 0.0) for r in rows], axis=0)
    pick = jnp.where(iota((128, 128), 0) % 4 == iota((128, 128), 1) // 32, 1.0, 0.0).astype(F32)
    out = jnp.dot(tall, pick, precision=EXACT, preferred_element_type=F32)
    return [out[16 * k : 16 * k + 16] for k in range(count)]


def plane_field(field, sx):
    return jnp.concatenate(
        [jnp.broadcast_to(field[4 * sx + sy : 4 * sx + sy + 1], (16, 128)) for sy in range(4)], axis=0
    )


def coarse_rows(matrix_ref, even, odd):
    wide = jnp.where(iota((64, 128), 1) < ND, even, odd)
    total = matrix_ref[:, 0:128] * wide[0:1]
    for t in range(1, 64):
        total = total + matrix_ref[:, 128 * t : 128 * t + 128] * wide[t : t + 1]
    column = jnp.sum(total, axis=1, keepdims=True)
    keep = iota((64, 128), 1) % ND == iota((64, 128), 0)
    return jnp.sum(jnp.where(keep, column, 0.0), axis=0, keepdims=True)


def total_sum(x):
    return jnp.sum(jnp.sum(x, axis=0, keepdims=True), axis=1, keepdims=True)


def start_kernel(r_ref, phase_ref, v_ref, xl_ref, xr_ref, send_ref):
    parts = []
    for sx in range(4):
        parts.append(r_ref[2 * sx] * v_ref[2 * sx] + r_ref[2 * sx + 1] * v_ref[2 * sx + 1])
    send_ref[...] = jnp.broadcast_to(row_sums(parts), (NDEV, 128))
    xl_ref[0:H_R] = r_ref[0:H_R]
    xr_ref[0:H_R] = r_ref[CX - H_R :]
    xl_ref[H_R : H_R + H_G] = jnp.where(phase_ref[0:H_G] == 1, 1.0, 0.0).astype(F32)
    xr_ref[H_R : H_R + H_G] = jnp.where(phase_ref[CX - H_G :] == 1, 1.0, 0.0).astype(F32)
    xl_ref[H_R + H_G :] = v_ref[0:H_V]
    xr_ref[H_R + H_G :] = v_ref[CX - H_V :]


def stacked_planes(r_ref, phase_ref, v_ref, fl_ref, fr_ref):
    planes = []
    for halo, own, base in ((H_R, "r", 0), (H_G, "g", H_R), (H_V, "v", H_R + H_G)):
        for rel in range(-halo, CX + halo):
            if rel < 0:
                planes.append(lambda s, k=base + rel + halo: fl_ref[k, s])
            elif rel >= CX:
                planes.append(lambda s, k=base + rel - CX: fr_ref[k, s])
            elif own == "r":
                planes.append(lambda s, k=rel: r_ref[k, s])
            elif own == "g":
                planes.append(lambda s, k=rel: jnp.where(phase_ref[k, s] == 1, 1.0, 0.0).astype(F32))
            else:
                planes.append(lambda s, k=rel: v_ref[k, s])
    return planes


def y_kernel(r_ref, phase_ref, v_ref, fl_ref, fr_ref, yl_ref, yr_ref):
    planes = stacked_planes(r_ref, phase_ref, v_ref, fl_ref, fr_ref)
    for k, plane in enumerate(planes):
        yl_ref[k] = plane(pl.ds(0, HY))
        yr_ref[k] = plane(pl.ds(CY - HY, HY))


def pack_lanes(ext_ref, zl_ref, zr_ref, count):
    slot = iota((PY, CZ), 1) // 8
    for group in range(zl_ref.shape[0]):
        left = jnp.zeros((PY, CZ), F32)
        right = jnp.zeros((PY, CZ), F32)
        for m in range(16):
            k = 16 * group + m
            if k >= count:
                break
            plane = ext_ref[k]
            left = jnp.where(slot == m, pltpu.roll(plane, 8 * m, 1) if m else plane, left)
            shift = (8 * m + 8) % CZ
            right = jnp.where(slot == m, pltpu.roll(plane, shift, 1) if shift else plane, right)
        zl_ref[group] = left
        zr_ref[group] = right


def wide_plane(ext_ref, fl_ref, fr_ref, k):
    group, m = k // 16, k % 16
    lane = iota((PY, CZ), 1)
    shift = (CZ - 8 * m) % CZ
    ahead = pltpu.roll(fr_ref[group], shift, 1) if shift else fr_ref[group]
    shift = (CZ - 8 - 8 * m) % CZ
    behind = pltpu.roll(fl_ref[group], shift, 1) if shift else fl_ref[group]
    side = jnp.where(lane < 8, ahead, jnp.where(lane >= CZ - 8, behind, 0.0))
    return jnp.concatenate([ext_ref[k], side], axis=1)


def z_kernel(r_ref, phase_ref, v_ref, fl_ref, fr_ref, yd_ref, yu_ref, ext_ref, zl_ref, zr_ref):
    planes = stacked_planes(r_ref, phase_ref, v_ref, fl_ref, fr_ref)
    for k, plane in enumerate(planes):
        ext_ref[k, 0:HY] = yd_ref[k]
        ext_ref[k, HY : HY + CY] = plane(pl.ds(0, CY))
        ext_ref[k, HY + CY :] = yu_ref[k]
    pack_lanes(ext_ref, zl_ref, zr_ref, N_ALL)


def y2_kernel(p_ref, fl_ref, fr_ref, yl_ref, yr_ref):
    for i in range(PX):
        rel = i - HX
        src, k = (fl_ref, i) if rel < 0 else (fr_ref, rel - CX) if rel >= CX else (p_ref, rel)
        yl_ref[i] = src[k, 0:HY]
        yr_ref[i] = src[k, CY - HY :]


def z2_kernel(p_ref, fl_ref, fr_ref, yd_ref, yu_ref, ext_ref, zl_ref, zr_ref):
    for i in range(PX):
        rel = i - HX
        src, k = (fl_ref, i) if rel < 0 else (fr_ref, rel - CX) if rel >= CX else (p_ref, rel)
        ext_ref[i, 0:HY] = yd_ref[i]
        ext_ref[i, HY : HY + CY] = src[k]
        ext_ref[i, HY + CY :] = yu_ref[i]
    pack_lanes(ext_ref, zl_ref, zr_ref, PX)


def chebyshev(halo, w_ref, rp_ref, a_ref, b_ref):
    _, weights = recurrence()
    now, before = a_ref, b_ref
    for index, (keep, push) in enumerate(weights):
        halo -= 1

        def body(i, carry, now=now, before=before, first=index == 0, keep=keep, push=push):
            around = neighbours(now, i)
            total = rp_ref[i]
            for d in range(6):
                total = total + w_ref[d, i] * around[d]
            new = (1.0 + keep - push) * now[i] + push * total
            if not first:
                new = new - keep * before[i]
            before[i] = new
            return carry

        lax.fori_loop(HX - halo, HX + CX + halo, body, 0)
        now, before = before, now
    return now


def smooth_kernel(pos, ext_ref, zl_ref, zr_ref, sums_ref, matrix_ref, p_ref, xl_ref, xr_ref, g_ref, v_ref, w_ref, rp_ref, a_ref, b_ref):
    mask = inside_yz(pos)
    for i in range(PX):
        g_ref[i] = wide_plane(ext_ref, zl_ref, zr_ref, N_R + i) * (mask * inside_x(pos, i - HX))
    for i in range(N_V):
        v_ref[i] = wide_plane(ext_ref, zl_ref, zr_ref, N_R + N_G + i) * (mask * inside_x(pos, i - H_V))
    for k in range(N_R):
        rp_ref[k - H_R + HX] = wide_plane(ext_ref, zl_ref, zr_ref, k)
    first_scale, _ = recurrence()

    def prepare(i, carry):
        around = neighbours(g_ref, i)
        first, second = pair(g_ref[i])
        count = (around[0] + around[1]) + (around[2] + around[3]) + (around[4] + around[5])
        inverse = inside_yz(pos) * inside_x(pos, i - HX) / (6.0 * first + second * count)
        first, second = first * inverse, second * inverse
        for d in range(6):
            w_ref[d, i] = first + second * around[d]
        scaled = rp_ref[i] * inverse
        rp_ref[i] = scaled
        a_ref[i] = scaled * first_scale
        return carry

    lax.fori_loop(HX - H_R, HX + CX + H_R, prepare, 0)
    result = chebyshev(H_R, w_ref, rp_ref, a_ref, b_ref)
    even = sums_ref[pl.ds(0, 64, stride=2), :]
    odd = sums_ref[pl.ds(1, 64, stride=2), :]
    amounts = coarse_rows(matrix_ref, even, odd)
    (field,) = fields([amounts])
    for x in range(CX):
        value = result[HX + x, HY : HY + CY, 0:CZ]
        value = value + v_ref[x + H_V, HY : HY + CY, 0:CZ] * plane_field(field, x // 2)
        p_ref[x] = value
        if x < HX:
            xl_ref[x] = value
        if x >= CX - HX:
            xr_ref[x - CX + HX] = value


def product_kernel(g_ref, v_ref, out_ref):
    last_y = iota((CY, CZ), 0) % 16 == 15
    last_z = iota((CY, CZ), 1) % 32 == 31
    quads = [[], [], [], []]

    def own(a):
        return a[HY : HY + CY, 0:CZ]

    for sx in range(4):
        sums = [jnp.zeros((CY, CZ), F32) for _ in range(4)]
        for x in (2 * sx, 2 * sx + 1):
            labels = neighbours(g_ref, x + HX)
            values = neighbours(v_ref, x + H_V)
            first, second = pair(own(g_ref[x + HX]))
            mine = own(v_ref[x + H_V])
            count = sum(own(a) for a in labels)
            sums[0] = sums[0] + (6.0 * first + second * count) * mine * mine
            cross = [(first + second * own(labels[d])) * mine * own(values[d]) for d in (1, 3, 5)]
            if x % 2 == 0:
                sums[0] = sums[0] - 2.0 * cross[0]
            else:
                sums[1] = sums[1] - cross[0]
            sums[0] = sums[0] - 2.0 * jnp.where(last_y, 0.0, cross[1]) - 2.0 * jnp.where(last_z, 0.0, cross[2])
            sums[2] = sums[2] - jnp.where(last_y, cross[1], 0.0)
            sums[3] = sums[3] - jnp.where(last_z, cross[2], 0.0)
        for n in range(4):
            quads[n].append(sums[n])
    for n in range(4):
        out_ref[n : n + 1] = row_sums(quads[n])


def image_plane(ref, i, first, second, labels):
    mine = ref[i]
    around = neighbours(ref, i)
    total = (first + second * labels[0]) * (mine - around[0])
    for d in range(1, 6):
        total = total + (first + second * labels[d]) * (mine - around[d])
    return total


def image_kernel(
    pos, ext_ref, zl_ref, zr_ref, g_ref, r_ref, v_ref, e_ref, q_ref, c_ref, y_ref, send_ref, full_ref, w_ref, rp_ref, a_ref, b_ref
):
    mask = inside_yz(pos)
    for i in range(PX):
        full_ref[i] = wide_plane(ext_ref, zl_ref, zr_ref, i) * (mask * inside_x(pos, i - HX))
    first_scale, _ = recurrence()

    def prepare(i, carry):
        labels = neighbours(g_ref, i)
        first, second = pair(g_ref[i])
        count = (labels[0] + labels[1]) + (labels[2] + labels[3]) + (labels[4] + labels[5])
        inverse = inside_yz(pos) * inside_x(pos, i - HX) / (6.0 * first + second * count)
        image = image_plane(full_ref, i, first, second, labels)
        b_ref[i] = image
        first, second = first * inverse, second * inverse
        for d in range(6):
            w_ref[d, i] = first + second * labels[d]
        scaled = image * inverse
        rp_ref[i] = scaled
        a_ref[i] = scaled * first_scale
        return carry

    lax.fori_loop(1, PX - 1, prepare, 0)
    parts = []
    energy = jnp.zeros((CY, CZ), F32)
    curve = jnp.zeros((CY, CZ), F32)
    for x in range(CX):
        image = b_ref[HX + x, HY : HY + CY, 0:CZ]
        value = full_ref[HX + x, HY : HY + CY, 0:CZ]
        q_ref[x] = image
        energy = energy + r_ref[x] * value
        curve = curve + image * value
        term = v_ref[x] * image
        if x % 2 == 0:
            parts.append(term)
        else:
            parts[-1] = parts[-1] + term
    result = chebyshev(HX - 1, w_ref, rp_ref, a_ref, b_ref)
    for x in range(CX):
        i = HX + x
        first, second = pair(g_ref[i])
        image = image_plane(result, i, first, second, neighbours(g_ref, i))
        c_ref[x] = result[i, HY : HY + CY, 0:CZ]
        y_ref[x] = image[HY : HY + CY, 0:CZ]
    lane = iota((1, 128), 1)
    scalars = jnp.where(lane == 64, total_sum(energy), jnp.where(lane == 65, total_sum(curve), 0.0))
    send = jnp.concatenate(
        [
            jnp.where(lane < ND, row_sums(parts), e_ref[0:1]),
            jnp.where(lane < ND, e_ref[1:2], e_ref[2:3]),
            jnp.where(lane < ND, e_ref[3:4], scalars),
        ],
        axis=1,
    )
    send_ref[...] = jnp.broadcast_to(send, (NDEV, 384))


def first_scalars(sums_ref):
    totals = jnp.sum(sums_ref[:, 256:384], axis=0, keepdims=True)
    energy = totals[0:1, 64:65]
    curve = totals[0:1, 65:66]
    return energy, curve, energy / curve


def amounts_kernel(sums_ref, matrix_ref, p_ref, q_ref, c_ref, y_ref, v_ref, r_ref, send_ref, piece_ref):
    _, _, alpha = first_scalars(sums_ref)
    piece_ref[...] = sums_ref[:, 0:128]
    even = piece_ref[pl.ds(0, 64, stride=2), :]
    odd = pltpu.roll(piece_ref[pl.ds(1, 64, stride=2), :], 64, 1)
    amounts = coarse_rows(matrix_ref, even, odd)
    (field,) = fields([amounts])
    sums = [jnp.zeros((CY, CZ), F32) for _ in range(3)]
    for x in range(CX):
        lifted = v_ref[x] * plane_field(field, x // 2)
        p, q, c = p_ref[x], q_ref[x], c_ref[x]
        residual = r_ref[x] - alpha * q
        smooth = p - alpha * c
        smooth_image = q - alpha * y_ref[x]
        precond = smooth - alpha * lifted
        sums[0] = sums[0] + residual * precond
        sums[1] = sums[1] + precond * q
        sums[2] = sums[2] + smooth_image * (smooth - 2.0 * alpha * lifted)
    lane = iota((1, 128), 1)
    row = jnp.where(lane < ND, amounts, 0.0)
    for n in range(3):
        row = jnp.where(lane == ND + n, total_sum(sums[n]), row)
    send_ref[...] = jnp.broadcast_to(row, (NDEV, 128))


def final_kernel(
    pos, sums_ref, got_ref, p_ref, q_ref, c_ref, y_ref, r_ref, vx_ref, g_ref, pressure_ref, residual_ref, lift_ref
):
    energy, curve, alpha = first_scalars(sums_ref)
    got = got_ref[...]
    lane = iota((NDEV, 128), 1)
    dup = jnp.where(lane < ND, got, pltpu.roll(got, 64, 1))
    sz, sy, sx = lane % 4, (lane // 4) % 4, (lane // 16) % 4
    next_z = jnp.where(sz < 3, pltpu.roll(dup, 127, 1), pltpu.roll(pltpu.roll(dup, 3, 1), NDEV - 1, 0))
    next_y = jnp.where(sy < 3, pltpu.roll(dup, 124, 1), pltpu.roll(pltpu.roll(dup, 12, 1), NDEV - 8, 0))
    next_x = jnp.where(sx < 3, pltpu.roll(dup, 112, 1), pltpu.roll(pltpu.roll(dup, 48, 1), NDEV - 32, 0))
    one, two = sums_ref[:, 0:128], sums_ref[:, 128:256]
    three = sums_ref[:, 256:384]
    half = dup * pltpu.roll(one, 64, 1) + 2.0 * (next_x * two + next_y * pltpu.roll(two, 64, 1) + next_z * three)
    quad = total_sum(jnp.where(lane < ND, half * dup, 0.0))
    totals = jnp.sum(got, axis=0, keepdims=True)
    energy_next = totals[0:1, 64:65]
    mixed = totals[0:1, 65:66]
    beta = energy_next / energy
    curve_next = totals[0:1, 66:67] + alpha * alpha * quad + 2.0 * beta * mixed + beta * beta * curve
    alpha_next = energy_next / curve_next

    me = (pos[0] * 4 + pos[1]) * 8 + pos[2]
    rows = []
    for shift in (0, -32, 32, -8, 8, -1, 1):
        at = jnp.clip(me + shift, 0, NDEV - 1)
        rows.append(got_ref[pl.ds(at, 1), :])
    mine, xm, xp, ym, yp, zm, zp = fields(rows)
    lanes = iota((PY, CZ), 1)
    for i in range(N_V):
        x = i - H_V
        if x < 0 or x >= CX:
            own = plane_field(xm, 3) if x < 0 else plane_field(xp, 0)
            lift_ref[i, 0:HY] = jnp.zeros((HY, PZ), F32)
            lift_ref[i, HY + CY :] = jnp.zeros((HY, PZ), F32)
            lift_ref[i, HY : HY + CY, 0:CZ] = vx_ref[i, HY : HY + CY, 0:CZ] * own
            lift_ref[i, HY : HY + CY, CZ:PZ] = jnp.zeros((CY, CZ), F32)
            continue
        s = x // 2
        down = jnp.broadcast_to(ym[4 * s + 3 : 4 * s + 4], (HY, CZ))
        up = jnp.broadcast_to(yp[4 * s : 4 * s + 1], (HY, CZ))
        lift_ref[i, :, 0:CZ] = vx_ref[i, :, 0:CZ] * jnp.concatenate([down, plane_field(mine, s), up], axis=0)
        zeros = jnp.zeros((HY, CZ), F32)
        ahead = jnp.concatenate([zeros, plane_field(zp, s), zeros], axis=0)
        behind = jnp.concatenate([zeros, plane_field(zm, s), zeros], axis=0)
        side = jnp.where(lanes < 8, ahead, jnp.where(lanes >= CZ - 8, behind, 0.0))
        lift_ref[i, :, CZ:PZ] = vx_ref[i, :, CZ:PZ] * side
    for x in range(CX):
        first, second = pair(g_ref[x + HX])
        lifted_image = image_plane(lift_ref, x + H_V, first, second, neighbours(g_ref, x + HX))
        lifted_image = lifted_image[HY : HY + CY, 0:CZ]
        lifted = lift_ref[x + H_V, HY : HY + CY, 0:CZ]
        p, q = p_ref[x], q_ref[x]
        precond = p - alpha * (c_ref[x] + lifted)
        precond_image = q - alpha * (y_ref[x] + lifted_image)
        direction = precond + beta * p
        image = precond_image + beta * q
        pressure_ref[x] = alpha * p + alpha_next * direction
        residual_ref[x] = (r_ref[x] - alpha * q) - alpha_next * image


VMEM = pl.BlockSpec(memory_space=pltpu.VMEM)
SMEM = pl.BlockSpec(memory_space=pltpu.SMEM)


def call(kernel, outs, scratch=(), smem=False, cost=None):
    def run(*args):
        many = isinstance(outs, list)
        specs = [VMEM] * len(args)
        if smem:
            specs[0] = SMEM
        return pl.pallas_call(
            kernel,
            out_shape=[jax.ShapeDtypeStruct(s, F32) for s in outs] if many else jax.ShapeDtypeStruct(outs, F32),
            in_specs=specs,
            out_specs=[VMEM] * len(outs) if many else VMEM,
            scratch_shapes=[pltpu.VMEM(s, F32) for s in scratch],
            compiler_params=pltpu.CompilerParams(vmem_limit_bytes=48 * 1024 * 1024),
            cost_estimate=cost,
        )(*args)

    return run


def swap(to_left, to_right, axis):
    count = lax.axis_size(axis)
    from_right = lax.ppermute(to_left, axis, [((i + 1) % count, i) for i in range(count)])
    from_left = lax.ppermute(to_right, axis, [(i, (i + 1) % count) for i in range(count)])
    return from_left, from_right


def gather(rows):
    return lax.all_to_all(rows, AXES, 0, 0, tiled=True)


def local(right_side, phase, deflation_weights, coarse_inverse):
    pos = jnp.stack([lax.axis_index(a) for a in AXES]).astype(jnp.int32)
    block = (CX, CY, CZ)
    tall = (PX, PY, PZ)
    r, v = right_side, deflation_weights
    n_x = H_R + H_G + H_V
    xl, xr, send = call(start_kernel, [(n_x, CY, CZ), (n_x, CY, CZ), (NDEV, 128)])(r, phase, v)
    fl, fr = swap(xl, xr, "gx")
    sums = gather(send)
    yl, yr = call(y_kernel, [(N_ALL, HY, CZ)] * 2)(r, phase, v, fl, fr)
    yd, yu = swap(yl, yr, "gy")
    ext, zl, zr = call(z_kernel, [(N_ALL, PY, CZ), (GROUPS, PY, CZ), (GROUPS, PY, CZ)])(r, phase, v, fl, fr, yd, yu)
    zfl, zfr = swap(zl, zr, "gz")
    p, xl, xr, labels, v_wide = call(
        smooth_kernel,
        [block, (HX, CY, CZ), (HX, CY, CZ), tall, (N_V, PY, PZ)],
        scratch=[(6, *tall), tall, tall, tall],
        smem=True,
    )(pos, ext, zfl, zfr, sums, coarse_inverse)
    fl, fr = swap(xl, xr, "gx")
    quads = call(product_kernel, (4, 128), cost=pl.CostEstimate(flops=8_000_000, bytes_accessed=3_000_000, transcendentals=0))(
        labels, v_wide
    )
    yl, yr = call(y2_kernel, [(PX, HY, CZ)] * 2)(p, fl, fr)
    yd, yu = swap(yl, yr, "gy")
    ext, zl, zr = call(z2_kernel, [(PX, PY, CZ), (GROUPS_P, PY, CZ), (GROUPS_P, PY, CZ)])(p, fl, fr, yd, yu)
    zfl, zfr = swap(zl, zr, "gz")
    q, c, y, send = call(
        image_kernel,
        [block, block, block, (NDEV, 384)],
        scratch=[tall, (6, *tall), tall, tall, tall],
        smem=True,
    )(pos, ext, zfl, zfr, labels, r, v, quads)
    sums = gather(send)
    send = call(amounts_kernel, (NDEV, 128), scratch=[(NDEV, 128)])(sums, coarse_inverse, p, q, c, y, v, r)
    got = gather(send)
    pressure, residual = call(final_kernel, [block, block], scratch=[(N_V, PY, PZ)], smem=True)(
        pos, sums, got, p, q, c, y, r, v_wide, labels
    )
    return (pressure, residual)


def solution(mesh):
    return jax.shard_map(
        local,
        mesh=mesh,
        in_specs=(P(*AXES), P(*AXES), P(*AXES), P(AXES, None)),
        out_specs=(P(*AXES), P(*AXES)),
        check_vma=False,
    )
```

time: 727 us -> 134 us (0.18)
  blocking collectives: 331 us -> 33.2 us
  starting transfers between devices: 227 us -> 29.6 us
  waiting for transfers between devices: 99.6 us -> 31.5 us
  other arithmetic: 37.8 us -> 0.08 us
  Pallas kernels: 0 us -> 35.7 us
  local copies, waits for them, and re-layouts: 18.4 us -> 3.07 us
    ppermute x78 -> x12, starting transfers between devices: 227 us -> 19.8 us  [the longest x6 12.3 us: swap(): lax.ppermute(to_right, axis, [(i, (i + 1) % count) for i in range(count)])]
    psum x3 -> x0, blocking collectives: 195 us -> none  [the longest x2 131 us: energy_sum(): return lax.psum(jnp.sum(residual * precond), ('gx', 'gy', 'gz'))]
    unnamed x2 -> x0, blocking collectives: 136 us -> none
    ppermute x78 -> x12, waiting for transfers between devices: 99.6 us -> 22.3 us  [the longest x6 19.6 us: swap(): lax.ppermute(to_right, axis, [(i, (i + 1) % count) for i in range(count)])]
    pallas_call x0 -> x10, Pallas kernels: none -> 35.7 us  [run(): pl.pallas_call(kernel, out_shape=[jax.ShapeDtypeStruct(s, F32) for s in o...]
    all_to_all x0 -> x2, blocking collectives: none -> 33.2 us  [gather(): return lax.all_to_all(rows, AXES, 0, 0, tiled=True)]
    mul x39 -> x0, other arithmetic: 15.2 us -> none  [the longest x12 5.86 us: stencil(): flux_x = faces[0] * (padded[1:, 1:-1, 1:-1] - padded[:-1, 1:-1, 1:-1])]
    all_to_all x0 -> x1, starting transfers between devices: none -> 9.85 us  [gather(): return lax.all_to_all(rows, AXES, 0, 0, tiled=True)]
  transfers between devices with their start and end apart: 78 -> 13, of which waited for: 46 -> 7; matrix products, arithmetic and copies ran while one was open for 4% -> 0% of each run, Pallas kernels for 0% -> 1%
where the time goes in v1:
time: 134 us
  Pallas kernels  35.7 us (27%)
  blocking collectives  33.2 us (25%)
  waiting for transfers between devices  31.5 us (24%)
  starting transfers between devices  29.6 us (22%)
  local copies, waits for them, and re-layouts  3.07 us (2%)
    pallas_call x10, Pallas kernels, run(): pl.pallas_call(kernel, out_shape=[jax.ShapeDtypeStruct(s, F32) for s in o...  35.7 us
    all_to_all x2, blocking collectives, gather(): return lax.all_to_all(rows, AXES, 0, 0, tiled=True)  33.2 us
    ppermute x6, waiting for transfers between devices, swap(): lax.ppermute(to_right, axis, [(i, (i + 1) % count) for i in range(count)])  19.6 us
    ppermute x6, starting transfers between devices, swap(): lax.ppermute(to_right, axis, [(i, (i + 1) % count) for i in range(count)])  12.3 us
    all_to_all x1, starting transfers between devices, gather(): return lax.all_to_all(rows, AXES, 0, 0, tiled=True)  9.85 us
    all_to_all x1, waiting for transfers between devices, gather(): return lax.all_to_all(rows, AXES, 0, 0, tiled=True)  9.2 us
    ppermute x6, starting transfers between devices, swap(): lax.ppermute(to_left, axis, [((i + 1) % count, i) for i in range(count)])  7.51 us
    unnamed x13, local copies, waits for them, and re-layouts  2.87 us
  transfers between devices with their start and end apart: 13, of which 7 were waited for; matrix products, arithmetic and copies ran while one was open for 0% of the time, Pallas kernels for 1%

profile of v1, /device:TPU:1, one launch (start us, length us, event | category | flops | bytes accessed | tf_op | source)
XLA Modules:
  0.0 133.8 jit_solution(1896496099118289318)
XLA Ops:
  0.6 0.0 copy-start
  0.6 0.9 copy-done
  1.6 0.0 copy-start.3
  1.6 0.9 copy-done.3
  2.5 0.0 copy-start.5
  2.5 0.9 copy-done.5
  3.5 0.8 shard_map.59
  4.3 2.0 %collective-permute-start = (f32[13,64,128]{2,1,0:T(8,128)S(1)}, f32[13,64,128]{2,1,0:T(8,128)S(1)}, u32[]{:S(2)}, u32[]{:S(2)}) collective-permute-start(f32[13,64,128]{2,1,0:T(8,128)S(1)} %get-tuple-element.24), channel_id=1, source_target_pairs={{0,32},{32,64},{64,96},{96,0},{1,33},{33,65},{65,97},{97,1},{2,34}... | collective-permute-start | bytes 1277960 | tf_op jit(solution)/shard_map/ppermute | solution.py:498
  6.4 1.3 collective-permute-start.1
  7.6 9.1 %collective-permute-done.fl_ref = f32[13,64,128]{2,1,0:T(8,128)S(1)} collective-permute-done((f32[13,64,128]{2,1,0:T(8,128)S(1)}, f32[13,64,128]{2,1,0:T(8,128)S(1)}, u32[]{:S(2)}, u32[]{:S(2)}) %collective-permute-start) | collective-permute-done | bytes 426016 | tf_op jit(solution)/shard_map/ppermute | solution.py:498
  16.7 0.0 collective-permute-done.1.fr_ref
  16.8 1.7 %collective-permute-start.2 = (f32[50,8,128]{2,1,0:T(8,128)S(1)}, f32[50,8,128]{2,1,0:T(8,128)S(1)}, u32[]{:S(2)}, u32[]{:S(2)}) collective-permute-start(f32[50,8,128]{2,1,0:T(8,128)S(1)} %get-tuple-element.26), channel_id=1, source_target_pairs={{0,8},{8,16},{16,24},{24,0},{1,9},{9,17},{17,25},{25,1},{2,10},{10... | collective-permute-start | bytes 614408 | tf_op jit(solution)/shard_map/ppermute | solution.py:498
  18.5 1.5 %collective-permute-start.3 = (f32[50,8,128]{2,1,0:T(8,128)S(1)}, f32[50,8,128]{2,1,0:T(8,128)S(1)}, u32[]{:S(2)}, u32[]{:S(2)}) collective-permute-start(f32[50,8,128]{2,1,0:T(8,128)S(1)} %get-tuple-element.27), channel_id=1, source_target_pairs={{8,0},{16,8},{24,16},{0,24},{9,1},{17,9},{25,17},{1,25},{10,2},{18... | collective-permute-start | bytes 614408 | tf_op jit(solution)/shard_map/ppermute | solution.py:497
  20.0 3.5 %collective-permute-done.2.yd_ref = f32[50,8,128]{2,1,0:T(8,128)S(1)} collective-permute-done((f32[50,8,128]{2,1,0:T(8,128)S(1)}, f32[50,8,128]{2,1,0:T(8,128)S(1)}, u32[]{:S(2)}, u32[]{:S(2)}) %collective-permute-start.2) | collective-permute-done | bytes 204832 | tf_op jit(solution)/shard_map/ppermute | solution.py:498
  23.5 0.0 collective-permute-done.3.yu_ref
  23.5 1.0 shard_map.61
  24.6 4.0 %collective-permute-start.4 = (f32[4,80,128]{2,1,0:T(8,128)S(1)}, f32[4,80,128]{2,1,0:T(8,128)S(1)}, u32[]{:S(2)}, u32[]{:S(2)}) collective-permute-start(f32[4,80,128]{2,1,0:T(8,128)S(1)} %get-tuple-element.29), channel_id=1, source_target_pairs={{0,1},{1,2},{2,3},{3,4},{4,5},{5,6},{6,7},{7,0},{8,9},{9,10},{10,1... | collective-permute-start | bytes 491528 | tf_op jit(solution)/shard_map/ppermute | solution.py:498
  28.6 0.0 collective-permute-start.5
  28.6 9.8 %all-to-all-start = ((f32[128,1,128]{2,1,0:T(1,128)}), f32[128,1,128]{2,1,0:T(1,128)S(1)}, u32[]{:S(2)}, u32[]{:S(2)}) async-start(f32[128,1,128]{2,1,0:T(1,128)} %bitcast.4), calls=%async_computation | async-start | bytes 131072 | tf_op jit(solution)/shard_map/all_to_all | solution.py:503
  38.5 0.1 pad_add_fusion.pos
  38.5 9.2 %all-to-all-done = f32[128,1,128]{2,1,0:T(1,128)S(1)} async-done(((f32[128,1,128]{2,1,0:T(1,128)}), f32[128,1,128]{2,1,0:T(1,128)S(1)}, u32[]{:S(2)}, u32[]{:S(2)}) %all-to-all-start) | async-done | bytes 65568 | tf_op jit(solution)/shard_map/all_to_all | solution.py:503
  47.8 0.0 collective-permute-done.4.zl_ref
  47.8 0.0 collective-permute-done.5.zr_ref
  47.8 13.7 %shard_map.62 = (f32[8,64,128]{2,1,0:T(8,128)S(1)}, f32[7,64,128]{2,1,0:T(8,128)S(1)}, f32[7,64,128]{2,1,0:T(8,128)S(1)}, f32[22,80,256]{2,1,0:T(8,128)S(1)}, f32[10,80,256]{2,1,0:T(8,128)S(1)}) custom-call(s32[3]{0:T(128)S(1)} %pad_add_fusion.pos, f32[50,80,128]{2,1,0:T(8,128)S(1)} %get-tuple-element.28.ext_ref, ...), custom_call_target="tpu_custom_call" | custom-call | tf_op jit(solution)/shard_map/pallas_call | solution.py:482
  61.4 0.4 collective-permute-start.6
  61.8 2.4 %collective-permute-start.7 = (f32[7,64,128]{2,1,0:T(8,128)S(1)}, f32[7,64,128]{2,1,0:T(8,128)S(1)}, u32[]{:S(2)}, u32[]{:S(2)}) collective-permute-start(f32[7,64,128]{2,1,0:T(8,128)S(1)} %get-tuple-element.34), channel_id=1, source_target_pairs={{32,0},{64,32},{96,64},{0,96},{33,1},{65,33},{97,65},{1,97},{34,2}... | collective-permute-start | bytes 688136 | tf_op jit(solution)/shard_map/ppermute | solution.py:497
  64.2 4.4 %collective-permute-done.6.fl_ref = f32[7,64,128]{2,1,0:T(8,128)S(1)} collective-permute-done((f32[7,64,128]{2,1,0:T(8,128)S(1)}, f32[7,64,128]{2,1,0:T(8,128)S(1)}, u32[]{:S(2)}, u32[]{:S(2)}) %collective-permute-start.6) | collective-permute-done | bytes 229408 | tf_op jit(solution)/shard_map/ppermute | solution.py:498
  68.6 0.0 collective-permute-done.7.fr_ref
  68.6 0.0 copy-start.1
  68.6 0.4 collective-permute-start.8
  69.0 2.3 %collective-permute-start.9 = (f32[22,8,128]{2,1,0:T(8,128)S(1)}, f32[22,8,128]{2,1,0:T(8,128)S(1)}, u32[]{:S(2)}, u32[]{:S(2)}) collective-permute-start(f32[22,8,128]{2,1,0:T(8,128)S(1)} %get-tuple-element.36), channel_id=1, source_target_pairs={{8,0},{16,8},{24,16},{0,24},{9,1},{17,9},{25,17},{1,25},{10,2},{18... | collective-permute-start | bytes 270344 | tf_op jit(solution)/shard_map/ppermute | solution.py:497
  71.4 1.9 %collective-permute-done.8.yd_ref = f32[22,8,128]{2,1,0:T(8,128)S(1)} collective-permute-done((f32[22,8,128]{2,1,0:T(8,128)S(1)}, f32[22,8,128]{2,1,0:T(8,128)S(1)}, u32[]{:S(2)}, u32[]{:S(2)}) %collective-permute-start.8) | collective-permute-done | bytes 90144 | tf_op jit(solution)/shard_map/ppermute | solution.py:498
  73.3 0.0 collective-permute-done.9.yu_ref
  73.3 0.5 shard_map.64
  73.8 3.7 %collective-permute-start.10 = (f32[2,80,128]{2,1,0:T(8,128)S(1)}, f32[2,80,128]{2,1,0:T(8,128)S(1)}, u32[]{:S(2)}, u32[]{:S(2)}) collective-permute-start(f32[2,80,128]{2,1,0:T(8,128)S(1)} %get-tuple-element.38), channel_id=1, source_target_pairs={{0,1},{1,2},{2,3},{3,4},{4,5},{5,6},{6,7},{7,0},{8,9},{9,10},{10,1... | collective-permute-start | bytes 245768 | tf_op jit(solution)/shard_map/ppermute | solution.py:498
  77.5 0.0 collective-permute-start.11
  77.5 0.9 shard_map.65.e_ref
  78.4 0.6 collective-permute-done.10.zl_ref
  79.0 2.7 %collective-permute-done.11.zr_ref = f32[2,80,128]{2,1,0:T(8,128)S(1)} collective-permute-done((f32[2,80,128]{2,1,0:T(8,128)S(1)}, f32[2,80,128]{2,1,0:T(8,128)S(1)}, u32[]{:S(2)}, u32[]{:S(2)}) %collective-permute-start.11) | collective-permute-done | bytes 81952 | tf_op jit(solution)/shard_map/ppermute | solution.py:497
  81.7 0.0 copy-done.1
  81.7 0.0 copy-done.4
  81.7 15.5 %shard_map.66 = (f32[8,64,128]{2,1,0:T(8,128)S(1)}, f32[8,64,128]{2,1,0:T(8,128)S(1)}, f32[8,64,128]{2,1,0:T(8,128)S(1)}, f32[128,384]{1,0:T(8,128)S(1)}) custom-call(s32[3]{0:T(128)S(1)} %pad_add_fusion.pos, f32[22,80,128]{2,1,0:T(8,128)S(1)} %get-tuple-element.37.ext_ref, f32[2,80,128]{2,1,0:T(8,128)S(1)} %collective-permute-done.10.zl_ref, ...), custom_call_target="tpu_custom_call" | custom-call | tf_op jit(solution)/shard_map/pallas_call | solution.py:482
  97.2 0.2 copy.7
  97.4 19.5 %all_to_all.33 = f32[128,1,384]{2,1,0:T(1,128)S(1)} all-to-all(f32[128,1,384]{2,1,0:T(1,128)S(1)} %copy.7), channel_id=1, replica_groups=mesh['gx'=4,'gy'=4,'gz'=8] {'gx','gy','gz'}, dimensions={0} | all-to-all | bytes 393216 | tf_op jit(solution)/shard_map/all_to_all | solution.py:503
  117.0 0.0 copy-done.2
  117.0 0.7 shard_map.67
  117.7 13.6 %all_to_all.34 = f32[128,1,128]{2,1,0:T(1,128)S(1)} all-to-all(f32[128,1,128]{2,1,0:T(1,128)S(1)} %bitcast.19), channel_id=1, replica_groups=mesh['gx'=4,'gy'=4,'gz'=8] {'gx','gy','gz'}, dimensions={0} | all-to-all | bytes 131072 | tf_op jit(solution)/shard_map/all_to_all | solution.py:503
  131.3 2.5 %shard_map.68 = (f32[8,64,128]{2,1,0:T(8,128)}, f32[8,64,128]{2,1,0:T(8,128)}) custom-call(s32[3]{0:T(128)S(1)} %pad_add_fusion.pos, f32[128,384]{1,0:T(8,128)S(1)} %bitcast.16, f32[128,128]{1,0:T(8,128)S(1)} %bitcast.18, f32[8,64,128]{2,1,0:T(8,128)S(1)} %get-tuple-element.32.p_ref, f32[8,64,128]{2,1,0:T(8,128)S(1)} %get-tuple-element.43.q_ref, ...), custom_call_target="tpu_custom_call" | custom-call | tf_op jit(solution)/shard_map/pallas_call | solution.py:482
  (5 shorter events, 0.1 us)
Async XLA Ops:
  0.6 1.0 copy-start
  1.6 0.9 copy-start.3
  2.5 0.9 copy-start.5
  4.3 12.4 %collective-permute-start = (f32[13,64,128]{2,1,0:T(8,128)S(1)}, f32[13,64,128]{2,1,0:T(8,128)S(1)}, u32[]{:S(2)}, u32[]{:S(2)}) collective-permute-start(f32[13,64,128]{2,1,0:T(8,128)S(1)} %get-tuple-element.24), channel_id=1, source_target_pairs={{0,32},{32,64},{64,96},{96,0},{1,33},{33,65},{65,97},{97,1},{2,34}... | collective-permute-start | bytes 1277960 | tf_op jit(solution)/shard_map/ppermute | solution.py:498
  6.4 10.4 %collective-permute-start.1 = (f32[13,64,128]{2,1,0:T(8,128)S(1)}, f32[13,64,128]{2,1,0:T(8,128)S(1)}, u32[]{:S(2)}, u32[]{:S(2)}) collective-permute-start(f32[13,64,128]{2,1,0:T(8,128)S(1)} %get-tuple-element.25), channel_id=1, source_target_pairs={{32,0},{64,32},{96,64},{0,96},{33,1},{65,33},{97,65},{1,97},{34,2}... | collective-permute-start | bytes 1277960 | tf_op jit(solution)/shard_map/ppermute | solution.py:497
  16.8 6.8 %collective-permute-start.2 = (f32[50,8,128]{2,1,0:T(8,128)S(1)}, f32[50,8,128]{2,1,0:T(8,128)S(1)}, u32[]{:S(2)}, u32[]{:S(2)}) collective-permute-start(f32[50,8,128]{2,1,0:T(8,128)S(1)} %get-tuple-element.26), channel_id=1, source_target_pairs={{0,8},{8,16},{16,24},{24,0},{1,9},{9,17},{17,25},{25,1},{2,10},{10... | collective-permute-start | bytes 614408 | tf_op jit(solution)/shard_map/ppermute | solution.py:498
  18.5 5.1 %collective-permute-start.3 = (f32[50,8,128]{2,1,0:T(8,128)S(1)}, f32[50,8,128]{2,1,0:T(8,128)S(1)}, u32[]{:S(2)}, u32[]{:S(2)}) collective-permute-start(f32[50,8,128]{2,1,0:T(8,128)S(1)} %get-tuple-element.27), channel_id=1, source_target_pairs={{8,0},{16,8},{24,16},{0,24},{9,1},{17,9},{25,17},{1,25},{10,2},{18... | collective-permute-start | bytes 614408 | tf_op jit(solution)/shard_map/ppermute | solution.py:497
  24.6 23.2 %collective-permute-start.4 = (f32[4,80,128]{2,1,0:T(8,128)S(1)}, f32[4,80,128]{2,1,0:T(8,128)S(1)}, u32[]{:S(2)}, u32[]{:S(2)}) collective-permute-start(f32[4,80,128]{2,1,0:T(8,128)S(1)} %get-tuple-element.29), channel_id=1, source_target_pairs={{0,1},{1,2},{2,3},{3,4},{4,5},{5,6},{6,7},{7,0},{8,9},{9,10},{10,1... | collective-permute-start | bytes 491528 | tf_op jit(solution)/shard_map/ppermute | solution.py:498
  28.6 19.1 %collective-permute-start.5 = (f32[4,80,128]{2,1,0:T(8,128)S(1)}, f32[4,80,128]{2,1,0:T(8,128)S(1)}, u32[]{:S(2)}, u32[]{:S(2)}) collective-permute-start(f32[4,80,128]{2,1,0:T(8,128)S(1)} %get-tuple-element.30), channel_id=1, source_target_pairs={{1,0},{2,1},{3,2},{4,3},{5,4},{6,5},{7,6},{0,7},{9,8},{10,9},{11,1... | collective-permute-start | bytes 491528 | tf_op jit(solution)/shard_map/ppermute | solution.py:497
  28.6 19.1 %all-to-all-start = ((f32[128,1,128]{2,1,0:T(1,128)}), f32[128,1,128]{2,1,0:T(1,128)S(1)}, u32[]{:S(2)}, u32[]{:S(2)}) async-start(f32[128,1,128]{2,1,0:T(1,128)} %bitcast.4), calls=%async_computation | async-start | bytes 131072 | tf_op jit(solution)/shard_map/all_to_all | solution.py:503
  61.4 7.2 %collective-permute-start.6 = (f32[7,64,128]{2,1,0:T(8,128)S(1)}, f32[7,64,128]{2,1,0:T(8,128)S(1)}, u32[]{:S(2)}, u32[]{:S(2)}) collective-permute-start(f32[7,64,128]{2,1,0:T(8,128)S(1)} %get-tuple-element.33), channel_id=1, source_target_pairs={{0,32},{32,64},{64,96},{96,0},{1,33},{33,65},{65,97},{97,1},{2,34}... | collective-permute-start | bytes 688136 | tf_op jit(solution)/shard_map/ppermute | solution.py:498
  61.8 6.8 %collective-permute-start.7 = (f32[7,64,128]{2,1,0:T(8,128)S(1)}, f32[7,64,128]{2,1,0:T(8,128)S(1)}, u32[]{:S(2)}, u32[]{:S(2)}) collective-permute-start(f32[7,64,128]{2,1,0:T(8,128)S(1)} %get-tuple-element.34), channel_id=1, source_target_pairs={{32,0},{64,32},{96,64},{0,96},{33,1},{65,33},{97,65},{1,97},{34,2}... | collective-permute-start | bytes 688136 | tf_op jit(solution)/shard_map/ppermute | solution.py:497
  68.6 13.1 %copy-start.1 = (f32[8,64,128]{2,1,0:T(8,128)S(1)}, f32[8,64,128]{2,1,0:T(8,128)}, u32[]{:S(2)}) copy-start(f32[8,64,128]{2,1,0:T(8,128)} %r_ref.11) | copy-start | bytes 786436
  68.6 13.1 %copy-start.4 = (f32[8,64,128]{2,1,0:T(8,128)S(1)}, f32[8,64,128]{2,1,0:T(8,128)}, u32[]{:S(2)}) copy-start(f32[8,64,128]{2,1,0:T(8,128)} %v_ref.9) | copy-start | bytes 786436
  68.6 4.7 %collective-permute-start.8 = (f32[22,8,128]{2,1,0:T(8,128)S(1)}, f32[22,8,128]{2,1,0:T(8,128)S(1)}, u32[]{:S(2)}, u32[]{:S(2)}) collective-permute-start(f32[22,8,128]{2,1,0:T(8,128)S(1)} %get-tuple-element.35), channel_id=1, source_target_pairs={{0,8},{8,16},{16,24},{24,0},{1,9},{9,17},{17,25},{25,1},{2,10},{10... | collective-permute-start | bytes 270344 | tf_op jit(solution)/shard_map/ppermute | solution.py:498
  69.0 4.3 %collective-permute-start.9 = (f32[22,8,128]{2,1,0:T(8,128)S(1)}, f32[22,8,128]{2,1,0:T(8,128)S(1)}, u32[]{:S(2)}, u32[]{:S(2)}) collective-permute-start(f32[22,8,128]{2,1,0:T(8,128)S(1)} %get-tuple-element.36), channel_id=1, source_target_pairs={{8,0},{16,8},{24,16},{0,24},{9,1},{17,9},{25,17},{1,25},{10,2},{18... | collective-permute-start | bytes 270344 | tf_op jit(solution)/shard_map/ppermute | solution.py:497
  73.8 5.2 %collective-permute-start.10 = (f32[2,80,128]{2,1,0:T(8,128)S(1)}, f32[2,80,128]{2,1,0:T(8,128)S(1)}, u32[]{:S(2)}, u32[]{:S(2)}) collective-permute-start(f32[2,80,128]{2,1,0:T(8,128)S(1)} %get-tuple-element.38), channel_id=1, source_target_pairs={{0,1},{1,2},{2,3},{3,4},{4,5},{5,6},{6,7},{7,0},{8,9},{9,10},{10,1... | collective-permute-start | bytes 245768 | tf_op jit(solution)/shard_map/ppermute | solution.py:498
  77.5 4.2 %collective-permute-start.11 = (f32[2,80,128]{2,1,0:T(8,128)S(1)}, f32[2,80,128]{2,1,0:T(8,128)S(1)}, u32[]{:S(2)}, u32[]{:S(2)}) collective-permute-start(f32[2,80,128]{2,1,0:T(8,128)S(1)} %get-tuple-element.39), channel_id=1, source_target_pairs={{1,0},{2,1},{3,2},{4,3},{5,4},{6,5},{7,6},{0,7},{9,8},{10,9},{11,1... | collective-permute-start | bytes 245768 | tf_op jit(solution)/shard_map/ppermute | solution.py:497
  81.7 35.3 %copy-start.2 = (f32[64,8192]{1,0:T(8,128)S(1)}, f32[64,8192]{1,0:T(8,128)}, u32[]{:S(2)}) copy-start(f32[64,8192]{1,0:T(8,128)} %matrix_ref.3) | copy-start | bytes 6291460

commit v2 on v1

--- a/solution.py
+++ b/solution.py
@@ -24,6 +24,7 @@
 GROUPS = -(-N_ALL // 16)
 GROUPS_P = -(-PX // 16)
 NDEV = 128
+ROWS = PY // 8
 
 LIQUID = np.float32(1.0)
 GAS = np.float32(0.001)
@@ -52,11 +53,20 @@
     return lax.broadcasted_iota(jnp.int32, shape, dim)
 
 
+def whole(ref, i):
+    return jnp.concatenate([ref[0, i], ref[1, i]], axis=1)
+
+
+def put(ref, i, plane):
+    ref[0, i] = plane[:, 0:CZ]
+    ref[1, i] = plane[:, CZ:PZ]
+
+
 def neighbours(ref, i):
-    v = ref[i]
+    v = whole(ref, i)
     return (
-        ref[i - 1],
-        ref[i + 1],
+        whole(ref, i - 1),
+        whole(ref, i + 1),
         pltpu.roll(v, 1, 0),
         pltpu.roll(v, PY - 1, 0),
         pltpu.roll(v, 1, 1),
@@ -64,10 +74,29 @@
     )
 
 
-def inside_yz(pos):
+def strided(ref, i, j):
+    rows = pl.ds(j, 8, stride=ROWS)
+    return jnp.concatenate([ref[0, i, rows, :], ref[1, i, rows, :]], axis=1)
+
+
+def around_strided(load, i, j):
+    v = load(i, j)
+    return (
+        load(i - 1, j),
+        load(i + 1, j),
+        load(i, j - 1) if j else pltpu.roll(load(i, ROWS - 1), 1, 0),
+        load(i, j + 1) if j < ROWS - 1 else pltpu.roll(load(i, 0), 7, 0),
+        pltpu.roll(v, 1, 1),
+        pltpu.roll(v, PZ - 1, 1),
+    )
+
+
+def inside_yz(pos, j=None):
     gy, gz = pos[1], pos[2]
-    row = iota((PY, PZ), 0) - HY + gy * CY
-    lane = iota((PY, PZ), 1)
+    shape = (PY, PZ) if j is None else (8, PZ)
+    row = iota(shape, 0) if j is None else iota(shape, 0) * ROWS + j
+    row = row - HY + gy * CY
+    lane = iota(shape, 1)
     near = jnp.where(lane < CZ + CZ // 2, lane, lane - PZ) + gz * CZ
     kept = (lane < CZ + 8) | (lane >= PZ - 8)
     good = (row >= 0) & (row < 4 * CY) & (near >= 0) & (near < 8 * CZ) & kept
@@ -125,20 +154,27 @@
     return jnp.sum(jnp.sum(x, axis=0, keepdims=True), axis=1, keepdims=True)
 
 
-def start_kernel(r_ref, phase_ref, v_ref, xl_ref, xr_ref, send_ref):
+def start_kernel(r_in, phase_in, v_in, xl_ref, xr_ref, send_ref, r_ref, g_ref, v_ref, phase_ref, sem):
+    pairs = ((r_in, r_ref), (v_in, v_ref), (phase_in, phase_ref))
+    copies = [pltpu.make_async_copy(src, dst, sem.at[n]) for n, (src, dst) in enumerate(pairs)]
+    for copy in copies:
+        copy.start()
+    for copy in copies:
+        copy.wait()
     parts = []
     for sx in range(4):
         parts.append(r_ref[2 * sx] * v_ref[2 * sx] + r_ref[2 * sx + 1] * v_ref[2 * sx + 1])
     send_ref[...] = jnp.broadcast_to(row_sums(parts), (NDEV, 128))
     xl_ref[0:H_R] = r_ref[0:H_R]
     xr_ref[0:H_R] = r_ref[CX - H_R :]
-    xl_ref[H_R : H_R + H_G] = jnp.where(phase_ref[0:H_G] == 1, 1.0, 0.0).astype(F32)
-    xr_ref[H_R : H_R + H_G] = jnp.where(phase_ref[CX - H_G :] == 1, 1.0, 0.0).astype(F32)
+    g_ref[...] = jnp.where(phase_ref[...] == 1, 1.0, 0.0).astype(F32)
+    xl_ref[H_R : H_R + H_G] = g_ref[0:H_G]
+    xr_ref[H_R : H_R + H_G] = g_ref[CX - H_G :]
     xl_ref[H_R + H_G :] = v_ref[0:H_V]
     xr_ref[H_R + H_G :] = v_ref[CX - H_V :]
 
 
-def stacked_planes(r_ref, phase_ref, v_ref, fl_ref, fr_ref):
+def stacked_planes(r_ref, g_ref, v_ref, fl_ref, fr_ref):
     planes = []
     for halo, own, base in ((H_R, "r", 0), (H_G, "g", H_R), (H_V, "v", H_R + H_G)):
         for rel in range(-halo, CX + halo):
@@ -149,14 +185,14 @@
             elif own == "r":
                 planes.append(lambda s, k=rel: r_ref[k, s])
             elif own == "g":
-                planes.append(lambda s, k=rel: jnp.where(phase_ref[k, s] == 1, 1.0, 0.0).astype(F32))
+                planes.append(lambda s, k=rel: g_ref[k, s])
             else:
                 planes.append(lambda s, k=rel: v_ref[k, s])
     return planes
 
 
-def y_kernel(r_ref, phase_ref, v_ref, fl_ref, fr_ref, yl_ref, yr_ref):
-    planes = stacked_planes(r_ref, phase_ref, v_ref, fl_ref, fr_ref)
+def y_kernel(r_ref, g_ref, v_ref, fl_ref, fr_ref, yl_ref, yr_ref):
+    planes = stacked_planes(r_ref, g_ref, v_ref, fl_ref, fr_ref)
     for k, plane in enumerate(planes):
         yl_ref[k] = plane(pl.ds(0, HY))
         yr_ref[k] = plane(pl.ds(CY - HY, HY))
@@ -190,8 +226,8 @@
     return jnp.concatenate([ext_ref[k], side], axis=1)
 
 
-def z_kernel(r_ref, phase_ref, v_ref, fl_ref, fr_ref, yd_ref, yu_ref, ext_ref, zl_ref, zr_ref):
-    planes = stacked_planes(r_ref, phase_ref, v_ref, fl_ref, fr_ref)
+def z_kernel(r_ref, g_ref, v_ref, fl_ref, fr_ref, yd_ref, yu_ref, ext_ref, zl_ref, zr_ref):
+    planes = stacked_planes(r_ref, g_ref, v_ref, fl_ref, fr_ref)
     for k, plane in enumerate(planes):
         ext_ref[k, 0:HY] = yd_ref[k]
         ext_ref[k, HY : HY + CY] = plane(pl.ds(0, CY))
@@ -222,55 +258,53 @@
     now, before = a_ref, b_ref
     for index, (keep, push) in enumerate(weights):
         halo -= 1
-
-        def body(i, carry, now=now, before=before, first=index == 0, keep=keep, push=push):
-            around = neighbours(now, i)
-            total = rp_ref[i]
-            for d in range(6):
-                total = total + w_ref[d, i] * around[d]
-            new = (1.0 + keep - push) * now[i] + push * total
-            if not first:
-                new = new - keep * before[i]
-            before[i] = new
-            return carry
-
-        lax.fori_loop(HX - halo, HX + CX + halo, body, 0)
+        for i in range(HX - halo, HX + CX + halo):
+            for j in range(ROWS):
+                around = around_strided(lambda i, j: now[i, j], i, j)
+                total = rp_ref[i, j]
+                for d in range(6):
+                    total = total + w_ref[d, i, j] * around[d]
+                new = (1.0 + keep - push) * now[i, j] + push * total
+                if index:
+                    new = new - keep * before[i, j]
+                before[i, j] = new
         now, before = before, now
     return now
 
 
-def smooth_kernel(pos, ext_ref, zl_ref, zr_ref, sums_ref, matrix_ref, p_ref, xl_ref, xr_ref, g_ref, v_ref, w_ref, rp_ref, a_ref, b_ref):
+def smooth_kernel(pos, ext_ref, zl_ref, zr_ref, sums_ref, matrix_ref, p_ref, xl_ref, xr_ref, g_ref, v_ref, wide_ref, w_ref, rp_ref, a_ref, b_ref):
     mask = inside_yz(pos)
     for i in range(PX):
-        g_ref[i] = wide_plane(ext_ref, zl_ref, zr_ref, N_R + i) * (mask * inside_x(pos, i - HX))
+        put(g_ref, i, wide_plane(ext_ref, zl_ref, zr_ref, N_R + i) * (mask * inside_x(pos, i - HX)))
     for i in range(N_V):
-        v_ref[i] = wide_plane(ext_ref, zl_ref, zr_ref, N_R + N_G + i) * (mask * inside_x(pos, i - H_V))
+        put(v_ref, i, wide_plane(ext_ref, zl_ref, zr_ref, N_R + N_G + i) * (mask * inside_x(pos, i - H_V)))
     for k in range(N_R):
-        rp_ref[k - H_R + HX] = wide_plane(ext_ref, zl_ref, zr_ref, k)
+        put(wide_ref, k, wide_plane(ext_ref, zl_ref, zr_ref, k))
     first_scale, _ = recurrence()
-
-    def prepare(i, carry):
-        around = neighbours(g_ref, i)
-        first, second = pair(g_ref[i])
-        count = (around[0] + around[1]) + (around[2] + around[3]) + (around[4] + around[5])
-        inverse = inside_yz(pos) * inside_x(pos, i - HX) / (6.0 * first + second * count)
-        first, second = first * inverse, second * inverse
-        for d in range(6):
-            w_ref[d, i] = first + second * around[d]
-        scaled = rp_ref[i] * inverse
-        rp_ref[i] = scaled
-        a_ref[i] = scaled * first_scale
-        return carry
-
-    lax.fori_loop(HX - H_R, HX + CX + H_R, prepare, 0)
+    for j in range(ROWS):
+        mask = inside_yz(pos, j)
+        for i in range(HX - H_R, HX + CX + H_R):
+            labels = around_strided(lambda i, j: strided(g_ref, i, j), i, j)
+            first, second = pair(strided(g_ref, i, j))
+            count = (labels[0] + labels[1]) + (labels[2] + labels[3]) + (labels[4] + labels[5])
+            inverse = mask * inside_x(pos, i - HX) / (6.0 * first + second * count)
+            first, second = first * inverse, second * inverse
+            for d in range(6):
+                w_ref[d, i, j] = first + second * labels[d]
+            scaled = strided(wide_ref, i - HX + H_R, j) * inverse
+            rp_ref[i, j] = scaled
+            a_ref[i, j] = scaled * first_scale
     result = chebyshev(H_R, w_ref, rp_ref, a_ref, b_ref)
+    for x in range(CX):
+        for j in range(ROWS):
+            wide_ref[0, x, pl.ds(j, 8, stride=ROWS), :] = result[HX + x, j, :, 0:CZ]
     even = sums_ref[pl.ds(0, 64, stride=2), :]
     odd = sums_ref[pl.ds(1, 64, stride=2), :]
     amounts = coarse_rows(matrix_ref, even, odd)
     (field,) = fields([amounts])
     for x in range(CX):
-        value = result[HX + x, HY : HY + CY, 0:CZ]
-        value = value + v_ref[x + H_V, HY : HY + CY, 0:CZ] * plane_field(field, x // 2)
+        value = wide_ref[0, x, HY : HY + CY]
+        value = value + v_ref[0, x + H_V, HY : HY + CY] * plane_field(field, x // 2)
         p_ref[x] = value
         if x < HX:
             xl_ref[x] = value
@@ -291,8 +325,8 @@
         for x in (2 * sx, 2 * sx + 1):
             labels = neighbours(g_ref, x + HX)
             values = neighbours(v_ref, x + H_V)
-            first, second = pair(own(g_ref[x + HX]))
-            mine = own(v_ref[x + H_V])
+            first, second = pair(own(whole(g_ref, x + HX)))
+            mine = own(whole(v_ref, x + H_V))
             count = sum(own(a) for a in labels)
             sums[0] = sums[0] + (6.0 * first + second * count) * mine * mine
             cross = [(first + second * own(labels[d])) * mine * own(values[d]) for d in (1, 3, 5)]
@@ -310,7 +344,7 @@
 
 
 def image_plane(ref, i, first, second, labels):
-    mine = ref[i]
+    mine = whole(ref, i)
     around = neighbours(ref, i)
     total = (first + second * labels[0]) * (mine - around[0])
     for d in range(1, 6):
@@ -319,35 +353,37 @@
 
 
 def image_kernel(
-    pos, ext_ref, zl_ref, zr_ref, g_ref, r_ref, v_ref, e_ref, q_ref, c_ref, y_ref, send_ref, full_ref, w_ref, rp_ref, a_ref, b_ref
+    pos, ext_ref, zl_ref, zr_ref, g_ref, r_ref, v_ref, e_ref, q_ref, c_ref, y_ref, send_ref, full_ref, plane_ref, w_ref, rp_ref, a_ref, b_ref
 ):
     mask = inside_yz(pos)
     for i in range(PX):
-        full_ref[i] = wide_plane(ext_ref, zl_ref, zr_ref, i) * (mask * inside_x(pos, i - HX))
+        put(full_ref, i, wide_plane(ext_ref, zl_ref, zr_ref, i) * (mask * inside_x(pos, i - HX)))
     first_scale, _ = recurrence()
-
-    def prepare(i, carry):
-        labels = neighbours(g_ref, i)
-        first, second = pair(g_ref[i])
-        count = (labels[0] + labels[1]) + (labels[2] + labels[3]) + (labels[4] + labels[5])
-        inverse = inside_yz(pos) * inside_x(pos, i - HX) / (6.0 * first + second * count)
-        image = image_plane(full_ref, i, first, second, labels)
-        b_ref[i] = image
-        first, second = first * inverse, second * inverse
-        for d in range(6):
-            w_ref[d, i] = first + second * labels[d]
-        scaled = image * inverse
-        rp_ref[i] = scaled
-        a_ref[i] = scaled * first_scale
-        return carry
-
-    lax.fori_loop(1, PX - 1, prepare, 0)
+    for j in range(ROWS):
+        mask = inside_yz(pos, j)
+        for i in range(1, PX - 1):
+            labels = around_strided(lambda i, j: strided(g_ref, i, j), i, j)
+            values = around_strided(lambda i, j: strided(full_ref, i, j), i, j)
+            first, second = pair(strided(g_ref, i, j))
+            count = (labels[0] + labels[1]) + (labels[2] + labels[3]) + (labels[4] + labels[5])
+            inverse = mask * inside_x(pos, i - HX) / (6.0 * first + second * count)
+            mine = strided(full_ref, i, j)
+            image = jnp.zeros_like(mine)
+            for d in range(6):
+                face = first + second * labels[d]
+                image = image + face * (mine - values[d])
+                w_ref[d, i, j] = face * inverse
+            if HX <= i < HX + CX:
+                plane_ref[i - HX, pl.ds(j, 8, stride=ROWS), :] = image[:, 0:CZ]
+            scaled = image * inverse
+            rp_ref[i, j] = scaled
+            a_ref[i, j] = scaled * first_scale
     parts = []
     energy = jnp.zeros((CY, CZ), F32)
     curve = jnp.zeros((CY, CZ), F32)
     for x in range(CX):
-        image = b_ref[HX + x, HY : HY + CY, 0:CZ]
-        value = full_ref[HX + x, HY : HY + CY, 0:CZ]
+        image = plane_ref[x, HY : HY + CY]
+        value = full_ref[0, HX + x, HY : HY + CY]
         q_ref[x] = image
         energy = energy + r_ref[x] * value
         curve = curve + image * value
@@ -359,10 +395,18 @@
     result = chebyshev(HX - 1, w_ref, rp_ref, a_ref, b_ref)
     for x in range(CX):
         i = HX + x
-        first, second = pair(g_ref[i])
-        image = image_plane(result, i, first, second, neighbours(g_ref, i))
-        c_ref[x] = result[i, HY : HY + CY, 0:CZ]
-        y_ref[x] = image[HY : HY + CY, 0:CZ]
+        for j in range(ROWS):
+            labels = around_strided(lambda i, j: strided(g_ref, i, j), i, j)
+            values = around_strided(lambda i, j: result[i, j], i, j)
+            first, second = pair(strided(g_ref, i, j))
+            mine = result[i, j]
+            image = jnp.zeros_like(mine)
+            for d in range(6):
+                image = image + (first + second * labels[d]) * (mine - values[d])
+            full_ref[0, x, pl.ds(j, 8, stride=ROWS), :] = mine[:, 0:CZ]
+            plane_ref[x, pl.ds(j, 8, stride=ROWS), :] = image[:, 0:CZ]
+        c_ref[x] = full_ref[0, x, HY : HY + CY]
+        y_ref[x] = plane_ref[x, HY : HY + CY]
     lane = iota((1, 128), 1)
     scalars = jnp.where(lane == 64, total_sum(energy), jnp.where(lane == 65, total_sum(curve), 0.0))
     send = jnp.concatenate(
@@ -437,29 +481,28 @@
         rows.append(got_ref[pl.ds(at, 1), :])
     mine, xm, xp, ym, yp, zm, zp = fields(rows)
     lanes = iota((PY, CZ), 1)
+    zeros = jnp.zeros((HY, CZ), F32)
     for i in range(N_V):
         x = i - H_V
         if x < 0 or x >= CX:
             own = plane_field(xm, 3) if x < 0 else plane_field(xp, 0)
-            lift_ref[i, 0:HY] = jnp.zeros((HY, PZ), F32)
-            lift_ref[i, HY + CY :] = jnp.zeros((HY, PZ), F32)
-            lift_ref[i, HY : HY + CY, 0:CZ] = vx_ref[i, HY : HY + CY, 0:CZ] * own
-            lift_ref[i, HY : HY + CY, CZ:PZ] = jnp.zeros((CY, CZ), F32)
-            continue
-        s = x // 2
-        down = jnp.broadcast_to(ym[4 * s + 3 : 4 * s + 4], (HY, CZ))
-        up = jnp.broadcast_to(yp[4 * s : 4 * s + 1], (HY, CZ))
-        lift_ref[i, :, 0:CZ] = vx_ref[i, :, 0:CZ] * jnp.concatenate([down, plane_field(mine, s), up], axis=0)
-        zeros = jnp.zeros((HY, CZ), F32)
-        ahead = jnp.concatenate([zeros, plane_field(zp, s), zeros], axis=0)
-        behind = jnp.concatenate([zeros, plane_field(zm, s), zeros], axis=0)
-        side = jnp.where(lanes < 8, ahead, jnp.where(lanes >= CZ - 8, behind, 0.0))
-        lift_ref[i, :, CZ:PZ] = vx_ref[i, :, CZ:PZ] * side
+            middle = jnp.concatenate([zeros, own, zeros], axis=0)
+            side = jnp.zeros((PY, CZ), F32)
+        else:
+            s = x // 2
+            down = jnp.broadcast_to(ym[4 * s + 3 : 4 * s + 4], (HY, CZ))
+            up = jnp.broadcast_to(yp[4 * s : 4 * s + 1], (HY, CZ))
+            middle = jnp.concatenate([down, plane_field(mine, s), up], axis=0)
+            ahead = jnp.concatenate([zeros, plane_field(zp, s), zeros], axis=0)
+            behind = jnp.concatenate([zeros, plane_field(zm, s), zeros], axis=0)
+            side = jnp.where(lanes < 8, ahead, jnp.where(lanes >= CZ - 8, behind, 0.0))
+        lift_ref[0, i] = vx_ref[0, i] * middle
+        lift_ref[1, i] = vx_ref[1, i] * side
     for x in range(CX):
-        first, second = pair(g_ref[x + HX])
+        first, second = pair(whole(g_ref, x + HX))
         lifted_image = image_plane(lift_ref, x + H_V, first, second, neighbours(g_ref, x + HX))
         lifted_image = lifted_image[HY : HY + CY, 0:CZ]
-        lifted = lift_ref[x + H_V, HY : HY + CY, 0:CZ]
+        lifted = lift_ref[0, x + H_V, HY : HY + CY]
         p, q = p_ref[x], q_ref[x]
         precond = p - alpha * (c_ref[x] + lifted)
         precond_image = q - alpha * (y_ref[x] + lifted_image)
@@ -473,23 +516,29 @@
 SMEM = pl.BlockSpec(memory_space=pltpu.SMEM)
 
 
-def call(kernel, outs, scratch=(), smem=False, cost=None):
+def call(kernel, outs, scratch=(), smem=False, hbm=0, mib=48, cost=None):
     def run(*args):
         many = isinstance(outs, list)
         specs = [VMEM] * len(args)
         if smem:
             specs[0] = SMEM
+        for n in range(hbm):
+            specs[n] = pl.BlockSpec(memory_space=pltpu.HBM)
         return pl.pallas_call(
             kernel,
             out_shape=[jax.ShapeDtypeStruct(s, F32) for s in outs] if many else jax.ShapeDtypeStruct(outs, F32),
             in_specs=specs,
             out_specs=[VMEM] * len(outs) if many else VMEM,
-            scratch_shapes=[pltpu.VMEM(s, F32) for s in scratch],
-            compiler_params=pltpu.CompilerParams(vmem_limit_bytes=48 * 1024 * 1024),
+            scratch_shapes=[pltpu.VMEM(s, F32) if isinstance(s, tuple) else s for s in scratch],
+            compiler_params=pltpu.CompilerParams(vmem_limit_bytes=mib * 1024 * 1024),
             cost_estimate=cost,
         )(*args)
 
     return run
+
+
+def cost(us):
+    return pl.CostEstimate(flops=int(us * 1e6), bytes_accessed=int(us * 3e6), transcendentals=0)
 
 
 def swap(to_left, to_right, axis):
@@ -506,24 +555,30 @@
 def local(right_side, phase, deflation_weights, coarse_inverse):
     pos = jnp.stack([lax.axis_index(a) for a in AXES]).astype(jnp.int32)
     block = (CX, CY, CZ)
-    tall = (PX, PY, PZ)
-    r, v = right_side, deflation_weights
+    tall = (2, PX, PY, CZ)
+    split = (PX, ROWS, 8, PZ)
     n_x = H_R + H_G + H_V
-    xl, xr, send = call(start_kernel, [(n_x, CY, CZ), (n_x, CY, CZ), (NDEV, 128)])(r, phase, v)
+    xl, xr, send, r, g, v = call(
+        start_kernel,
+        [(n_x, CY, CZ), (n_x, CY, CZ), (NDEV, 128), block, block, block],
+        scratch=[pltpu.VMEM(block, jnp.int32), pltpu.SemaphoreType.DMA((3,))],
+        hbm=3,
+    )(right_side, phase, deflation_weights)
     fl, fr = swap(xl, xr, "gx")
     sums = gather(send)
-    yl, yr = call(y_kernel, [(N_ALL, HY, CZ)] * 2)(r, phase, v, fl, fr)
+    fl, fr, sums = lax.optimization_barrier((fl, fr, sums))
+    yl, yr = call(y_kernel, [(N_ALL, HY, CZ)] * 2)(r, g, v, fl, fr)
     yd, yu = swap(yl, yr, "gy")
-    ext, zl, zr = call(z_kernel, [(N_ALL, PY, CZ), (GROUPS, PY, CZ), (GROUPS, PY, CZ)])(r, phase, v, fl, fr, yd, yu)
+    ext, zl, zr = call(z_kernel, [(N_ALL, PY, CZ), (GROUPS, PY, CZ), (GROUPS, PY, CZ)])(r, g, v, fl, fr, yd, yu)
     zfl, zfr = swap(zl, zr, "gz")
     p, xl, xr, labels, v_wide = call(
         smooth_kernel,
-        [block, (HX, CY, CZ), (HX, CY, CZ), tall, (N_V, PY, PZ)],
-        scratch=[(6, *tall), tall, tall, tall],
+        [block, (HX, CY, CZ), (HX, CY, CZ), tall, (2, N_V, PY, CZ)],
+        scratch=[(2, N_R, PY, CZ), (6, *split), split, split, split],
         smem=True,
     )(pos, ext, zfl, zfr, sums, coarse_inverse)
     fl, fr = swap(xl, xr, "gx")
-    quads = call(product_kernel, (4, 128), cost=pl.CostEstimate(flops=8_000_000, bytes_accessed=3_000_000, transcendentals=0))(
+    quads = call(product_kernel, (4, 128), cost=cost(1))(
         labels, v_wide
     )
     yl, yr = call(y2_kernel, [(PX, HY, CZ)] * 2)(p, fl, fr)
@@ -533,13 +588,13 @@
     q, c, y, send = call(
         image_kernel,
         [block, block, block, (NDEV, 384)],
-        scratch=[tall, (6, *tall), tall, tall, tall],
+        scratch=[tall, (CX, PY, CZ), (6, *split), split, split, split],
         smem=True,
     )(pos, ext, zfl, zfr, labels, r, v, quads)
     sums = gather(send)
     send = call(amounts_kernel, (NDEV, 128), scratch=[(NDEV, 128)])(sums, coarse_inverse, p, q, c, y, v, r)
     got = gather(send)
-    pressure, residual = call(final_kernel, [block, block], scratch=[(N_V, PY, PZ)], smem=True)(
+    pressure, residual = call(final_kernel, [block, block], scratch=[(2, N_V, PY, CZ)], smem=True)(
         pos, sums, got, p, q, c, y, r, v_wide, labels
     )
     return (pressure, residual)

time: 134 us -> 116 us (0.87)
  blocking collectives: 33.2 us -> 52.9 us
  Pallas kernels: 35.7 us -> 22.6 us
  starting transfers between devices: 29.6 us -> 17.1 us
  waiting for transfers between devices: 31.5 us -> 19 us
    all_to_all x2 -> x3, blocking collectives: 33.2 us -> 52.9 us  [gather(): return lax.all_to_all(rows, AXES, 0, 0, tiled=True)]
    pallas_call x10, Pallas kernels: 35.7 us -> 22.6 us  [run(): pl.pallas_call(kernel, out_shape=[jax.ShapeDtypeStruct(s, F32) for s in o...]
    all_to_all x1 -> x0, starting transfers between devices: 9.85 us -> none  [gather(): return lax.all_to_all(rows, AXES, 0, 0, tiled=True)]
    all_to_all x1 -> x0, waiting for transfers between devices: 9.2 us -> none  [gather(): return lax.all_to_all(rows, AXES, 0, 0, tiled=True)]
    ppermute x6, waiting for transfers between devices: 19.6 us -> 13.5 us  [swap(): lax.ppermute(to_right, axis, [(i, (i + 1) % count) for i in range(count)])]
    ppermute x6, starting transfers between devices: 12.3 us -> 8.02 us  [swap(): lax.ppermute(to_right, axis, [(i, (i + 1) % count) for i in range(count)])]
    ppermute x6, waiting for transfers between devices: 2.69 us -> 5.46 us  [swap(): lax.ppermute(to_left, axis, [((i + 1) % count, i) for i in range(count)])]
    ppermute x6, starting transfers between devices: 7.51 us -> 9.04 us  [swap(): lax.ppermute(to_left, axis, [((i + 1) % count, i) for i in range(count)])]
  transfers between devices with their start and end apart: 13 -> 12, of which waited for: 7 -> 7; matrix products, arithmetic and copies ran while one was open for 0% -> 0% of each run, Pallas kernels for 1% -> 1%
where the time goes in v2:
time: 116 us; the launch traced here: 115 us
  blocking collectives  52.9 us (46%)
  Pallas kernels  22.6 us (19%)
  waiting for transfers between devices  19 us (16%)
  starting transfers between devices  17.1 us (15%)
  local copies, waits for them, and re-layouts  3.06 us (3%)
    all_to_all x3, blocking collectives, gather(): return lax.all_to_all(rows, AXES, 0, 0, tiled=True)  52.9 us
    pallas_call x10, Pallas kernels, run(): pl.pallas_call(kernel, out_shape=[jax.ShapeDtypeStruct(s, F32) for s in o...  22.6 us
    ppermute x6, waiting for transfers between devices, swap(): lax.ppermute(to_right, axis, [(i, (i + 1) % count) for i in range(count)])  13.5 us
    ppermute x6, starting transfers between devices, swap(): lax.ppermute(to_left, axis, [((i + 1) % count, i) for i in range(count)])  9.04 us
    ppermute x6, starting transfers between devices, swap(): lax.ppermute(to_right, axis, [(i, (i + 1) % count) for i in range(count)])  8.02 us
    ppermute x6, waiting for transfers between devices, swap(): lax.ppermute(to_left, axis, [((i + 1) % count, i) for i in range(count)])  5.46 us
    unnamed x9, local copies, waits for them, and re-layouts  2.86 us
  transfers between devices with their start and end apart: 12, of which 7 were waited for; matrix products, arithmetic and copies ran while one was open for 0% of the time, Pallas kernels for 1%

profile of v2, /device:TPU:1, one launch (start us, length us, event | category | flops | bytes accessed | tf_op | source)
XLA Modules:
  0.0 115.4 jit_solution(7010028959019529161)
XLA Ops:
  0.6 0.0 copy-start.1
  0.6 0.9 copy-done.1
  1.6 0.0 copy-start.2
  1.6 0.9 copy-done.2
  2.5 0.0 copy-start.3
  2.5 0.9 copy-done.3
  3.5 0.4 shard_map.59
  3.9 2.1 %collective-permute-start = (f32[13,64,128]{2,1,0:T(8,128)S(1)}, f32[13,64,128]{2,1,0:T(8,128)S(1)}, u32[]{:S(2)}, u32[]{:S(2)}) collective-permute-start(f32[13,64,128]{2,1,0:T(8,128)S(1)} %get-tuple-element.33), channel_id=1, source_target_pairs={{0,32},{32,64},{64,96},{96,0},{1,33},{33,65},{65,97},{97,1},{2,34}... | collective-permute-start | bytes 1277960 | tf_op jit(solution)/shard_map/ppermute | solution.py:547
  6.0 1.3 %collective-permute-start.1 = (f32[13,64,128]{2,1,0:T(8,128)S(1)}, f32[13,64,128]{2,1,0:T(8,128)S(1)}, u32[]{:S(2)}, u32[]{:S(2)}) collective-permute-start(f32[13,64,128]{2,1,0:T(8,128)S(1)} %get-tuple-element.34), channel_id=1, source_target_pairs={{32,0},{64,32},{96,64},{0,96},{33,1},{65,33},{97,65},{1,97},{34,2}... | collective-permute-start | bytes 1277960 | tf_op jit(solution)/shard_map/ppermute | solution.py:546
  7.3 19.3 %all_to_all.34 = f32[128,1,128]{2,1,0:T(1,128)S(1)} all-to-all(f32[128,1,128]{2,1,0:T(1,128)S(1)} %bitcast.21), channel_id=1, replica_groups=mesh['gx'=4,'gy'=4,'gz'=8] {'gx','gy','gz'}, dimensions={0} | all-to-all | bytes 131072 | tf_op jit(solution)/shard_map/all_to_all | solution.py:552
  26.6 0.0 collective-permute-done.fl_ref
  26.6 0.0 collective-permute-done.1.fr_ref
  26.7 0.4 collective-permute-start.2
  27.1 2.3 %collective-permute-start.3 = (f32[50,8,128]{2,1,0:T(8,128)S(1)}, f32[50,8,128]{2,1,0:T(8,128)S(1)}, u32[]{:S(2)}, u32[]{:S(2)}) collective-permute-start(f32[50,8,128]{2,1,0:T(8,128)S(1)} %get-tuple-element.39), channel_id=1, source_target_pairs={{8,0},{16,8},{24,16},{0,24},{9,1},{17,9},{25,17},{1,25},{10,2},{18... | collective-permute-start | bytes 614408 | tf_op jit(solution)/shard_map/ppermute | solution.py:546
  29.4 3.9 %collective-permute-done.2.yd_ref = f32[50,8,128]{2,1,0:T(8,128)S(1)} collective-permute-done((f32[50,8,128]{2,1,0:T(8,128)S(1)}, f32[50,8,128]{2,1,0:T(8,128)S(1)}, u32[]{:S(2)}, u32[]{:S(2)}) %collective-permute-start.2) | collective-permute-done | bytes 204832 | tf_op jit(solution)/shard_map/ppermute | solution.py:547
  33.3 0.0 collective-permute-done.3.yu_ref
  33.3 1.1 shard_map.61
  34.4 2.6 %collective-permute-start.4 = (f32[4,80,128]{2,1,0:T(8,128)S(1)}, f32[4,80,128]{2,1,0:T(8,128)S(1)}, u32[]{:S(2)}, u32[]{:S(2)}) collective-permute-start(f32[4,80,128]{2,1,0:T(8,128)S(1)} %get-tuple-element.41), channel_id=1, source_target_pairs={{0,1},{1,2},{2,3},{3,4},{4,5},{5,6},{6,7},{7,0},{8,9},{9,10},{10,1... | collective-permute-start | bytes 491528 | tf_op jit(solution)/shard_map/ppermute | solution.py:547
  37.0 0.0 collective-permute-start.5
  37.0 0.1 pad_add_fusion.pos
  37.0 2.2 %collective-permute-done.4.zl_ref = f32[4,80,128]{2,1,0:T(8,128)S(1)} collective-permute-done((f32[4,80,128]{2,1,0:T(8,128)S(1)}, f32[4,80,128]{2,1,0:T(8,128)S(1)}, u32[]{:S(2)}, u32[]{:S(2)}) %collective-permute-start.4) | collective-permute-done | bytes 163872 | tf_op jit(solution)/shard_map/ppermute | solution.py:547
  39.2 2.8 %collective-permute-done.5.zr_ref = f32[4,80,128]{2,1,0:T(8,128)S(1)} collective-permute-done((f32[4,80,128]{2,1,0:T(8,128)S(1)}, f32[4,80,128]{2,1,0:T(8,128)S(1)}, u32[]{:S(2)}, u32[]{:S(2)}) %collective-permute-start.5) | collective-permute-done | bytes 163872 | tf_op jit(solution)/shard_map/ppermute | solution.py:546
  42.0 7.8 %shard_map.62 = (f32[8,64,128]{2,1,0:T(8,128)S(1)}, f32[7,64,128]{2,1,0:T(8,128)S(1)}, f32[7,64,128]{2,1,0:T(8,128)S(1)}, f32[2,22,80,128]{3,2,1,0:T(8,128)S(1)}, f32[2,10,80,128]{3,2,1,0:T(8,128)S(1)}) custom-call(s32[3]{0:T(128)S(1)} %pad_add_fusion.pos, f32[50,80,128]{2,1,0:T(8,128)S(1)} %get-tuple-element.40.ext_ref, ...), custom_call_target="tpu_custom_call" | custom-call | tf_op jit(solution)/shard_map/pallas_call | solution.py:527
  49.7 0.3 collective-permute-start.6
  50.1 2.4 %collective-permute-start.7 = (f32[7,64,128]{2,1,0:T(8,128)S(1)}, f32[7,64,128]{2,1,0:T(8,128)S(1)}, u32[]{:S(2)}, u32[]{:S(2)}) collective-permute-start(f32[7,64,128]{2,1,0:T(8,128)S(1)} %get-tuple-element.46), channel_id=1, source_target_pairs={{32,0},{64,32},{96,64},{0,96},{33,1},{65,33},{97,65},{1,97},{34,2}... | collective-permute-start | bytes 688136 | tf_op jit(solution)/shard_map/ppermute | solution.py:546
  52.5 5.2 %collective-permute-done.6.fl_ref = f32[7,64,128]{2,1,0:T(8,128)S(1)} collective-permute-done((f32[7,64,128]{2,1,0:T(8,128)S(1)}, f32[7,64,128]{2,1,0:T(8,128)S(1)}, u32[]{:S(2)}, u32[]{:S(2)}) %collective-permute-start.6) | collective-permute-done | bytes 229408 | tf_op jit(solution)/shard_map/ppermute | solution.py:547
  57.7 0.0 collective-permute-done.7.fr_ref
  57.7 0.1 collective-permute-start.8
  57.8 2.9 %collective-permute-start.9 = (f32[22,8,128]{2,1,0:T(8,128)S(1)}, f32[22,8,128]{2,1,0:T(8,128)S(1)}, u32[]{:S(2)}, u32[]{:S(2)}) collective-permute-start(f32[22,8,128]{2,1,0:T(8,128)S(1)} %get-tuple-element.48), channel_id=1, source_target_pairs={{8,0},{16,8},{24,16},{0,24},{9,1},{17,9},{25,17},{1,25},{10,2},{18... | collective-permute-start | bytes 270344 | tf_op jit(solution)/shard_map/ppermute | solution.py:546
  60.7 1.7 %collective-permute-done.8.yd_ref = f32[22,8,128]{2,1,0:T(8,128)S(1)} collective-permute-done((f32[22,8,128]{2,1,0:T(8,128)S(1)}, f32[22,8,128]{2,1,0:T(8,128)S(1)}, u32[]{:S(2)}, u32[]{:S(2)}) %collective-permute-start.8) | collective-permute-done | bytes 90144 | tf_op jit(solution)/shard_map/ppermute | solution.py:547
  62.4 0.0 collective-permute-done.9.yu_ref
  62.4 0.5 shard_map.64
  62.9 2.5 %collective-permute-start.10 = (f32[2,80,128]{2,1,0:T(8,128)S(1)}, f32[2,80,128]{2,1,0:T(8,128)S(1)}, u32[]{:S(2)}, u32[]{:S(2)}) collective-permute-start(f32[2,80,128]{2,1,0:T(8,128)S(1)} %get-tuple-element.50), channel_id=1, source_target_pairs={{0,1},{1,2},{2,3},{3,4},{4,5},{5,6},{6,7},{7,0},{8,9},{9,10},{10,1... | collective-permute-start | bytes 245768 | tf_op jit(solution)/shard_map/ppermute | solution.py:547
  65.4 0.0 collective-permute-start.11
  65.4 0.9 shard_map.65.e_ref
  66.3 0.6 collective-permute-done.10.zl_ref
  66.9 2.7 %collective-permute-done.11.zr_ref = f32[2,80,128]{2,1,0:T(8,128)S(1)} collective-permute-done((f32[2,80,128]{2,1,0:T(8,128)S(1)}, f32[2,80,128]{2,1,0:T(8,128)S(1)}, u32[]{:S(2)}, u32[]{:S(2)}) %collective-permute-start.11) | collective-permute-done | bytes 81952 | tf_op jit(solution)/shard_map/ppermute | solution.py:546
  69.6 0.0 copy-start
  69.6 8.8 %shard_map.66 = (f32[8,64,128]{2,1,0:T(8,128)S(1)}, f32[8,64,128]{2,1,0:T(8,128)S(1)}, f32[8,64,128]{2,1,0:T(8,128)S(1)}, f32[128,384]{1,0:T(8,128)S(1)}) custom-call(s32[3]{0:T(128)S(1)} %pad_add_fusion.pos, f32[22,80,128]{2,1,0:T(8,128)S(1)} %get-tuple-element.49.ext_ref, f32[2,80,128]{2,1,0:T(8,128)S(1)} %collective-permute-done.10.zl_ref, ...), custom_call_target="tpu_custom_call" | custom-call | tf_op jit(solution)/shard_map/pallas_call | solution.py:527
  78.4 0.2 copy.7
  78.6 20.0 %all_to_all.35 = f32[128,1,384]{2,1,0:T(1,128)S(1)} all-to-all(f32[128,1,384]{2,1,0:T(1,128)S(1)} %copy.7), channel_id=1, replica_groups=mesh['gx'=4,'gy'=4,'gz'=8] {'gx','gy','gz'}, dimensions={0} | all-to-all | bytes 393216 | tf_op jit(solution)/shard_map/all_to_all | solution.py:552
  98.6 0.0 copy-done
  98.6 0.7 shard_map.67
  99.3 13.6 %all_to_all.36 = f32[128,1,128]{2,1,0:T(1,128)S(1)} all-to-all(f32[128,1,128]{2,1,0:T(1,128)S(1)} %bitcast.19), channel_id=1, replica_groups=mesh['gx'=4,'gy'=4,'gz'=8] {'gx','gy','gz'}, dimensions={0} | all-to-all | bytes 131072 | tf_op jit(solution)/shard_map/all_to_all | solution.py:552
  112.9 2.5 %shard_map.68 = (f32[8,64,128]{2,1,0:T(8,128)}, f32[8,64,128]{2,1,0:T(8,128)}) custom-call(s32[3]{0:T(128)S(1)} %pad_add_fusion.pos, f32[128,384]{1,0:T(8,128)S(1)} %bitcast.16, f32[128,128]{1,0:T(8,128)S(1)} %bitcast.18, f32[8,64,128]{2,1,0:T(8,128)S(1)} %get-tuple-element.44.p_ref, f32[8,64,128]{2,1,0:T(8,128)S(1)} %get-tuple-element.55.q_ref, ...), custom_call_target="tpu_custom_call" | custom-call | tf_op jit(solution)/shard_map/pallas_call | solution.py:527
  (3 shorter events, 0.1 us)
Async XLA Ops:
  0.6 1.0 copy-start.1
  1.6 0.9 copy-start.2
  2.5 0.9 copy-start.3
  3.9 22.8 %collective-permute-start = (f32[13,64,128]{2,1,0:T(8,128)S(1)}, f32[13,64,128]{2,1,0:T(8,128)S(1)}, u32[]{:S(2)}, u32[]{:S(2)}) collective-permute-start(f32[13,64,128]{2,1,0:T(8,128)S(1)} %get-tuple-element.33), channel_id=1, source_target_pairs={{0,32},{32,64},{64,96},{96,0},{1,33},{33,65},{65,97},{97,1},{2,34}... | collective-permute-start | bytes 1277960 | tf_op jit(solution)/shard_map/ppermute | solution.py:547
  6.0 20.6 %collective-permute-start.1 = (f32[13,64,128]{2,1,0:T(8,128)S(1)}, f32[13,64,128]{2,1,0:T(8,128)S(1)}, u32[]{:S(2)}, u32[]{:S(2)}) collective-permute-start(f32[13,64,128]{2,1,0:T(8,128)S(1)} %get-tuple-element.34), channel_id=1, source_target_pairs={{32,0},{64,32},{96,64},{0,96},{33,1},{65,33},{97,65},{1,97},{34,2}... | collective-permute-start | bytes 1277960 | tf_op jit(solution)/shard_map/ppermute | solution.py:546
  26.7 6.6 %collective-permute-start.2 = (f32[50,8,128]{2,1,0:T(8,128)S(1)}, f32[50,8,128]{2,1,0:T(8,128)S(1)}, u32[]{:S(2)}, u32[]{:S(2)}) collective-permute-start(f32[50,8,128]{2,1,0:T(8,128)S(1)} %get-tuple-element.38), channel_id=1, source_target_pairs={{0,8},{8,16},{16,24},{24,0},{1,9},{9,17},{17,25},{25,1},{2,10},{10... | collective-permute-start | bytes 614408 | tf_op jit(solution)/shard_map/ppermute | solution.py:547
  27.1 6.2 %collective-permute-start.3 = (f32[50,8,128]{2,1,0:T(8,128)S(1)}, f32[50,8,128]{2,1,0:T(8,128)S(1)}, u32[]{:S(2)}, u32[]{:S(2)}) collective-permute-start(f32[50,8,128]{2,1,0:T(8,128)S(1)} %get-tuple-element.39), channel_id=1, source_target_pairs={{8,0},{16,8},{24,16},{0,24},{9,1},{17,9},{25,17},{1,25},{10,2},{18... | collective-permute-start | bytes 614408 | tf_op jit(solution)/shard_map/ppermute | solution.py:546
  34.4 4.9 %collective-permute-start.4 = (f32[4,80,128]{2,1,0:T(8,128)S(1)}, f32[4,80,128]{2,1,0:T(8,128)S(1)}, u32[]{:S(2)}, u32[]{:S(2)}) collective-permute-start(f32[4,80,128]{2,1,0:T(8,128)S(1)} %get-tuple-element.41), channel_id=1, source_target_pairs={{0,1},{1,2},{2,3},{3,4},{4,5},{5,6},{6,7},{7,0},{8,9},{9,10},{10,1... | collective-permute-start | bytes 491528 | tf_op jit(solution)/shard_map/ppermute | solution.py:547
  37.0 5.0 %collective-permute-start.5 = (f32[4,80,128]{2,1,0:T(8,128)S(1)}, f32[4,80,128]{2,1,0:T(8,128)S(1)}, u32[]{:S(2)}, u32[]{:S(2)}) collective-permute-start(f32[4,80,128]{2,1,0:T(8,128)S(1)} %get-tuple-element.42), channel_id=1, source_target_pairs={{1,0},{2,1},{3,2},{4,3},{5,4},{6,5},{7,6},{0,7},{9,8},{10,9},{11,1... | collective-permute-start | bytes 491528 | tf_op jit(solution)/shard_map/ppermute | solution.py:546
  49.7 8.0 %collective-permute-start.6 = (f32[7,64,128]{2,1,0:T(8,128)S(1)}, f32[7,64,128]{2,1,0:T(8,128)S(1)}, u32[]{:S(2)}, u32[]{:S(2)}) collective-permute-start(f32[7,64,128]{2,1,0:T(8,128)S(1)} %get-tuple-element.45), channel_id=1, source_target_pairs={{0,32},{32,64},{64,96},{96,0},{1,33},{33,65},{65,97},{97,1},{2,34}... | collective-permute-start | bytes 688136 | tf_op jit(solution)/shard_map/ppermute | solution.py:547
  50.1 7.7 %collective-permute-start.7 = (f32[7,64,128]{2,1,0:T(8,128)S(1)}, f32[7,64,128]{2,1,0:T(8,128)S(1)}, u32[]{:S(2)}, u32[]{:S(2)}) collective-permute-start(f32[7,64,128]{2,1,0:T(8,128)S(1)} %get-tuple-element.46), channel_id=1, source_target_pairs={{32,0},{64,32},{96,64},{0,96},{33,1},{65,33},{97,65},{1,97},{34,2}... | collective-permute-start | bytes 688136 | tf_op jit(solution)/shard_map/ppermute | solution.py:546
  57.7 4.7 %collective-permute-start.8 = (f32[22,8,128]{2,1,0:T(8,128)S(1)}, f32[22,8,128]{2,1,0:T(8,128)S(1)}, u32[]{:S(2)}, u32[]{:S(2)}) collective-permute-start(f32[22,8,128]{2,1,0:T(8,128)S(1)} %get-tuple-element.47), channel_id=1, source_target_pairs={{0,8},{8,16},{16,24},{24,0},{1,9},{9,17},{17,25},{25,1},{2,10},{10... | collective-permute-start | bytes 270344 | tf_op jit(solution)/shard_map/ppermute | solution.py:547
  57.8 4.6 %collective-permute-start.9 = (f32[22,8,128]{2,1,0:T(8,128)S(1)}, f32[22,8,128]{2,1,0:T(8,128)S(1)}, u32[]{:S(2)}, u32[]{:S(2)}) collective-permute-start(f32[22,8,128]{2,1,0:T(8,128)S(1)} %get-tuple-element.48), channel_id=1, source_target_pairs={{8,0},{16,8},{24,16},{0,24},{9,1},{17,9},{25,17},{1,25},{10,2},{18... | collective-permute-start | bytes 270344 | tf_op jit(solution)/shard_map/ppermute | solution.py:546
  62.9 4.0 %collective-permute-start.10 = (f32[2,80,128]{2,1,0:T(8,128)S(1)}, f32[2,80,128]{2,1,0:T(8,128)S(1)}, u32[]{:S(2)}, u32[]{:S(2)}) collective-permute-start(f32[2,80,128]{2,1,0:T(8,128)S(1)} %get-tuple-element.50), channel_id=1, source_target_pairs={{0,1},{1,2},{2,3},{3,4},{4,5},{5,6},{6,7},{7,0},{8,9},{9,10},{10,1... | collective-permute-start | bytes 245768 | tf_op jit(solution)/shard_map/ppermute | solution.py:547
  65.4 4.2 %collective-permute-start.11 = (f32[2,80,128]{2,1,0:T(8,128)S(1)}, f32[2,80,128]{2,1,0:T(8,128)S(1)}, u32[]{:S(2)}, u32[]{:S(2)}) collective-permute-start(f32[2,80,128]{2,1,0:T(8,128)S(1)} %get-tuple-element.51), channel_id=1, source_target_pairs={{1,0},{2,1},{3,2},{4,3},{5,4},{6,5},{7,6},{0,7},{9,8},{10,9},{11,1... | collective-permute-start | bytes 245768 | tf_op jit(solution)/shard_map/ppermute | solution.py:546
  69.6 29.0 %copy-start = (f32[64,8192]{1,0:T(8,128)S(1)}, f32[64,8192]{1,0:T(8,128)}, u32[]{:S(2)}) copy-start(f32[64,8192]{1,0:T(8,128)} %matrix_ref.3) | copy-start | bytes 6291460

commit v3 on v2

v3 whole, which is shorter than its diff:
```python
import functools

import jax
import jax.numpy as jnp
import numpy as np
from jax import lax
from jax.experimental import pallas as pl
from jax.experimental.pallas import tpu as pltpu
from jax.sharding import PartitionSpec as P

AXES = ("gx", "gy", "gz")
SBX = 4
ND = 64
DEG = 6
spectrum_low = 0.08
spectrum_high = 2.0

CX, CY, CZ = 8, 64, 128
HX, HY = 7, 8
PX, PY, PZ = CX + 2 * HX, CY + 2 * HY, 2 * CZ
H_R, H_G, H_V = 5, 7, 1
N_R, N_G, N_V = CX + 2 * H_R, CX + 2 * H_G, CX + 2 * H_V
N_ALL = N_R + N_G + N_V
GROUPS = -(-N_ALL // 16)
GROUPS_P = -(-PX // 16)
NDEV = 128
ROWS = PY // 8

LIQUID = np.float32(1.0)
GAS = np.float32(0.001)
F_LL = np.float32(2.0) / (LIQUID + LIQUID)
F_LG = np.float32(2.0) / (LIQUID + GAS)
F_GG = np.float32(2.0) / (GAS + GAS)

F32 = jnp.float32
EXACT = lax.Precision.HIGHEST


def recurrence():
    center = 0.5 * (spectrum_high + spectrum_low)
    half_width = 0.5 * (spectrum_high - spectrum_low)
    ratio = center / half_width
    earlier = 1.0 / ratio
    weights = []
    for index in range(DEG - 1):
        later = 1.0 / (2.0 * ratio - earlier)
        weights.append((later * earlier, 2.0 * later / half_width))
        earlier = later
    return (1.0 / center, weights)


def iota(shape, dim):
    return lax.broadcasted_iota(jnp.int32, shape, dim)


def whole(ref, i):
    return jnp.concatenate([ref[0, i], ref[1, i]], axis=1)


def put(ref, i, plane):
    ref[0, i] = plane[:, 0:CZ]
    ref[1, i] = plane[:, CZ:PZ]


def neighbours(ref, i):
    v = whole(ref, i)
    return (
        whole(ref, i - 1),
        whole(ref, i + 1),
        pltpu.roll(v, 1, 0),
        pltpu.roll(v, PY - 1, 0),
        pltpu.roll(v, 1, 1),
        pltpu.roll(v, PZ - 1, 1),
    )


def strided(ref, i, j):
    rows = pl.ds(j, 8, stride=ROWS)
    return jnp.concatenate([ref[0, i, rows, :], ref[1, i, rows, :]], axis=1)


def around_strided(load, i, j):
    v = load(i, j)
    return (
        load(i - 1, j),
        load(i + 1, j),
        load(i, j - 1) if j else pltpu.roll(load(i, ROWS - 1), 1, 0),
        load(i, j + 1) if j < ROWS - 1 else pltpu.roll(load(i, 0), 7, 0),
        pltpu.roll(v, 1, 1),
        pltpu.roll(v, PZ - 1, 1),
    )


def inside_yz(pos, j=None):
    gy, gz = pos[1], pos[2]
    shape = (PY, PZ) if j is None else (8, PZ)
    row = iota(shape, 0) if j is None else iota(shape, 0) * ROWS + j
    row = row - HY + gy * CY
    lane = iota(shape, 1)
    near = jnp.where(lane < CZ + CZ // 2, lane, lane - PZ) + gz * CZ
    kept = (lane < CZ + 8) | (lane >= PZ - 8)
    good = (row >= 0) & (row < 4 * CY) & (near >= 0) & (near < 8 * CZ) & kept
    return jnp.where(good, 1.0, 0.0).astype(F32)


def inside_x(pos, rel):
    x = pos[0] * CX + rel
    return jnp.where((x >= 0) & (x < 4 * CX), 1.0, 0.0).astype(F32)


def pair(labels):
    gas = labels > 0.5
    return jnp.where(gas, F_LG, F_LL), jnp.where(gas, F_GG - F_LG, F_LG - F_LL)


def row_sums(arrays):
    rows = []
    for parts in arrays:
        for part in parts:
            for sy in range(4):
                rows.append(jnp.sum(part[16 * sy : 16 * sy + 16], axis=0, keepdims=True))
    stacked = jnp.concatenate(rows, axis=0)
    pick = jnp.where(iota((128, 128), 0) // 32 == iota((128, 128), 1) % 4, 1.0, 0.0).astype(F32)
    spread = jnp.dot(stacked, pick, precision=EXACT, preferred_element_type=F32)
    keep = (iota((16, 128), 1) // 4) % 16 == iota((16, 128), 0)
    return [
        jnp.sum(jnp.where(keep, spread[16 * n : 16 * n + 16], 0.0), axis=0, keepdims=True) for n in range(len(arrays))
    ]


def fields(rows):
    count = len(rows)
    keep = (iota((16, 128), 1) // 4 == iota((16, 128), 0)) & (iota((16, 128), 1) < ND)
    tall = jnp.concatenate([jnp.where(keep, jnp.broadcast_to(r, (16, 128)), 0.0) for r in rows], axis=0)
    pick = jnp.where(iota((128, 128), 0) % 4 == iota((128, 128), 1) // 32, 1.0, 0.0).astype(F32)
    out = jnp.dot(tall, pick, precision=EXACT, preferred_element_type=F32)
    return [out[16 * k : 16 * k + 16] for k in range(count)]


def plane_field(field, sx):
    return jnp.concatenate(
        [jnp.broadcast_to(field[4 * sx + sy : 4 * sx + sy + 1], (16, 128)) for sy in range(4)], axis=0
    )


def coarse_rows(matrix_ref, even, odd):
    wide = jnp.where(iota((64, 128), 1) < ND, even, odd)
    total = matrix_ref[:, 0:128] * wide[0:1]
    for t in range(1, 64):
        total = total + matrix_ref[:, 128 * t : 128 * t + 128] * wide[t : t + 1]
    column = jnp.sum(total, axis=1, keepdims=True)
    keep = iota((64, 128), 1) % ND == iota((64, 128), 0)
    return jnp.sum(jnp.where(keep, column, 0.0), axis=0, keepdims=True)


def total_sum(x):
    return jnp.sum(jnp.sum(x, axis=0, keepdims=True), axis=1, keepdims=True)


def start_kernel(pos, r_in, phase_in, v_in, xa_ref, xb_ref, send_ref, r_ref, g_ref, v_ref, phase_ref, sem):
    pairs = ((r_in, r_ref), (v_in, v_ref), (phase_in, phase_ref))
    copies = [pltpu.make_async_copy(src, dst, sem.at[n]) for n, (src, dst) in enumerate(pairs)]
    for copy in copies:
        copy.start()
    for copy in copies:
        copy.wait()
    parts = []
    for sx in range(4):
        parts.append(r_ref[2 * sx] * v_ref[2 * sx] + r_ref[2 * sx + 1] * v_ref[2 * sx + 1])
    (row,) = row_sums([parts])
    send_ref[...] = jnp.broadcast_to(row, (NDEV, 128))
    g_ref[...] = jnp.where(phase_ref[...] == 1, 1.0, 0.0).astype(F32)
    even = is_even(pos, 0)
    for base, ref, halo in ((0, r_ref, H_R), (H_R, g_ref, H_G), (H_R + H_G, v_ref, H_V)):
        for k in range(halo):
            put_pair(even, xa_ref, xb_ref, base + k, ref[k], ref[CX - halo + k])


def is_even(pos, axis):
    return (pos[axis] & 1) == 0


def put_pair(even, a_ref, b_ref, k, down, up):
    a_ref[k] = jnp.where(even, up, down)
    b_ref[k] = jnp.where(even, down, up)


class Pair:
    def __init__(self, pos, axis, a_ref, b_ref):
        self.even, self.a, self.b = is_even(pos, axis), a_ref, b_ref

    def below(self, *at):
        return jnp.where(self.even, self.b[at], self.a[at])

    def above(self, *at):
        return jnp.where(self.even, self.a[at], self.b[at])


def stacked_planes(r_ref, g_ref, v_ref, sides):
    planes = []
    for halo, ref, base in ((H_R, r_ref, 0), (H_G, g_ref, H_R), (H_V, v_ref, H_R + H_G)):
        for rel in range(-halo, CX + halo):
            if rel < 0:
                planes.append(lambda s, k=base + rel + halo: sides.below(k, s))
            elif rel >= CX:
                planes.append(lambda s, k=base + rel - CX: sides.above(k, s))
            else:
                planes.append(lambda s, k=rel, ref=ref: ref[k, s])
    return planes


def padded_planes(p_ref, sides):
    planes = []
    for rel in range(-HX, CX + HX):
        if rel < 0:
            planes.append(lambda s, k=rel + HX: sides.below(k, s))
        elif rel >= CX:
            planes.append(lambda s, k=rel - CX: sides.above(k, s))
        else:
            planes.append(lambda s, k=rel: p_ref[k, s])
    return planes


def all_planes(refs, pos):
    sides = Pair(pos, 0, *refs[-2:])
    return padded_planes(refs[0], sides) if len(refs) == 3 else stacked_planes(*refs[:3], sides)


def y_kernel(pos, *refs):
    even = is_even(pos, 1)
    for k, plane in enumerate(all_planes(refs[:-2], pos)):
        put_pair(even, *refs[-2:], k, plane(pl.ds(0, HY)), plane(pl.ds(CY - HY, HY)))


def pack_lanes(values, rows):
    slot = iota((rows, CZ), 1) // 8
    packed = []
    for base in range(0, len(values), 16):
        left = right = jnp.zeros((rows, CZ), F32)
        for m, value in enumerate(values[base : base + 16]):
            value = value()
            left = jnp.where(slot == m, pltpu.roll(value, 8 * m, 1) if m else value, left)
            shift = (8 * m + 8) % CZ
            right = jnp.where(slot == m, pltpu.roll(value, shift, 1) if shift else value, right)
        packed.append((left, right))
    return packed


def z_own_kernel(pos, *refs):
    planes = all_planes(refs[:-2], pos)
    values = [lambda plane=plane: plane(pl.ds(0, CY)) for plane in planes]
    for group, (left, right) in enumerate(pack_lanes(values, CY)):
        refs[-2][group] = left
        refs[-1][group] = right


def z_kernel(pos, ya_ref, yb_ref, left_ref, right_ref, za_ref, zb_ref):
    even = is_even(pos, 2)
    sides = Pair(pos, 1, ya_ref, yb_ref)
    count = ya_ref.shape[0]
    below = pack_lanes([lambda k=k: sides.below(k) for k in range(count)], HY)
    above = pack_lanes([lambda k=k: sides.above(k) for k in range(count)], HY)
    for group in range(len(below)):
        left = jnp.concatenate([below[group][0], left_ref[group], above[group][0]], axis=0)
        right = jnp.concatenate([below[group][1], right_ref[group], above[group][1]], axis=0)
        put_pair(even, za_ref, zb_ref, group, left, right)


class Wide:
    def __init__(self, planes, pos, ya_ref, yb_ref, za_ref, zb_ref):
        self.planes = planes
        self.y = Pair(pos, 1, ya_ref, yb_ref)
        z = Pair(pos, 2, za_ref, zb_ref)
        groups = za_ref.shape[0]
        self.behind = [z.below(g) for g in range(groups)]
        self.ahead = [z.above(g) for g in range(groups)]

    def __call__(self, k):
        group, m = k // 16, k % 16
        lane = iota((PY, CZ), 1)
        shift = (CZ - 8 * m) % CZ
        ahead = pltpu.roll(self.ahead[group], shift, 1) if shift else self.ahead[group]
        shift = (CZ - 8 - 8 * m) % CZ
        behind = pltpu.roll(self.behind[group], shift, 1) if shift else self.behind[group]
        side = jnp.where(lane < 8, ahead, jnp.where(lane >= CZ - 8, behind, 0.0))
        middle = jnp.concatenate([self.y.below(k), self.planes[k](pl.ds(0, CY)), self.y.above(k)], axis=0)
        return jnp.concatenate([middle, side], axis=1)


def first_amounts_kernel(sums_ref, matrix_ref, out_ref):
    out_ref[...] = coarse_rows(matrix_ref, sums_ref[pl.ds(0, 64, stride=2), :], sums_ref[pl.ds(1, 64, stride=2), :])


def chebyshev(halo, w_ref, rp_ref, a_ref, b_ref):
    _, weights = recurrence()
    now, before = a_ref, b_ref
    for index, (keep, push) in enumerate(weights):
        halo -= 1
        for i in range(HX - halo, HX + CX + halo):
            for j in range(ROWS):
                around = around_strided(lambda i, j: now[i, j], i, j)
                total = rp_ref[i, j]
                for d in range(6):
                    total = total + w_ref[d, i, j] * around[d]
                new = (1.0 + keep - push) * now[i, j] + push * total
                if index:
                    new = new - keep * before[i, j]
                before[i, j] = new
        now, before = before, now
    return now


def smooth_kernel(
    pos, r_ref, g_in, v_in, xa_ref, xb_ref, ya_ref, yb_ref, za_ref, zb_ref, amounts_ref,
    p_ref, xa_out, xb_out, vx_ref, w_ref, diag_ref,
    g_ref, wide_ref, rp_ref, a_ref, b_ref, nat_ref,
):
    wide = Wide(stacked_planes(r_ref, g_in, v_in, Pair(pos, 0, xa_ref, xb_ref)), pos, ya_ref, yb_ref, za_ref, zb_ref)
    mask = inside_yz(pos)
    for i in range(PX):
        put(g_ref, i, wide(N_R + i) * (mask * inside_x(pos, i - HX)))
    for i in range(N_V):
        put(vx_ref, i, wide(N_R + N_G + i) * (mask * inside_x(pos, i - H_V)))
    for k in range(N_R):
        put(wide_ref, k, wide(k))
    first_scale, _ = recurrence()
    for j in range(ROWS):
        mask = inside_yz(pos, j)
        for i in range(1, PX - 1):
            labels = around_strided(lambda i, j: strided(g_ref, i, j), i, j)
            first, second = pair(strided(g_ref, i, j))
            count = (labels[0] + labels[1]) + (labels[2] + labels[3]) + (labels[4] + labels[5])
            diagonal = 6.0 * first + second * count
            if HX <= i < HX + CX:
                diag_ref[i - HX, j] = diagonal[:, 0:CZ]
            inverse = mask * inside_x(pos, i - HX) / diagonal
            first, second = first * inverse, second * inverse
            for d in range(6):
                w_ref[d, i, j] = first + second * labels[d]
            if HX - H_R <= i < HX + CX + H_R:
                scaled = strided(wide_ref, i - HX + H_R, j) * inverse
                rp_ref[i, j] = scaled
                a_ref[i, j] = scaled * first_scale
    result = chebyshev(H_R, w_ref, rp_ref, a_ref, b_ref)
    for j in range(ROWS):
        for x in range(CX):
            nat_ref[x, pl.ds(j, 8, stride=ROWS), :] = result[HX + x, j, :, 0:CZ]
    (field,) = fields([amounts_ref[...]])
    for x in range(CX):
        p_ref[x] = nat_ref[x, HY : HY + CY] + v_in[x] * plane_field(field, x // 2)
    even = is_even(pos, 0)
    for k in range(HX):
        put_pair(even, xa_out, xb_out, k, p_ref[k], p_ref[CX - HX + k])


def product_kernel(vx_ref, w_ref, diag_ref, out_ref, acc_ref):
    for j in range(ROWS):
        rows = pl.ds(j, 8, stride=ROWS)
        last_y = (iota((8, CZ), 0) * ROWS + j - HY) % 16 == 15
        last_z = iota((8, CZ), 1) % 32 == 31
        for sx in range(4):
            sums = [jnp.zeros((8, CZ), F32) for _ in range(4)]
            for x in (2 * sx, 2 * sx + 1):
                mine = strided(vx_ref, x + H_V, j)
                ahead = (
                    strided(vx_ref, x + H_V + 1, j),
                    strided(vx_ref, x + H_V, j + 1) if j < ROWS - 1 else pltpu.roll(strided(vx_ref, x + H_V, 0), 7, 0),
                    pltpu.roll(mine, PZ - 1, 1),
                )
                scaled = diag_ref[x, j] * mine[:, 0:CZ]
                cross = [scaled * w_ref[2 * d + 1, x + HX, j, :, 0:CZ] * ahead[d][:, 0:CZ] for d in range(3)]
                inner = jnp.where(last_y, 0.0, cross[1]) + jnp.where(last_z, 0.0, cross[2])
                if x % 2 == 0:
                    inner = inner + cross[0]
                else:
                    sums[1] = sums[1] - cross[0]
                sums[0] = sums[0] + (scaled * mine[:, 0:CZ] - 2.0 * inner)
                sums[2] = sums[2] - jnp.where(last_y, cross[1], 0.0)
                sums[3] = sums[3] - jnp.where(last_z, cross[2], 0.0)
            for n in range(4):
                acc_ref[4 * n + sx, rows, :] = sums[n]
    quads = row_sums([[acc_ref[4 * n + sx, HY : HY + CY] for sx in range(4)] for n in range(4)])
    for n in range(4):
        out_ref[n : n + 1] = quads[n]


def image_of(ref, w_ref, diag_ref, x, j):
    values = around_strided(lambda i, j: ref[i, j], x + HX, j)
    mine = ref[x + HX, j]
    total = w_ref[0, x + HX, j] * (mine - values[0])
    for d in range(1, 6):
        total = total + w_ref[d, x + HX, j] * (mine - values[d])
    return mine[:, 0:CZ], total[:, 0:CZ] * diag_ref[x, j]


def twice(x, half):
    lane = iota(x.shape, 1)
    other = pltpu.roll(x, ND, 1)
    return jnp.where(lane < ND, x, other) if half == 0 else jnp.where(lane < ND, other, x)


def ahead_behind(x, step, sign):
    lane = iota(x.shape, 1)
    stride, devices = ((16, 32), (4, 8), (1, 1))[step]
    place = (lane // stride) % 4
    near = pltpu.roll(x, (128 - stride * sign) % 128, 1)
    far = pltpu.roll(x, (3 * stride * sign) % 128, 1)
    far = pltpu.roll(far, (NDEV - devices * sign) % NDEV, 0)
    return jnp.where(place != (3 if sign > 0 else 0), near, far)


def image_kernel(
    pos, p_ref, xa_ref, xb_ref, ya_ref, yb_ref, za_ref, zb_ref, w_ref, diag_ref, r_ref, v_ref, e_ref,
    q_ref, c_ref, y_ref, send_ref,
    full_ref, plane_ref, rp_ref, a_ref, b_ref,
):
    wide = Wide(padded_planes(p_ref, Pair(pos, 0, xa_ref, xb_ref)), pos, ya_ref, yb_ref, za_ref, zb_ref)
    mask = inside_yz(pos)
    for i in range(PX):
        put(full_ref, i, wide(i) * (mask * inside_x(pos, i - HX)))
    first_scale, _ = recurrence()
    for j in range(ROWS):
        rows = pl.ds(j, 8, stride=ROWS)
        for i in range(1, PX - 1):
            values = around_strided(lambda i, j: strided(full_ref, i, j), i, j)
            mine = strided(full_ref, i, j)
            total = w_ref[0, i, j] * (mine - values[0])
            for d in range(1, 6):
                total = total + w_ref[d, i, j] * (mine - values[d])
            rp_ref[i, j] = total
            a_ref[i, j] = total * first_scale
            if HX <= i < HX + CX:
                plane_ref[i - HX, rows, :] = total[:, 0:CZ] * diag_ref[i - HX, j]
    result = chebyshev(HX - 1, w_ref, rp_ref, a_ref, b_ref)
    for x in range(CX):
        for j in range(ROWS):
            rows = pl.ds(j, 8, stride=ROWS)
            mine, image = image_of(result, w_ref, diag_ref, x, j)
            plane_ref[CX + x, rows, :] = mine
            plane_ref[2 * CX + x, rows, :] = image
    parts = [jnp.zeros((CY, CZ), F32) for _ in range(4)]
    energy = jnp.zeros((CY, CZ), F32)
    curve = jnp.zeros((CY, CZ), F32)
    for x in range(CX):
        q, c, y = (plane_ref[CX * n + x, HY : HY + CY] for n in range(3))
        q_ref[x], c_ref[x], y_ref[x] = q, c, y
        energy = energy + r_ref[x] * p_ref[x]
        curve = curve + q * p_ref[x]
        parts[x // 2] = parts[x // 2] + v_ref[x] * q
    lane = iota((1, 128), 1)
    scalars = jnp.where(lane == 64, total_sum(energy), jnp.where(lane == 65, total_sum(curve), 0.0))
    (row,) = row_sums([parts])
    send = jnp.concatenate(
        [
            jnp.where(lane < ND, row, e_ref[0:1]),
            jnp.where(lane < ND, e_ref[1:2], e_ref[2:3]),
            jnp.where(lane < ND, e_ref[3:4], scalars),
        ],
        axis=1,
    )
    send_ref[...] = jnp.broadcast_to(send, (NDEV, 384))


def first_scalars(sums_ref):
    totals = jnp.sum(sums_ref[:, 256:384], axis=0, keepdims=True)
    energy = totals[0:1, 64:65]
    curve = totals[0:1, 65:66]
    return energy, curve, energy / curve


def amounts_kernel(sums_ref, matrix_ref, p_ref, q_ref, c_ref, y_ref, v_ref, r_ref, send_ref, piece_ref):
    _, _, alpha = first_scalars(sums_ref)
    piece_ref[...] = sums_ref[:, 0:128]
    even = piece_ref[pl.ds(0, 64, stride=2), :]
    odd = pltpu.roll(piece_ref[pl.ds(1, 64, stride=2), :], 64, 1)
    amounts = coarse_rows(matrix_ref, even, odd)
    (field,) = fields([amounts])
    sums = [jnp.zeros((CY, CZ), F32) for _ in range(3)]
    for x in range(CX):
        lifted = v_ref[x] * plane_field(field, x // 2)
        p, q, c = p_ref[x], q_ref[x], c_ref[x]
        residual = r_ref[x] - alpha * q
        smooth = p - alpha * c
        smooth_image = q - alpha * y_ref[x]
        precond = smooth - alpha * lifted
        sums[0] = sums[0] + residual * precond
        sums[1] = sums[1] + precond * q
        sums[2] = sums[2] + smooth_image * (smooth - 2.0 * alpha * lifted)
    lane = iota((1, 128), 1)
    row = jnp.where(lane < ND, amounts, 0.0)
    for n in range(3):
        row = jnp.where(lane == ND + n, total_sum(sums[n]), row)
    send_ref[...] = jnp.broadcast_to(row, (NDEV, 128))


def final_kernel(
    pos, sums_ref, got_ref, p_ref, q_ref, c_ref, y_ref, r_ref, vx_ref, w_ref, diag_ref,
    pressure_ref, residual_ref,
    lift_ref, plane_ref,
):
    energy, curve, alpha = first_scalars(sums_ref)
    got = got_ref[...]
    dup = twice(got, 0)
    half = twice(sums_ref[:, 0:128], 1) * dup
    towards = (twice(sums_ref[:, 128:256], 0), twice(sums_ref[:, 128:256], 1), twice(sums_ref[:, 256:384], 0))
    for step in range(3):
        half = half + 2.0 * towards[step] * ahead_behind(dup, step, 1)
    quad = total_sum(jnp.where(iota((NDEV, 128), 1) < ND, half * dup, 0.0))
    totals = jnp.sum(got, axis=0, keepdims=True)
    energy_next = totals[0:1, 64:65]
    mixed = totals[0:1, 65:66]
    beta = energy_next / energy
    curve_next = totals[0:1, 66:67] + alpha * alpha * quad + 2.0 * beta * mixed + beta * beta * curve
    alpha_next = energy_next / curve_next

    me = (pos[0] * 4 + pos[1]) * 8 + pos[2]
    rows = []
    for shift in (0, -32, 32, -8, 8, -1, 1):
        at = jnp.clip(me + shift, 0, NDEV - 1)
        rows.append(got_ref[pl.ds(at, 1), :])
    mine, xm, xp, ym, yp, zm, zp = fields(rows)
    lanes = iota((PY, CZ), 1)
    zeros = jnp.zeros((HY, CZ), F32)
    for i in range(N_V):
        x = i - H_V
        if x < 0 or x >= CX:
            own = plane_field(xm, 3) if x < 0 else plane_field(xp, 0)
            middle = jnp.concatenate([zeros, own, zeros], axis=0)
            side = jnp.zeros((PY, CZ), F32)
        else:
            s = x // 2
            down = jnp.broadcast_to(ym[4 * s + 3 : 4 * s + 4], (HY, CZ))
            up = jnp.broadcast_to(yp[4 * s : 4 * s + 1], (HY, CZ))
            middle = jnp.concatenate([down, plane_field(mine, s), up], axis=0)
            ahead = jnp.concatenate([zeros, plane_field(zp, s), zeros], axis=0)
            behind = jnp.concatenate([zeros, plane_field(zm, s), zeros], axis=0)
            side = jnp.where(lanes < 8, ahead, jnp.where(lanes >= CZ - 8, behind, 0.0))
        lift_ref[0, i] = vx_ref[0, i] * middle
        lift_ref[1, i] = vx_ref[1, i] * side
    for x in range(CX):
        for j in range(ROWS):
            values = around_strided(lambda i, j: strided(lift_ref, i, j), x + H_V, j)
            mine = strided(lift_ref, x + H_V, j)
            total = w_ref[0, x + HX, j] * (mine - values[0])
            for d in range(1, 6):
                total = total + w_ref[d, x + HX, j] * (mine - values[d])
            plane_ref[x, pl.ds(j, 8, stride=ROWS), :] = total[:, 0:CZ] * diag_ref[x, j]
        lifted_image = plane_ref[x, HY : HY + CY]
        lifted = lift_ref[0, x + H_V, HY : HY + CY]
        p, q = p_ref[x], q_ref[x]
        precond = p - alpha * (c_ref[x] + lifted)
        precond_image = q - alpha * (y_ref[x] + lifted_image)
        direction = precond + beta * p
        image = precond_image + beta * q
        pressure_ref[x] = alpha * p + alpha_next * direction
        residual_ref[x] = (r_ref[x] - alpha * q) - alpha_next * image


VMEM = pl.BlockSpec(memory_space=pltpu.VMEM)
SMEM = pl.BlockSpec(memory_space=pltpu.SMEM)


def call(kernel, outs, scratch=(), smem=False, hbm=0, mib=20, cost=None):
    def run(*args):
        many = isinstance(outs, list)
        specs = [VMEM] * len(args)
        if smem:
            specs[0] = SMEM
        for n in range(int(smem), int(smem) + hbm):
            specs[n] = pl.BlockSpec(memory_space=pltpu.HBM)
        return pl.pallas_call(
            kernel,
            out_shape=[jax.ShapeDtypeStruct(s, F32) for s in outs] if many else jax.ShapeDtypeStruct(outs, F32),
            in_specs=specs,
            out_specs=[VMEM] * len(outs) if many else VMEM,
            scratch_shapes=[pltpu.VMEM(s, F32) if isinstance(s, tuple) else s for s in scratch],
            compiler_params=pltpu.CompilerParams(vmem_limit_bytes=mib * 1024 * 1024),
            cost_estimate=cost,
        )(*args)

    return run


def cost(us):
    return pl.CostEstimate(flops=int(us * 1e6), bytes_accessed=int(us * 3e6), transcendentals=0)


def swap(a, b, axis):
    count = lax.axis_size(axis)
    got_a = lax.ppermute(a, axis, [(i, i ^ 1) for i in range(count)])
    got_b = lax.ppermute(b, axis, [(i, (i - 1 if i % 2 == 0 else i + 1) % count) for i in range(count)])
    return got_a, got_b


def gather(rows):
    return lax.all_to_all(rows, AXES, 0, 0, tiled=True)


def exchange_yz(pos, own, count):
    groups = -(-count // 16)
    ya, yb = call(y_kernel, [(count, HY, CZ)] * 2, smem=True)(pos, *own)
    ya, yb = swap(ya, yb, "gy")
    left, right = call(z_own_kernel, [(groups, CY, CZ)] * 2, smem=True, cost=cost(1))(pos, *own)
    za, zb = call(z_kernel, [(groups, PY, CZ)] * 2, smem=True)(pos, ya, yb, left, right)
    return (ya, yb, *swap(za, zb, "gz"))


def local(right_side, phase, deflation_weights, coarse_inverse):
    pos = jnp.stack([lax.axis_index(a) for a in AXES]).astype(jnp.int32)
    block = (CX, CY, CZ)
    tall = (2, PX, PY, CZ)
    split = (PX, ROWS, 8, PZ)
    n_x = H_R + H_G + H_V
    xa, xb, send, r, g, v = call(
        start_kernel,
        [(n_x, CY, CZ), (n_x, CY, CZ), (NDEV, 128), block, block, block],
        scratch=[pltpu.VMEM(block, jnp.int32), pltpu.SemaphoreType.DMA((3,))],
        smem=True,
        hbm=3,
    )(pos, right_side, phase, deflation_weights)
    xa, xb = swap(xa, xb, "gx")
    sums = gather(send)
    xa, xb, sums = lax.optimization_barrier((xa, xb, sums))
    own = (r, g, v, xa, xb)
    halos = exchange_yz(pos, own, N_ALL)
    amounts = call(first_amounts_kernel, (1, 128), cost=cost(1))(sums, coarse_inverse)
    p, xa, xb, v_wide, w, diag = call(
        smooth_kernel,
        [block, (HX, CY, CZ), (HX, CY, CZ), (2, N_V, PY, CZ), (6, *split), (CX, ROWS, 8, CZ)],
        scratch=[tall, (2, N_R, PY, CZ), split, split, split, (CX, PY, CZ)],
        smem=True,
    )(pos, *own, *halos, amounts)
    own = (p, *swap(xa, xb, "gx"))
    quads = call(product_kernel, (4, 128), scratch=[(16, PY, CZ)], cost=cost(1))(v_wide, w, diag)
    halos = exchange_yz(pos, own, PX)
    q, c, y, send = call(
        image_kernel,
        [block, block, block, (NDEV, 384)],
        scratch=[tall, (3 * CX, PY, CZ), split, split, split],
        smem=True,
    )(pos, *own, *halos, w, diag, r, v, quads)
    sums = gather(send)
    send = call(amounts_kernel, (NDEV, 128), scratch=[(NDEV, 128)])(sums, coarse_inverse, p, q, c, y, v, r)
    got = gather(send)
    pressure, residual = call(
        final_kernel, [block, block], scratch=[(2, N_V, PY, CZ), (CX, PY, CZ)], smem=True
    )(pos, sums, got, p, q, c, y, r, v_wide, w, diag)
    return (pressure, residual)


def solution(mesh):
    return jax.shard_map(
        local,
        mesh=mesh,
        in_specs=(P(*AXES), P(*AXES), P(*AXES), P(AXES, None)),
        out_specs=(P(*AXES), P(*AXES)),
        check_vma=False,
    )
```

time: 116 us -> 112 us (0.966)
  blocking collectives: 52.9 us -> 47 us
  Pallas kernels: 22.6 us -> 25.9 us
  local copies, waits for them, and re-layouts: 3.06 us -> 4.66 us
  starting transfers between devices: 17.1 us -> 15.7 us
  waiting for transfers between devices: 19 us -> 17.7 us
    all_to_all x3, blocking collectives: 52.9 us -> 47 us  [gather(): return lax.all_to_all(rows, AXES, 0, 0, tiled=True)]
    pallas_call x10 -> x13, Pallas kernels: 22.6 us -> 25.9 us  [run(): pl.pallas_call(kernel, out_shape=[jax.ShapeDtypeStruct(s, F32) for s in o...]
    unnamed x9 -> x11, local copies, waits for them, and re-layouts: 2.86 us -> 4.46 us
    ppermute x12, starting transfers between devices: 17.1 us -> 15.7 us  [the longest x6 9.23 us: swap(): got_a = lax.ppermute(a, axis, [(i, i ^ 1) for i in range(count)])]
    ppermute x12, waiting for transfers between devices: 19 us -> 17.7 us  [the longest x6 9.68 us: swap(): lax.ppermute(b, axis, [(i, (i - 1 if i % 2 == 0 else i + 1) % count) for...]
  transfers between devices with their start and end apart: 12 -> 12, of which waited for: 7 -> 9; matrix products, arithmetic and copies ran while one was open for 0% -> 0% of each run, Pallas kernels for 1% -> 3%
where the time goes in v3:
time: 112 us
  blocking collectives  47 us (42%)
  Pallas kernels  25.9 us (23%)
  waiting for transfers between devices  17.7 us (16%)
  starting transfers between devices  15.7 us (14%)
  local copies, waits for them, and re-layouts  4.66 us (4%)
    all_to_all x3, blocking collectives, gather(): return lax.all_to_all(rows, AXES, 0, 0, tiled=True)  47 us
    pallas_call x13, Pallas kernels, run(): pl.pallas_call(kernel, out_shape=[jax.ShapeDtypeStruct(s, F32) for s in o...  25.9 us
    ppermute x6, waiting for transfers between devices, swap(): lax.ppermute(b, axis, [(i, (i - 1 if i % 2 == 0 else i + 1) % count) for...  9.68 us
    ppermute x6, starting transfers between devices, swap(): got_a = lax.ppermute(a, axis, [(i, i ^ 1) for i in range(count)])  9.23 us
    ppermute x6, waiting for transfers between devices, swap(): got_a = lax.ppermute(a, axis, [(i, i ^ 1) for i in range(count)])  8 us
    ppermute x6, starting transfers between devices, swap(): lax.ppermute(b, axis, [(i, (i - 1 if i % 2 == 0 else i + 1) % count) for...  6.46 us
    unnamed x11, local copies, waits for them, and re-layouts  4.46 us
  transfers between devices with their start and end apart: 12, of which 9 were waited for; matrix products, arithmetic and copies ran while one was open for 0% of the time, Pallas kernels for 3%

profile of v3, /device:TPU:1, one launch (start us, length us, event | category | flops | bytes accessed | tf_op | source)
XLA Modules:
  0.0 111.8 jit_solution(4380770868900990873)
XLA Ops:
  0.6 0.1 pad_add_fusion.pos
  0.7 0.0 copy-start.2
  0.7 0.9 copy-done.2
  1.7 0.9 copy-done.3
  2.6 0.9 copy-done.4
  3.6 0.9 shard_map.59
  4.5 2.1 %collective-permute-start = (f32[13,64,128]{2,1,0:T(8,128)S(1)}, f32[13,64,128]{2,1,0:T(8,128)S(1)}, u32[]{:S(2)}, u32[]{:S(2)}) collective-permute-start(f32[13,64,128]{2,1,0:T(8,128)S(1)} %get-tuple-element.36), channel_id=1, source_target_pairs={{0,32},{32,0},{64,96},{96,64},{1,33},{33,1},{65,97},{97,65},{2,34}... | collective-permute-start | bytes 1277960 | tf_op jit(solution)/shard_map/ppermute | solution.py:590
  6.6 1.8 %collective-permute-start.1 = (f32[13,64,128]{2,1,0:T(8,128)S(1)}, f32[13,64,128]{2,1,0:T(8,128)S(1)}, u32[]{:S(2)}, u32[]{:S(2)}) collective-permute-start(f32[13,64,128]{2,1,0:T(8,128)S(1)} %get-tuple-element.37), channel_id=1, source_target_pairs={{0,96},{32,64},{64,32},{96,0},{1,97},{33,65},{65,33},{97,1},{2,98}... | collective-permute-start | bytes 1277960 | tf_op jit(solution)/shard_map/ppermute | solution.py:591
  8.4 18.5 %all_to_all.34 = f32[128,1,128]{2,1,0:T(1,128)S(1)} all-to-all(f32[128,1,128]{2,1,0:T(1,128)S(1)} %bitcast.21), channel_id=1, replica_groups=mesh['gx'=4,'gy'=4,'gz'=8] {'gx','gy','gz'}, dimensions={0} | all-to-all | bytes 131072 | tf_op jit(solution)/shard_map/all_to_all | solution.py:596
  26.9 0.0 collective-permute-done.refs_3_.xa_ref
  26.9 0.0 collective-permute-done.1.refs_4_.xb_ref
  27.0 0.6 shard_map.60
  27.5 0.4 collective-permute-start.2
  28.0 1.3 %collective-permute-start.3 = (f32[50,8,128]{2,1,0:T(8,128)S(1)}, f32[50,8,128]{2,1,0:T(8,128)S(1)}, u32[]{:S(2)}, u32[]{:S(2)}) collective-permute-start(f32[50,8,128]{2,1,0:T(8,128)S(1)} %get-tuple-element.42), channel_id=1, source_target_pairs={{0,24},{8,16},{16,8},{24,0},{1,25},{9,17},{17,9},{25,1},{2,26},{10... | collective-permute-start | bytes 614408 | tf_op jit(solution)/shard_map/ppermute | solution.py:591
  29.3 1.4 %shard_map.61 = (f32[4,64,128]{2,1,0:T(8,128)S(1)}, f32[4,64,128]{2,1,0:T(8,128)S(1)}) custom-call(s32[3]{0:T(128)S(1)} %pad_add_fusion.pos, f32[8,64,128]{2,1,0:T(8,128)S(1)} %get-tuple-element.33.refs_0_.r_ref, f32[8,64,128]{2,1,0:T(8,128)S(1)} %get-tuple-element.34.refs_1_.g_in, f32[8,64,128]{2,1,0:T(8,128)S(1)} %get-tuple-element.35.refs_2_.v_in.v_ref, ...), custom_call_target="tpu_custom_call" | custom-call | flops 1000000 | bytes 3000000 | tf_op jit(solution)/shard_map/pallas_call | solution.py:571
  30.7 2.3 %collective-permute-done.2.ya_ref = f32[50,8,128]{2,1,0:T(8,128)S(1)} collective-permute-done((f32[50,8,128]{2,1,0:T(8,128)S(1)}, f32[50,8,128]{2,1,0:T(8,128)S(1)}, u32[]{:S(2)}, u32[]{:S(2)}) %collective-permute-start.2) | collective-permute-done | bytes 204832 | tf_op jit(solution)/shard_map/ppermute | solution.py:590
  33.0 1.3 %collective-permute-done.3.yb_ref = f32[50,8,128]{2,1,0:T(8,128)S(1)} collective-permute-done((f32[50,8,128]{2,1,0:T(8,128)S(1)}, f32[50,8,128]{2,1,0:T(8,128)S(1)}, u32[]{:S(2)}, u32[]{:S(2)}) %collective-permute-start.3) | collective-permute-done | bytes 204832 | tf_op jit(solution)/shard_map/ppermute | solution.py:591
  34.2 0.8 shard_map.62
  35.1 2.5 %collective-permute-start.4 = (f32[4,80,128]{2,1,0:T(8,128)S(1)}, f32[4,80,128]{2,1,0:T(8,128)S(1)}, u32[]{:S(2)}, u32[]{:S(2)}) collective-permute-start(f32[4,80,128]{2,1,0:T(8,128)S(1)} %get-tuple-element.45), channel_id=1, source_target_pairs={{0,1},{1,0},{2,3},{3,2},{4,5},{5,4},{6,7},{7,6},{8,9},{9,8},{10,11... | collective-permute-start | bytes 491528 | tf_op jit(solution)/shard_map/ppermute | solution.py:590
  37.6 0.5 collective-permute-start.5
  38.1 1.6 %copy-done = f32[64,8192]{1,0:T(8,128)S(1)} copy-done((f32[64,8192]{1,0:T(8,128)S(1)}, f32[64,8192]{1,0:T(8,128)}, u32[]{:S(2)}) %copy-start) | copy-done | bytes 2097176
  39.7 0.3 shard_map.63.amounts_ref
  40.0 0.0 collective-permute-done.4.za_ref
  40.0 2.6 %collective-permute-done.5.zb_ref = f32[4,80,128]{2,1,0:T(8,128)S(1)} collective-permute-done((f32[4,80,128]{2,1,0:T(8,128)S(1)}, f32[4,80,128]{2,1,0:T(8,128)S(1)}, u32[]{:S(2)}, u32[]{:S(2)}) %collective-permute-start.5) | collective-permute-done | bytes 163872 | tf_op jit(solution)/shard_map/ppermute | solution.py:591
  42.6 7.9 %shard_map.64 = (f32[8,64,128]{2,1,0:T(8,128)S(1)}, f32[7,64,128]{2,1,0:T(8,128)S(1)}, f32[7,64,128]{2,1,0:T(8,128)S(1)}, f32[2,10,80,128]{3,2,1,0:T(8,128)S(1)}...) custom-call(s32[3]{0:T(128)S(1)} %pad_add_fusion.pos, ...), custom_call_target="tpu_custom_call" | custom-call | tf_op jit(solution)/shard_map/pallas_call | solution.py:571
  50.5 0.4 collective-permute-start.6
  50.9 1.2 %collective-permute-start.7 = (f32[7,64,128]{2,1,0:T(8,128)S(1)}, f32[7,64,128]{2,1,0:T(8,128)S(1)}, u32[]{:S(2)}, u32[]{:S(2)}) collective-permute-start(f32[7,64,128]{2,1,0:T(8,128)S(1)} %get-tuple-element.50), channel_id=1, source_target_pairs={{0,96},{32,64},{64,32},{96,0},{1,97},{33,65},{65,33},{97,1},{2,98}... | collective-permute-start | bytes 688136 | tf_op jit(solution)/shard_map/ppermute | solution.py:591
  52.1 4.6 %collective-permute-done.6.refs_1_.xa_ref = f32[7,64,128]{2,1,0:T(8,128)S(1)} collective-permute-done((f32[7,64,128]{2,1,0:T(8,128)S(1)}, f32[7,64,128]{2,1,0:T(8,128)S(1)}, u32[]{:S(2)}, u32[]{:S(2)}) %collective-permute-start.6) | collective-permute-done | bytes 229408 | tf_op jit(solution)/shard_map/ppermute | solution.py:590
  56.7 1.2 %collective-permute-done.7.refs_2_.xb_ref = f32[7,64,128]{2,1,0:T(8,128)S(1)} collective-permute-done((f32[7,64,128]{2,1,0:T(8,128)S(1)}, f32[7,64,128]{2,1,0:T(8,128)S(1)}, u32[]{:S(2)}, u32[]{:S(2)}) %collective-permute-start.7) | collective-permute-done | bytes 229408 | tf_op jit(solution)/shard_map/ppermute | solution.py:591
  57.9 0.6 shard_map.65
  58.5 0.1 collective-permute-start.8
  58.6 1.4 %collective-permute-start.9 = (f32[22,8,128]{2,1,0:T(8,128)S(1)}, f32[22,8,128]{2,1,0:T(8,128)S(1)}, u32[]{:S(2)}, u32[]{:S(2)}) collective-permute-start(f32[22,8,128]{2,1,0:T(8,128)S(1)} %get-tuple-element.52), channel_id=1, source_target_pairs={{0,24},{8,16},{16,8},{24,0},{1,25},{9,17},{17,9},{25,1},{2,26},{10... | collective-permute-start | bytes 270344 | tf_op jit(solution)/shard_map/ppermute | solution.py:591
  60.0 1.0 shard_map.66
  61.0 1.0 collective-permute-done.8.ya_ref
  62.0 1.3 %collective-permute-done.9.yb_ref = f32[22,8,128]{2,1,0:T(8,128)S(1)} collective-permute-done((f32[22,8,128]{2,1,0:T(8,128)S(1)}, f32[22,8,128]{2,1,0:T(8,128)S(1)}, u32[]{:S(2)}, u32[]{:S(2)}) %collective-permute-start.9) | collective-permute-done | bytes 90144 | tf_op jit(solution)/shard_map/ppermute | solution.py:591
  63.3 0.7 shard_map.67
  64.0 3.7 %collective-permute-start.10 = (f32[2,80,128]{2,1,0:T(8,128)S(1)}, f32[2,80,128]{2,1,0:T(8,128)S(1)}, u32[]{:S(2)}, u32[]{:S(2)}) collective-permute-start(f32[2,80,128]{2,1,0:T(8,128)S(1)} %get-tuple-element.55), channel_id=1, source_target_pairs={{0,1},{1,0},{2,3},{3,2},{4,5},{5,4},{6,7},{7,6},{8,9},{9,8},{10,11... | collective-permute-start | bytes 245768 | tf_op jit(solution)/shard_map/ppermute | solution.py:590
  67.7 0.2 collective-permute-start.11
  67.9 0.6 shard_map.68.e_ref
  68.4 0.2 collective-permute-done.10.za_ref
  68.6 3.2 %collective-permute-done.11.zb_ref = f32[2,80,128]{2,1,0:T(8,128)S(1)} collective-permute-done((f32[2,80,128]{2,1,0:T(8,128)S(1)}, f32[2,80,128]{2,1,0:T(8,128)S(1)}, u32[]{:S(2)}, u32[]{:S(2)}) %collective-permute-start.11) | collective-permute-done | bytes 81952 | tf_op jit(solution)/shard_map/ppermute | solution.py:591
  71.8 8.3 %shard_map.69 = (f32[8,64,128]{2,1,0:T(8,128)S(1)}, f32[8,64,128]{2,1,0:T(8,128)S(1)}, f32[8,64,128]{2,1,0:T(8,128)S(1)}, f32[128,384]{1,0:T(8,128)S(1)}) custom-call(s32[3]{0:T(128)S(1)} %pad_add_fusion.pos, f32[8,64,128]{2,1,0:T(8,128)S(1)} %get-tuple-element.48.refs_0_.p_ref, f32[7,64,128]{2,1,0:T(8,128)S(1)} %collective-permute-done.6.refs_1_.xa_ref, ...), custom_call_target="tpu_custom_call" | custom-call | tf_op jit(solution)/shard_map/pallas_call | solution.py:571
  80.1 0.2 copy.7
  80.4 14.8 %all_to_all.35 = f32[128,1,384]{2,1,0:T(1,128)S(1)} all-to-all(f32[128,1,384]{2,1,0:T(1,128)S(1)} %copy.7), channel_id=1, replica_groups=mesh['gx'=4,'gy'=4,'gz'=8] {'gx','gy','gz'}, dimensions={0} | all-to-all | bytes 393216 | tf_op jit(solution)/shard_map/all_to_all | solution.py:596
  95.2 0.0 copy-done.1
  95.2 0.7 shard_map.70
  96.0 13.6 %all_to_all.36 = f32[128,1,128]{2,1,0:T(1,128)S(1)} all-to-all(f32[128,1,128]{2,1,0:T(1,128)S(1)} %bitcast.18), channel_id=1, replica_groups=mesh['gx'=4,'gy'=4,'gz'=8] {'gx','gy','gz'}, dimensions={0} | all-to-all | bytes 131072 | tf_op jit(solution)/shard_map/all_to_all | solution.py:596
  109.6 2.2 %shard_map.71 = (f32[8,64,128]{2,1,0:T(8,128)}, f32[8,64,128]{2,1,0:T(8,128)}) custom-call(s32[3]{0:T(128)S(1)} %pad_add_fusion.pos, f32[128,384]{1,0:T(8,128)S(1)} %bitcast.16, f32[128,128]{1,0:T(8,128)S(1)} %bitcast.17, f32[8,64,128]{2,1,0:T(8,128)S(1)} %get-tuple-element.48.refs_0_.p_ref, f32[8,64,128]{2,1,0:T(8,128)S(1)} %get-tuple-element.61.q_ref, ...), custom_call_target="tpu_custom_call" | custom-call | tf_op jit(solution)/shard_map/pallas_call | solution.py:571
  (5 shorter events, 0.0 us)
Async XLA Ops:
  0.7 1.0 copy-start.2
  1.7 0.9 copy-start.3
  2.6 0.9 copy-start.4
  4.5 22.4 %collective-permute-start = (f32[13,64,128]{2,1,0:T(8,128)S(1)}, f32[13,64,128]{2,1,0:T(8,128)S(1)}, u32[]{:S(2)}, u32[]{:S(2)}) collective-permute-start(f32[13,64,128]{2,1,0:T(8,128)S(1)} %get-tuple-element.36), channel_id=1, source_target_pairs={{0,32},{32,0},{64,96},{96,64},{1,33},{33,1},{65,97},{97,65},{2,34}... | collective-permute-start | bytes 1277960 | tf_op jit(solution)/shard_map/ppermute | solution.py:590
  6.6 20.3 %collective-permute-start.1 = (f32[13,64,128]{2,1,0:T(8,128)S(1)}, f32[13,64,128]{2,1,0:T(8,128)S(1)}, u32[]{:S(2)}, u32[]{:S(2)}) collective-permute-start(f32[13,64,128]{2,1,0:T(8,128)S(1)} %get-tuple-element.37), channel_id=1, source_target_pairs={{0,96},{32,64},{64,32},{96,0},{1,97},{33,65},{65,33},{97,1},{2,98}... | collective-permute-start | bytes 1277960 | tf_op jit(solution)/shard_map/ppermute | solution.py:591
  27.5 5.4 %collective-permute-start.2 = (f32[50,8,128]{2,1,0:T(8,128)S(1)}, f32[50,8,128]{2,1,0:T(8,128)S(1)}, u32[]{:S(2)}, u32[]{:S(2)}) collective-permute-start(f32[50,8,128]{2,1,0:T(8,128)S(1)} %get-tuple-element.41), channel_id=1, source_target_pairs={{0,8},{8,0},{16,24},{24,16},{1,9},{9,1},{17,25},{25,17},{2,10},{10... | collective-permute-start | bytes 614408 | tf_op jit(solution)/shard_map/ppermute | solution.py:590
  28.0 6.3 %collective-permute-start.3 = (f32[50,8,128]{2,1,0:T(8,128)S(1)}, f32[50,8,128]{2,1,0:T(8,128)S(1)}, u32[]{:S(2)}, u32[]{:S(2)}) collective-permute-start(f32[50,8,128]{2,1,0:T(8,128)S(1)} %get-tuple-element.42), channel_id=1, source_target_pairs={{0,24},{8,16},{16,8},{24,0},{1,25},{9,17},{17,9},{25,1},{2,26},{10... | collective-permute-start | bytes 614408 | tf_op jit(solution)/shard_map/ppermute | solution.py:591
  35.1 4.9 %collective-permute-start.4 = (f32[4,80,128]{2,1,0:T(8,128)S(1)}, f32[4,80,128]{2,1,0:T(8,128)S(1)}, u32[]{:S(2)}, u32[]{:S(2)}) collective-permute-start(f32[4,80,128]{2,1,0:T(8,128)S(1)} %get-tuple-element.45), channel_id=1, source_target_pairs={{0,1},{1,0},{2,3},{3,2},{4,5},{5,4},{6,7},{7,6},{8,9},{9,8},{10,11... | collective-permute-start | bytes 491528 | tf_op jit(solution)/shard_map/ppermute | solution.py:590
  37.6 5.0 %collective-permute-start.5 = (f32[4,80,128]{2,1,0:T(8,128)S(1)}, f32[4,80,128]{2,1,0:T(8,128)S(1)}, u32[]{:S(2)}, u32[]{:S(2)}) collective-permute-start(f32[4,80,128]{2,1,0:T(8,128)S(1)} %get-tuple-element.46), channel_id=1, source_target_pairs={{0,7},{1,2},{2,1},{3,4},{4,3},{5,6},{6,5},{7,0},{8,15},{9,10},{10,... | collective-permute-start | bytes 491528 | tf_op jit(solution)/shard_map/ppermute | solution.py:591
  38.1 1.6 %copy-start = (f32[64,8192]{1,0:T(8,128)S(1)}, f32[64,8192]{1,0:T(8,128)}, u32[]{:S(2)}) copy-start(f32[64,8192]{1,0:T(8,128)} %matrix_ref.3) | copy-start | bytes 6291460
  50.5 6.2 %collective-permute-start.6 = (f32[7,64,128]{2,1,0:T(8,128)S(1)}, f32[7,64,128]{2,1,0:T(8,128)S(1)}, u32[]{:S(2)}, u32[]{:S(2)}) collective-permute-start(f32[7,64,128]{2,1,0:T(8,128)S(1)} %get-tuple-element.49), channel_id=1, source_target_pairs={{0,32},{32,0},{64,96},{96,64},{1,33},{33,1},{65,97},{97,65},{2,34}... | collective-permute-start | bytes 688136 | tf_op jit(solution)/shard_map/ppermute | solution.py:590
  50.9 7.0 %collective-permute-start.7 = (f32[7,64,128]{2,1,0:T(8,128)S(1)}, f32[7,64,128]{2,1,0:T(8,128)S(1)}, u32[]{:S(2)}, u32[]{:S(2)}) collective-permute-start(f32[7,64,128]{2,1,0:T(8,128)S(1)} %get-tuple-element.50), channel_id=1, source_target_pairs={{0,96},{32,64},{64,32},{96,0},{1,97},{33,65},{65,33},{97,1},{2,98}... | collective-permute-start | bytes 688136 | tf_op jit(solution)/shard_map/ppermute | solution.py:591
  58.5 3.5 %collective-permute-start.8 = (f32[22,8,128]{2,1,0:T(8,128)S(1)}, f32[22,8,128]{2,1,0:T(8,128)S(1)}, u32[]{:S(2)}, u32[]{:S(2)}) collective-permute-start(f32[22,8,128]{2,1,0:T(8,128)S(1)} %get-tuple-element.51), channel_id=1, source_target_pairs={{0,8},{8,0},{16,24},{24,16},{1,9},{9,1},{17,25},{25,17},{2,10},{10... | collective-permute-start | bytes 270344 | tf_op jit(solution)/shard_map/ppermute | solution.py:590
  58.6 4.7 %collective-permute-start.9 = (f32[22,8,128]{2,1,0:T(8,128)S(1)}, f32[22,8,128]{2,1,0:T(8,128)S(1)}, u32[]{:S(2)}, u32[]{:S(2)}) collective-permute-start(f32[22,8,128]{2,1,0:T(8,128)S(1)} %get-tuple-element.52), channel_id=1, source_target_pairs={{0,24},{8,16},{16,8},{24,0},{1,25},{9,17},{17,9},{25,1},{2,26},{10... | collective-permute-start | bytes 270344 | tf_op jit(solution)/shard_map/ppermute | solution.py:591
  64.0 4.6 %collective-permute-start.10 = (f32[2,80,128]{2,1,0:T(8,128)S(1)}, f32[2,80,128]{2,1,0:T(8,128)S(1)}, u32[]{:S(2)}, u32[]{:S(2)}) collective-permute-start(f32[2,80,128]{2,1,0:T(8,128)S(1)} %get-tuple-element.55), channel_id=1, source_target_pairs={{0,1},{1,0},{2,3},{3,2},{4,5},{5,4},{6,7},{7,6},{8,9},{9,8},{10,11... | collective-permute-start | bytes 245768 | tf_op jit(solution)/shard_map/ppermute | solution.py:590
  67.7 4.2 %collective-permute-start.11 = (f32[2,80,128]{2,1,0:T(8,128)S(1)}, f32[2,80,128]{2,1,0:T(8,128)S(1)}, u32[]{:S(2)}, u32[]{:S(2)}) collective-permute-start(f32[2,80,128]{2,1,0:T(8,128)S(1)} %get-tuple-element.56), channel_id=1, source_target_pairs={{0,7},{1,2},{2,1},{3,4},{4,3},{5,6},{6,5},{7,0},{8,15},{9,10},{10,... | collective-permute-start | bytes 245768 | tf_op jit(solution)/shard_map/ppermute | solution.py:591
  67.9 27.3 %copy-start.1 = (f32[64,8192]{1,0:T(8,128)S(1)}, f32[64,8192]{1,0:T(8,128)}, u32[]{:S(2)}) copy-start(f32[64,8192]{1,0:T(8,128)} %matrix_ref.3) | copy-start | bytes 6291460

commit v4 on v3

--- a/solution.py
+++ b/solution.py
@@ -21,8 +21,6 @@
 H_R, H_G, H_V = 5, 7, 1
 N_R, N_G, N_V = CX + 2 * H_R, CX + 2 * H_G, CX + 2 * H_V
 N_ALL = N_R + N_G + N_V
-GROUPS = -(-N_ALL // 16)
-GROUPS_P = -(-PX // 16)
 NDEV = 128
 ROWS = PY // 8
 
@@ -31,6 +29,26 @@
 F_LL = np.float32(2.0) / (LIQUID + LIQUID)
 F_LG = np.float32(2.0) / (LIQUID + GAS)
 F_GG = np.float32(2.0) / (GAS + GAS)
+
+def strips(widths):
+    room, places = [], {}
+    for k, width in sorted(enumerate(widths), key=lambda item: -item[1]):
+        if width <= 0:
+            continue
+        at = next((n for n, free in enumerate(room) if free >= width), len(room))
+        if at == len(room):
+            room.append(8)
+        places[k] = (at, 8 - room[at], width)
+        room[at] -= width
+    return places, len(room)
+
+
+def reach(halo, extent):
+    return [extent - max(0, -rel, rel - CX + 1) for rel in range(-halo, CX + halo)]
+
+
+PLACES_1 = strips(reach(H_R, H_R) + reach(H_G, H_G) + reach(H_V, H_V))
+PLACES_2 = strips(reach(HX, HX))
 
 F32 = jnp.float32
 EXACT = lax.Precision.HIGHEST
@@ -226,64 +244,99 @@
     return padded_planes(refs[0], sides) if len(refs) == 3 else stacked_planes(*refs[:3], sides)
 
 
+def places_of(refs):
+    return PLACES_2[0] if len(refs) == 3 else PLACES_1[0]
+
+
+def turn(x, shift, axis):
+    shift %= x.shape[axis]
+    return pltpu.roll(x, shift, axis) if shift else x
+
+
 def y_kernel(pos, *refs):
+    refs, (a_ref, b_ref) = refs[:-2], refs[-2:]
     even = is_even(pos, 1)
-    for k, plane in enumerate(all_planes(refs[:-2], pos)):
-        put_pair(even, *refs[-2:], k, plane(pl.ds(0, HY)), plane(pl.ds(CY - HY, HY)))
-
-
-def pack_lanes(values, rows):
-    slot = iota((rows, CZ), 1) // 8
-    packed = []
-    for base in range(0, len(values), 16):
-        left = right = jnp.zeros((rows, CZ), F32)
-        for m, value in enumerate(values[base : base + 16]):
-            value = value()
-            left = jnp.where(slot == m, pltpu.roll(value, 8 * m, 1) if m else value, left)
-            shift = (8 * m + 8) % CZ
-            right = jnp.where(slot == m, pltpu.roll(value, shift, 1) if shift else value, right)
-        packed.append((left, right))
+    planes = all_planes(refs, pos)
+    row = iota((HY, CZ), 0)
+    tiles = {}
+    for k, (at, off, width) in places_of(refs).items():
+        down, up = tiles.get(at, (jnp.zeros((HY, CZ), F32),) * 2)
+        here = (row >= off) & (row < off + width)
+        down = jnp.where(here, turn(planes[k](pl.ds(0, HY)), off, 0), down)
+        up = jnp.where(here, turn(planes[k](pl.ds(CY - HY, HY)), off + width, 0), up)
+        tiles[at] = (down, up)
+    for at, (down, up) in tiles.items():
+        put_pair(even, a_ref, b_ref, at, down, up)
+
+
+def pack_lanes(value, places, rows):
+    lane = iota((rows, CZ), 1)
+    packed = {}
+    for k, (at, off, width) in places.items():
+        group, start = at // 16, at % 16 * 8 + off
+        left, right = packed.get(group, (jnp.zeros((rows, CZ), F32),) * 2)
+        here = (lane >= start) & (lane < start + width)
+        left = jnp.where(here, turn(value(k), start, 1), left)
+        right = jnp.where(here, turn(value(k), start + width, 1), right)
+        packed[group] = (left, right)
     return packed
 
 
 def z_own_kernel(pos, *refs):
-    planes = all_planes(refs[:-2], pos)
-    values = [lambda plane=plane: plane(pl.ds(0, CY)) for plane in planes]
-    for group, (left, right) in enumerate(pack_lanes(values, CY)):
-        refs[-2][group] = left
-        refs[-1][group] = right
-
-
-def z_kernel(pos, ya_ref, yb_ref, left_ref, right_ref, za_ref, zb_ref):
+    refs, (left_ref, right_ref) = refs[:-2], refs[-2:]
+    planes = all_planes(refs, pos)
+    for group, (left, right) in pack_lanes(lambda k: planes[k](pl.ds(0, CY)), places_of(refs), CY).items():
+        left_ref[group] = left
+        right_ref[group] = right
+
+
+class Rows:
+    def __init__(self, pos, places, a_ref, b_ref):
+        self.pair, self.places = Pair(pos, 1, a_ref, b_ref), places
+
+    def below(self, k):
+        if k not in self.places:
+            return jnp.zeros((HY, CZ), F32)
+        at, off, width = self.places[k]
+        return turn(self.pair.below(at), -off - width, 0)
+
+    def above(self, k):
+        if k not in self.places:
+            return jnp.zeros((HY, CZ), F32)
+        at, off, _ = self.places[k]
+        return turn(self.pair.above(at), -off, 0)
+
+
+def z_kernel(places, pos, ya_ref, yb_ref, left_ref, right_ref, za_ref, zb_ref):
     even = is_even(pos, 2)
-    sides = Pair(pos, 1, ya_ref, yb_ref)
-    count = ya_ref.shape[0]
-    below = pack_lanes([lambda k=k: sides.below(k) for k in range(count)], HY)
-    above = pack_lanes([lambda k=k: sides.above(k) for k in range(count)], HY)
-    for group in range(len(below)):
+    rows = Rows(pos, places, ya_ref, yb_ref)
+    below = pack_lanes(rows.below, places, HY)
+    above = pack_lanes(rows.above, places, HY)
+    for group in below:
         left = jnp.concatenate([below[group][0], left_ref[group], above[group][0]], axis=0)
         right = jnp.concatenate([below[group][1], right_ref[group], above[group][1]], axis=0)
         put_pair(even, za_ref, zb_ref, group, left, right)
 
 
 class Wide:
-    def __init__(self, planes, pos, ya_ref, yb_ref, za_ref, zb_ref):
-        self.planes = planes
-        self.y = Pair(pos, 1, ya_ref, yb_ref)
+    def __init__(self, planes, places, pos, ya_ref, yb_ref, za_ref, zb_ref):
+        self.planes, self.places = planes, places
+        self.rows = Rows(pos, places, ya_ref, yb_ref)
         z = Pair(pos, 2, za_ref, zb_ref)
         groups = za_ref.shape[0]
         self.behind = [z.below(g) for g in range(groups)]
         self.ahead = [z.above(g) for g in range(groups)]
 
     def __call__(self, k):
-        group, m = k // 16, k % 16
         lane = iota((PY, CZ), 1)
-        shift = (CZ - 8 * m) % CZ
-        ahead = pltpu.roll(self.ahead[group], shift, 1) if shift else self.ahead[group]
-        shift = (CZ - 8 - 8 * m) % CZ
-        behind = pltpu.roll(self.behind[group], shift, 1) if shift else self.behind[group]
-        side = jnp.where(lane < 8, ahead, jnp.where(lane >= CZ - 8, behind, 0.0))
-        middle = jnp.concatenate([self.y.below(k), self.planes[k](pl.ds(0, CY)), self.y.above(k)], axis=0)
+        side = jnp.zeros((PY, CZ), F32)
+        if k in self.places:
+            at, off, width = self.places[k]
+            group, start = at // 16, at % 16 * 8 + off
+            ahead = turn(self.ahead[group], -start, 1)
+            behind = turn(self.behind[group], -start - width, 1)
+            side = jnp.where(lane < 8, ahead, jnp.where(lane >= CZ - 8, behind, 0.0))
+        middle = jnp.concatenate([self.rows.below(k), self.planes[k](pl.ds(0, CY)), self.rows.above(k)], axis=0)
         return jnp.concatenate([middle, side], axis=1)
 
 
@@ -315,10 +368,11 @@
     p_ref, xa_out, xb_out, vx_ref, w_ref, diag_ref,
     g_ref, wide_ref, rp_ref, a_ref, b_ref, nat_ref,
 ):
-    wide = Wide(stacked_planes(r_ref, g_in, v_in, Pair(pos, 0, xa_ref, xb_ref)), pos, ya_ref, yb_ref, za_ref, zb_ref)
+    planes = stacked_planes(r_ref, g_in, v_in, Pair(pos, 0, xa_ref, xb_ref))
+    wide = Wide(planes, PLACES_1[0], pos, ya_ref, yb_ref, za_ref, zb_ref)
     mask = inside_yz(pos)
     for i in range(PX):
-        put(g_ref, i, wide(N_R + i) * (mask * inside_x(pos, i - HX)))
+        put(g_ref, i, jnp.where(wide(N_R + i) > 0.5, mask * inside_x(pos, i - HX), 0.0))
     for i in range(N_V):
         put(vx_ref, i, wide(N_R + N_G + i) * (mask * inside_x(pos, i - H_V)))
     for k in range(N_R):
@@ -414,7 +468,8 @@
     q_ref, c_ref, y_ref, send_ref,
     full_ref, plane_ref, rp_ref, a_ref, b_ref,
 ):
-    wide = Wide(padded_planes(p_ref, Pair(pos, 0, xa_ref, xb_ref)), pos, ya_ref, yb_ref, za_ref, zb_ref)
+    planes = padded_planes(p_ref, Pair(pos, 0, xa_ref, xb_ref))
+    wide = Wide(planes, PLACES_2[0], pos, ya_ref, yb_ref, za_ref, zb_ref)
     mask = inside_yz(pos)
     for i in range(PX):
         put(full_ref, i, wide(i) * (mask * inside_x(pos, i - HX)))
@@ -596,12 +651,14 @@
     return lax.all_to_all(rows, AXES, 0, 0, tiled=True)
 
 
-def exchange_yz(pos, own, count):
+def exchange_yz(pos, own):
+    places, count = PLACES_2 if len(own) == 3 else PLACES_1
     groups = -(-count // 16)
     ya, yb = call(y_kernel, [(count, HY, CZ)] * 2, smem=True)(pos, *own)
     ya, yb = swap(ya, yb, "gy")
     left, right = call(z_own_kernel, [(groups, CY, CZ)] * 2, smem=True, cost=cost(1))(pos, *own)
-    za, zb = call(z_kernel, [(groups, PY, CZ)] * 2, smem=True)(pos, ya, yb, left, right)
+    pack = functools.partial(z_kernel, places)
+    za, zb = call(pack, [(groups, PY, CZ)] * 2, smem=True)(pos, ya, yb, left, right)
     return (ya, yb, *swap(za, zb, "gz"))
 
 
@@ -622,7 +679,7 @@
     sums = gather(send)
     xa, xb, sums = lax.optimization_barrier((xa, xb, sums))
     own = (r, g, v, xa, xb)
-    halos = exchange_yz(pos, own, N_ALL)
+    halos = exchange_yz(pos, own)
     amounts = call(first_amounts_kernel, (1, 128), cost=cost(1))(sums, coarse_inverse)
     p, xa, xb, v_wide, w, diag = call(
         smooth_kernel,
@@ -632,7 +689,7 @@
     )(pos, *own, *halos, amounts)
     own = (p, *swap(xa, xb, "gx"))
     quads = call(product_kernel, (4, 128), scratch=[(16, PY, CZ)], cost=cost(1))(v_wide, w, diag)
-    halos = exchange_yz(pos, own, PX)
+    halos = exchange_yz(pos, own)
     q, c, y, send = call(
         image_kernel,
         [block, block, block, (NDEV, 384)],

time: 112 us -> 108 us (0.964)
  starting transfers between devices: 15.7 us -> 14 us
  waiting for transfers between devices: 17.7 us -> 16 us
    ppermute x6, starting transfers between devices: 6.46 us -> 4.58 us  [swap(): lax.ppermute(b, axis, [(i, (i - 1 if i % 2 == 0 else i + 1) % count) for...]
where the time goes in v4:
time: 108 us
  blocking collectives  46.9 us (43%)
  Pallas kernels  25.7 us (24%)
  waiting for transfers between devices  16 us (15%)
  starting transfers between devices  14 us (13%)
  local copies, waits for them, and re-layouts  4.66 us (4%)
    all_to_all x3, blocking collectives, gather(): return lax.all_to_all(rows, AXES, 0, 0, tiled=True)  46.9 us
    pallas_call x13, Pallas kernels, run(): pl.pallas_call(kernel, out_shape=[jax.ShapeDtypeStruct(s, F32) for s in o...  25.7 us
    ppermute x6, starting transfers between devices, swap(): got_a = lax.ppermute(a, axis, [(i, i ^ 1) for i in range(count)])  9.46 us
    ppermute x6, waiting for transfers between devices, swap(): lax.ppermute(b, axis, [(i, (i - 1 if i % 2 == 0 else i + 1) % count) for...  8.94 us
    ppermute x6, waiting for transfers between devices, swap(): got_a = lax.ppermute(a, axis, [(i, i ^ 1) for i in range(count)])  7.05 us
    ppermute x6, starting transfers between devices, swap(): lax.ppermute(b, axis, [(i, (i - 1 if i % 2 == 0 else i + 1) % count) for...  4.58 us
    unnamed x11, local copies, waits for them, and re-layouts  4.46 us
  transfers between devices with their start and end apart: 12, of which 9 were waited for; matrix products, arithmetic and copies ran while one was open for 0% of the time, Pallas kernels for 3%

profile of v4, /device:TPU:1, one launch (start us, length us, event | category | flops | bytes accessed | tf_op | source)
XLA Modules:
  0.0 108.1 jit_solution(4823409669493330707)
XLA Ops:
  0.6 0.1 pad_add_fusion.pos
  0.7 0.0 copy-start.2
  0.7 0.9 copy-done.2
  1.7 0.9 copy-done.3
  2.6 0.9 copy-done.4
  3.6 0.9 shard_map.59
  4.5 2.1 %collective-permute-start = (f32[13,64,128]{2,1,0:T(8,128)S(1)}, f32[13,64,128]{2,1,0:T(8,128)S(1)}, u32[]{:S(2)}, u32[]{:S(2)}) collective-permute-start(f32[13,64,128]{2,1,0:T(8,128)S(1)} %get-tuple-element.36), channel_id=1, source_target_pairs={{0,32},{32,0},{64,96},{96,64},{1,33},{33,1},{65,97},{97,65},{2,34}... | collective-permute-start | bytes 1277960 | tf_op jit(solution)/shard_map/ppermute | solution.py:645
  6.6 1.8 %collective-permute-start.1 = (f32[13,64,128]{2,1,0:T(8,128)S(1)}, f32[13,64,128]{2,1,0:T(8,128)S(1)}, u32[]{:S(2)}, u32[]{:S(2)}) collective-permute-start(f32[13,64,128]{2,1,0:T(8,128)S(1)} %get-tuple-element.37), channel_id=1, source_target_pairs={{0,96},{32,64},{64,32},{96,0},{1,97},{33,65},{65,33},{97,1},{2,98}... | collective-permute-start | bytes 1277960 | tf_op jit(solution)/shard_map/ppermute | solution.py:646
  8.4 18.5 %all_to_all.34 = f32[128,1,128]{2,1,0:T(1,128)S(1)} all-to-all(f32[128,1,128]{2,1,0:T(1,128)S(1)} %bitcast.21), channel_id=1, replica_groups=mesh['gx'=4,'gy'=4,'gz'=8] {'gx','gy','gz'}, dimensions={0} | all-to-all | bytes 131072 | tf_op jit(solution)/shard_map/all_to_all | solution.py:651
  26.9 0.0 collective-permute-done.refs_3_.xa_ref
  26.9 0.0 collective-permute-done.1.refs_4_.xb_ref
  27.0 0.6 shard_map.60
  27.5 0.4 collective-permute-start.2
  28.0 1.3 %collective-permute-start.3 = (f32[22,8,128]{2,1,0:T(8,128)S(1)}, f32[22,8,128]{2,1,0:T(8,128)S(1)}, u32[]{:S(2)}, u32[]{:S(2)}) collective-permute-start(f32[22,8,128]{2,1,0:T(8,128)S(1)} %get-tuple-element.42), channel_id=1, source_target_pairs={{0,24},{8,16},{16,8},{24,0},{1,25},{9,17},{17,9},{25,1},{2,26},{10... | collective-permute-start | bytes 270344 | tf_op jit(solution)/shard_map/ppermute | solution.py:646
  29.3 1.3 %shard_map.61 = (f32[2,64,128]{2,1,0:T(8,128)S(1)}, f32[2,64,128]{2,1,0:T(8,128)S(1)}) custom-call(s32[3]{0:T(128)S(1)} %pad_add_fusion.pos, f32[8,64,128]{2,1,0:T(8,128)S(1)} %get-tuple-element.33.refs_0_.r_ref, f32[8,64,128]{2,1,0:T(8,128)S(1)} %get-tuple-element.34.refs_1_.g_in, f32[8,64,128]{2,1,0:T(8,128)S(1)} %get-tuple-element.35.refs_2_.v_in.v_ref, ...), custom_call_target="tpu_custom_call" | custom-call | flops 1000000 | bytes 3000000 | tf_op jit(solution)/shard_map/pallas_call | solution.py:626
  30.6 0.4 collective-permute-done.2.ya_ref
  31.0 1.6 %collective-permute-done.3.yb_ref = f32[22,8,128]{2,1,0:T(8,128)S(1)} collective-permute-done((f32[22,8,128]{2,1,0:T(8,128)S(1)}, f32[22,8,128]{2,1,0:T(8,128)S(1)}, u32[]{:S(2)}, u32[]{:S(2)}) %collective-permute-start.3) | collective-permute-done | bytes 90144 | tf_op jit(solution)/shard_map/ppermute | solution.py:646
  32.6 0.8 shard_map.62
  33.4 2.7 %collective-permute-start.4 = (f32[2,80,128]{2,1,0:T(8,128)S(1)}, f32[2,80,128]{2,1,0:T(8,128)S(1)}, u32[]{:S(2)}, u32[]{:S(2)}) collective-permute-start(f32[2,80,128]{2,1,0:T(8,128)S(1)} %get-tuple-element.45), channel_id=1, source_target_pairs={{0,1},{1,0},{2,3},{3,2},{4,5},{5,4},{6,7},{7,6},{8,9},{9,8},{10,11... | collective-permute-start | bytes 245768 | tf_op jit(solution)/shard_map/ppermute | solution.py:645
  36.1 0.0 collective-permute-start.5
  36.1 1.6 %copy-done = f32[64,8192]{1,0:T(8,128)S(1)} copy-done((f32[64,8192]{1,0:T(8,128)S(1)}, f32[64,8192]{1,0:T(8,128)}, u32[]{:S(2)}) %copy-start) | copy-done | bytes 2097176
  37.7 0.3 shard_map.63.amounts_ref
  38.0 0.0 collective-permute-done.4.za_ref
  38.0 2.3 %collective-permute-done.5.zb_ref = f32[2,80,128]{2,1,0:T(8,128)S(1)} collective-permute-done((f32[2,80,128]{2,1,0:T(8,128)S(1)}, f32[2,80,128]{2,1,0:T(8,128)S(1)}, u32[]{:S(2)}, u32[]{:S(2)}) %collective-permute-start.5) | collective-permute-done | bytes 81952 | tf_op jit(solution)/shard_map/ppermute | solution.py:646
  40.2 7.8 %shard_map.64 = (f32[8,64,128]{2,1,0:T(8,128)S(1)}, f32[7,64,128]{2,1,0:T(8,128)S(1)}, f32[7,64,128]{2,1,0:T(8,128)S(1)}, f32[2,10,80,128]{3,2,1,0:T(8,128)S(1)}...) custom-call(s32[3]{0:T(128)S(1)} %pad_add_fusion.pos, ...), custom_call_target="tpu_custom_call" | custom-call | tf_op jit(solution)/shard_map/pallas_call | solution.py:626
  48.1 0.4 collective-permute-start.6
  48.4 0.7 collective-permute-start.7
  49.1 5.1 %collective-permute-done.6.refs_1_.xa_ref = f32[7,64,128]{2,1,0:T(8,128)S(1)} collective-permute-done((f32[7,64,128]{2,1,0:T(8,128)S(1)}, f32[7,64,128]{2,1,0:T(8,128)S(1)}, u32[]{:S(2)}, u32[]{:S(2)}) %collective-permute-start.6) | collective-permute-done | bytes 229408 | tf_op jit(solution)/shard_map/ppermute | solution.py:645
  54.2 1.2 %collective-permute-done.7.refs_2_.xb_ref = f32[7,64,128]{2,1,0:T(8,128)S(1)} collective-permute-done((f32[7,64,128]{2,1,0:T(8,128)S(1)}, f32[7,64,128]{2,1,0:T(8,128)S(1)}, u32[]{:S(2)}, u32[]{:S(2)}) %collective-permute-start.7) | collective-permute-done | bytes 229408 | tf_op jit(solution)/shard_map/ppermute | solution.py:646
  55.5 0.6 shard_map.65
  56.0 0.1 collective-permute-start.8
  56.1 0.8 collective-permute-start.9
  56.9 0.9 shard_map.66
  57.9 1.2 %collective-permute-done.8.ya_ref = f32[13,8,128]{2,1,0:T(8,128)S(1)} collective-permute-done((f32[13,8,128]{2,1,0:T(8,128)S(1)}, f32[13,8,128]{2,1,0:T(8,128)S(1)}, u32[]{:S(2)}, u32[]{:S(2)}) %collective-permute-start.8) | collective-permute-done | bytes 53280 | tf_op jit(solution)/shard_map/ppermute | solution.py:645
  59.1 1.3 %collective-permute-done.9.yb_ref = f32[13,8,128]{2,1,0:T(8,128)S(1)} collective-permute-done((f32[13,8,128]{2,1,0:T(8,128)S(1)}, f32[13,8,128]{2,1,0:T(8,128)S(1)}, u32[]{:S(2)}, u32[]{:S(2)}) %collective-permute-start.9) | collective-permute-done | bytes 53280 | tf_op jit(solution)/shard_map/ppermute | solution.py:646
  60.4 0.7 shard_map.67
  61.1 3.7 %collective-permute-start.10 = (f32[1,80,128]{2,1,0:T(8,128)S(1)}, f32[1,80,128]{2,1,0:T(8,128)S(1)}, u32[]{:S(2)}, u32[]{:S(2)}) collective-permute-start(f32[1,80,128]{2,1,0:T(8,128)S(1)} %get-tuple-element.55), channel_id=1, source_target_pairs={{0,1},{1,0},{2,3},{3,2},{4,5},{5,4},{6,7},{7,6},{8,9},{9,8},{10,11... | collective-permute-start | bytes 122888 | tf_op jit(solution)/shard_map/ppermute | solution.py:645
  64.8 0.0 collective-permute-start.11
  64.8 0.6 shard_map.68.e_ref
  65.4 0.3 collective-permute-done.10.za_ref
  65.7 2.6 %collective-permute-done.11.zb_ref = f32[1,80,128]{2,1,0:T(8,128)S(1)} collective-permute-done((f32[1,80,128]{2,1,0:T(8,128)S(1)}, f32[1,80,128]{2,1,0:T(8,128)S(1)}, u32[]{:S(2)}, u32[]{:S(2)}) %collective-permute-start.11) | collective-permute-done | bytes 40992 | tf_op jit(solution)/shard_map/ppermute | solution.py:646
  68.2 8.3 %shard_map.69 = (f32[8,64,128]{2,1,0:T(8,128)S(1)}, f32[8,64,128]{2,1,0:T(8,128)S(1)}, f32[8,64,128]{2,1,0:T(8,128)S(1)}, f32[128,384]{1,0:T(8,128)S(1)}) custom-call(s32[3]{0:T(128)S(1)} %pad_add_fusion.pos, f32[8,64,128]{2,1,0:T(8,128)S(1)} %get-tuple-element.48.refs_0_.p_ref, f32[7,64,128]{2,1,0:T(8,128)S(1)} %collective-permute-done.6.refs_1_.xa_ref, ...), custom_call_target="tpu_custom_call" | custom-call | tf_op jit(solution)/shard_map/pallas_call | solution.py:626
  76.5 0.2 copy.7
  76.7 14.8 %all_to_all.35 = f32[128,1,384]{2,1,0:T(1,128)S(1)} all-to-all(f32[128,1,384]{2,1,0:T(1,128)S(1)} %copy.7), channel_id=1, replica_groups=mesh['gx'=4,'gy'=4,'gz'=8] {'gx','gy','gz'}, dimensions={0} | all-to-all | bytes 393216 | tf_op jit(solution)/shard_map/all_to_all | solution.py:651
  91.5 0.0 copy-done.1
  91.5 0.7 shard_map.70
  92.2 13.6 %all_to_all.36 = f32[128,1,128]{2,1,0:T(1,128)S(1)} all-to-all(f32[128,1,128]{2,1,0:T(1,128)S(1)} %bitcast.18), channel_id=1, replica_groups=mesh['gx'=4,'gy'=4,'gz'=8] {'gx','gy','gz'}, dimensions={0} | all-to-all | bytes 131072 | tf_op jit(solution)/shard_map/all_to_all | solution.py:651
  105.9 2.2 %shard_map.71 = (f32[8,64,128]{2,1,0:T(8,128)}, f32[8,64,128]{2,1,0:T(8,128)}) custom-call(s32[3]{0:T(128)S(1)} %pad_add_fusion.pos, f32[128,384]{1,0:T(8,128)S(1)} %bitcast.16, f32[128,128]{1,0:T(8,128)S(1)} %bitcast.17, f32[8,64,128]{2,1,0:T(8,128)S(1)} %get-tuple-element.48.refs_0_.p_ref, f32[8,64,128]{2,1,0:T(8,128)S(1)} %get-tuple-element.61.q_ref, ...), custom_call_target="tpu_custom_call" | custom-call | tf_op jit(solution)/shard_map/pallas_call | solution.py:626
  (5 shorter events, 0.0 us)
Async XLA Ops:
  0.7 1.0 copy-start.2
  1.7 0.9 copy-start.3
  2.6 0.9 copy-start.4
  4.5 22.4 %collective-permute-start = (f32[13,64,128]{2,1,0:T(8,128)S(1)}, f32[13,64,128]{2,1,0:T(8,128)S(1)}, u32[]{:S(2)}, u32[]{:S(2)}) collective-permute-start(f32[13,64,128]{2,1,0:T(8,128)S(1)} %get-tuple-element.36), channel_id=1, source_target_pairs={{0,32},{32,0},{64,96},{96,64},{1,33},{33,1},{65,97},{97,65},{2,34}... | collective-permute-start | bytes 1277960 | tf_op jit(solution)/shard_map/ppermute | solution.py:645
  6.6 20.3 %collective-permute-start.1 = (f32[13,64,128]{2,1,0:T(8,128)S(1)}, f32[13,64,128]{2,1,0:T(8,128)S(1)}, u32[]{:S(2)}, u32[]{:S(2)}) collective-permute-start(f32[13,64,128]{2,1,0:T(8,128)S(1)} %get-tuple-element.37), channel_id=1, source_target_pairs={{0,96},{32,64},{64,32},{96,0},{1,97},{33,65},{65,33},{97,1},{2,98}... | collective-permute-start | bytes 1277960 | tf_op jit(solution)/shard_map/ppermute | solution.py:646
  27.5 3.5 %collective-permute-start.2 = (f32[22,8,128]{2,1,0:T(8,128)S(1)}, f32[22,8,128]{2,1,0:T(8,128)S(1)}, u32[]{:S(2)}, u32[]{:S(2)}) collective-permute-start(f32[22,8,128]{2,1,0:T(8,128)S(1)} %get-tuple-element.41), channel_id=1, source_target_pairs={{0,8},{8,0},{16,24},{24,16},{1,9},{9,1},{17,25},{25,17},{2,10},{10... | collective-permute-start | bytes 270344 | tf_op jit(solution)/shard_map/ppermute | solution.py:645
  28.0 4.6 %collective-permute-start.3 = (f32[22,8,128]{2,1,0:T(8,128)S(1)}, f32[22,8,128]{2,1,0:T(8,128)S(1)}, u32[]{:S(2)}, u32[]{:S(2)}) collective-permute-start(f32[22,8,128]{2,1,0:T(8,128)S(1)} %get-tuple-element.42), channel_id=1, source_target_pairs={{0,24},{8,16},{16,8},{24,0},{1,25},{9,17},{17,9},{25,1},{2,26},{10... | collective-permute-start | bytes 270344 | tf_op jit(solution)/shard_map/ppermute | solution.py:646
  33.4 4.6 %collective-permute-start.4 = (f32[2,80,128]{2,1,0:T(8,128)S(1)}, f32[2,80,128]{2,1,0:T(8,128)S(1)}, u32[]{:S(2)}, u32[]{:S(2)}) collective-permute-start(f32[2,80,128]{2,1,0:T(8,128)S(1)} %get-tuple-element.45), channel_id=1, source_target_pairs={{0,1},{1,0},{2,3},{3,2},{4,5},{5,4},{6,7},{7,6},{8,9},{9,8},{10,11... | collective-permute-start | bytes 245768 | tf_op jit(solution)/shard_map/ppermute | solution.py:645
  36.1 4.2 %collective-permute-start.5 = (f32[2,80,128]{2,1,0:T(8,128)S(1)}, f32[2,80,128]{2,1,0:T(8,128)S(1)}, u32[]{:S(2)}, u32[]{:S(2)}) collective-permute-start(f32[2,80,128]{2,1,0:T(8,128)S(1)} %get-tuple-element.46), channel_id=1, source_target_pairs={{0,7},{1,2},{2,1},{3,4},{4,3},{5,6},{6,5},{7,0},{8,15},{9,10},{10,... | collective-permute-start | bytes 245768 | tf_op jit(solution)/shard_map/ppermute | solution.py:646
  36.1 1.6 %copy-start = (f32[64,8192]{1,0:T(8,128)S(1)}, f32[64,8192]{1,0:T(8,128)}, u32[]{:S(2)}) copy-start(f32[64,8192]{1,0:T(8,128)} %matrix_ref.3) | copy-start | bytes 6291460
  48.1 6.2 %collective-permute-start.6 = (f32[7,64,128]{2,1,0:T(8,128)S(1)}, f32[7,64,128]{2,1,0:T(8,128)S(1)}, u32[]{:S(2)}, u32[]{:S(2)}) collective-permute-start(f32[7,64,128]{2,1,0:T(8,128)S(1)} %get-tuple-element.49), channel_id=1, source_target_pairs={{0,32},{32,0},{64,96},{96,64},{1,33},{33,1},{65,97},{97,65},{2,34}... | collective-permute-start | bytes 688136 | tf_op jit(solution)/shard_map/ppermute | solution.py:645
  48.4 7.0 %collective-permute-start.7 = (f32[7,64,128]{2,1,0:T(8,128)S(1)}, f32[7,64,128]{2,1,0:T(8,128)S(1)}, u32[]{:S(2)}, u32[]{:S(2)}) collective-permute-start(f32[7,64,128]{2,1,0:T(8,128)S(1)} %get-tuple-element.50), channel_id=1, source_target_pairs={{0,96},{32,64},{64,32},{96,0},{1,97},{33,65},{65,33},{97,1},{2,98}... | collective-permute-start | bytes 688136 | tf_op jit(solution)/shard_map/ppermute | solution.py:646
  56.0 3.1 %collective-permute-start.8 = (f32[13,8,128]{2,1,0:T(8,128)S(1)}, f32[13,8,128]{2,1,0:T(8,128)S(1)}, u32[]{:S(2)}, u32[]{:S(2)}) collective-permute-start(f32[13,8,128]{2,1,0:T(8,128)S(1)} %get-tuple-element.51), channel_id=1, source_target_pairs={{0,8},{8,0},{16,24},{24,16},{1,9},{9,1},{17,25},{25,17},{2,10},{10... | collective-permute-start | bytes 159752 | tf_op jit(solution)/shard_map/ppermute | solution.py:645
  56.1 4.3 %collective-permute-start.9 = (f32[13,8,128]{2,1,0:T(8,128)S(1)}, f32[13,8,128]{2,1,0:T(8,128)S(1)}, u32[]{:S(2)}, u32[]{:S(2)}) collective-permute-start(f32[13,8,128]{2,1,0:T(8,128)S(1)} %get-tuple-element.52), channel_id=1, source_target_pairs={{0,24},{8,16},{16,8},{24,0},{1,25},{9,17},{17,9},{25,1},{2,26},{10... | collective-permute-start | bytes 159752 | tf_op jit(solution)/shard_map/ppermute | solution.py:646
  61.1 4.6 %collective-permute-start.10 = (f32[1,80,128]{2,1,0:T(8,128)S(1)}, f32[1,80,128]{2,1,0:T(8,128)S(1)}, u32[]{:S(2)}, u32[]{:S(2)}) collective-permute-start(f32[1,80,128]{2,1,0:T(8,128)S(1)} %get-tuple-element.55), channel_id=1, source_target_pairs={{0,1},{1,0},{2,3},{3,2},{4,5},{5,4},{6,7},{7,6},{8,9},{9,8},{10,11... | collective-permute-start | bytes 122888 | tf_op jit(solution)/shard_map/ppermute | solution.py:645
  64.8 3.4 %collective-permute-start.11 = (f32[1,80,128]{2,1,0:T(8,128)S(1)}, f32[1,80,128]{2,1,0:T(8,128)S(1)}, u32[]{:S(2)}, u32[]{:S(2)}) collective-permute-start(f32[1,80,128]{2,1,0:T(8,128)S(1)} %get-tuple-element.56), channel_id=1, source_target_pairs={{0,7},{1,2},{2,1},{3,4},{4,3},{5,6},{6,5},{7,0},{8,15},{9,10},{10,... | collective-permute-start | bytes 122888 | tf_op jit(solution)/shard_map/ppermute | solution.py:646
  64.8 26.7 %copy-start.1 = (f32[64,8192]{1,0:T(8,128)S(1)}, f32[64,8192]{1,0:T(8,128)}, u32[]{:S(2)}) copy-start(f32[64,8192]{1,0:T(8,128)} %matrix_ref.3) | copy-start | bytes 6291460

commit v5 on v4

--- a/solution.py
+++ b/solution.py
@@ -175,19 +175,15 @@
     return jnp.sum(jnp.sum(x, axis=0, keepdims=True), axis=1, keepdims=True)
 
 
-def start_kernel(pos, r_in, phase_in, v_in, xa_ref, xb_ref, send_ref, r_ref, g_ref, v_ref, phase_ref, sem):
-    pairs = ((r_in, r_ref), (v_in, v_ref), (phase_in, phase_ref))
-    copies = [pltpu.make_async_copy(src, dst, sem.at[n]) for n, (src, dst) in enumerate(pairs)]
-    for copy in copies:
-        copy.start()
-    for copy in copies:
-        copy.wait()
+def start_kernel(pos, all_ref, xa_ref, xb_ref, send_ref, r_ref, g_ref, v_ref):
+    r_ref[...] = all_ref[0:CX]
+    g_ref[...] = all_ref[CX : 2 * CX]
+    v_ref[...] = all_ref[2 * CX :]
     parts = []
     for sx in range(4):
         parts.append(r_ref[2 * sx] * v_ref[2 * sx] + r_ref[2 * sx + 1] * v_ref[2 * sx + 1])
     (row,) = row_sums([parts])
     send_ref[...] = jnp.broadcast_to(row, (NDEV, 128))
-    g_ref[...] = jnp.where(phase_ref[...] == 1, 1.0, 0.0).astype(F32)
     even = is_even(pos, 0)
     for base, ref, halo in ((0, r_ref, H_R), (H_R, g_ref, H_G), (H_R + H_G, v_ref, H_V)):
         for k in range(halo):
@@ -344,6 +340,13 @@
     out_ref[...] = coarse_rows(matrix_ref, sums_ref[pl.ds(0, 64, stride=2), :], sums_ref[pl.ds(1, 64, stride=2), :])
 
 
+def store(ref, i, j, value, halo):
+    if max(HX - i, i - HX - CX + 1) >= halo:
+        ref[i, j, :, 0:CZ] = value[:, 0:CZ]
+    else:
+        ref[i, j] = value
+
+
 def chebyshev(halo, w_ref, rp_ref, a_ref, b_ref):
     _, weights = recurrence()
     now, before = a_ref, b_ref
@@ -358,7 +361,7 @@
                 new = (1.0 + keep - push) * now[i, j] + push * total
                 if index:
                     new = new - keep * before[i, j]
-                before[i, j] = new
+                store(before, i, j, new, halo)
         now, before = before, now
     return now
 
@@ -393,8 +396,8 @@
                 w_ref[d, i, j] = first + second * labels[d]
             if HX - H_R <= i < HX + CX + H_R:
                 scaled = strided(wide_ref, i - HX + H_R, j) * inverse
-                rp_ref[i, j] = scaled
-                a_ref[i, j] = scaled * first_scale
+                store(rp_ref, i, j, scaled, H_R)
+                store(a_ref, i, j, scaled * first_scale, H_R)
     result = chebyshev(H_R, w_ref, rp_ref, a_ref, b_ref)
     for j in range(ROWS):
         for x in range(CX):
@@ -482,8 +485,8 @@
             total = w_ref[0, i, j] * (mine - values[0])
             for d in range(1, 6):
                 total = total + w_ref[d, i, j] * (mine - values[d])
-            rp_ref[i, j] = total
-            a_ref[i, j] = total * first_scale
+            store(rp_ref, i, j, total, HX - 1)
+            store(a_ref, i, j, total * first_scale, HX - 1)
             if HX <= i < HX + CX:
                 plane_ref[i - HX, rows, :] = total[:, 0:CZ] * diag_ref[i - HX, j]
     result = chebyshev(HX - 1, w_ref, rp_ref, a_ref, b_ref)
@@ -668,13 +671,12 @@
     tall = (2, PX, PY, CZ)
     split = (PX, ROWS, 8, PZ)
     n_x = H_R + H_G + H_V
+    labels = jnp.where(phase == 1, 1.0, 0.0).astype(F32)
     xa, xb, send, r, g, v = call(
         start_kernel,
         [(n_x, CY, CZ), (n_x, CY, CZ), (NDEV, 128), block, block, block],
-        scratch=[pltpu.VMEM(block, jnp.int32), pltpu.SemaphoreType.DMA((3,))],
         smem=True,
-        hbm=3,
-    )(pos, right_side, phase, deflation_weights)
+    )(pos, jnp.concatenate([right_side, labels, deflation_weights], axis=0))
     xa, xb = swap(xa, xb, "gx")
     sums = gather(send)
     xa, xb, sums = lax.optimization_barrier((xa, xb, sums))

time: 108 us -> 107 us (level)
  local copies, waits for them, and re-layouts: 4.66 us -> 1.81 us
  other arithmetic: 0.08 us -> 2.15 us
    unnamed x11 -> x5, local copies, waits for them, and re-layouts: 4.46 us -> 1.61 us
    concatenate x0 -> x1, other arithmetic: none -> 1.1 us  [local(): jnp.concatenate([right_side, labels, deflation_weights], axis=0)]
where the time goes in v5:
time: 107 us
  blocking collectives  46.9 us (44%)
  Pallas kernels  25.5 us (24%)
  waiting for transfers between devices  16 us (15%)
  starting transfers between devices  14 us (13%)
  other arithmetic  2.15 us (2%)
  local copies, waits for them, and re-layouts  1.81 us (2%)
    all_to_all x3, blocking collectives, gather(): return lax.all_to_all(rows, AXES, 0, 0, tiled=True)  46.9 us
    pallas_call x13, Pallas kernels, run(): pl.pallas_call(kernel, out_shape=[jax.ShapeDtypeStruct(s, F32) for s in o...  25.5 us
    ppermute x6, starting transfers between devices, swap(): got_a = lax.ppermute(a, axis, [(i, i ^ 1) for i in range(count)])  9.46 us
    ppermute x6, waiting for transfers between devices, swap(): lax.ppermute(b, axis, [(i, (i - 1 if i % 2 == 0 else i + 1) % count) for...  8.94 us
    ppermute x6, waiting for transfers between devices, swap(): got_a = lax.ppermute(a, axis, [(i, i ^ 1) for i in range(count)])  7.05 us
    ppermute x6, starting transfers between devices, swap(): lax.ppermute(b, axis, [(i, (i - 1 if i % 2 == 0 else i + 1) % count) for...  4.58 us
  transfers between devices with their start and end apart: 12, of which 9 were waited for; matrix products, arithmetic and copies ran while one was open for 0% of the time, Pallas kernels for 3%

profile of v5, /device:TPU:1, one launch (start us, length us, event | category | flops | bytes accessed | tf_op | source)
XLA Modules:
  0.0 107.1 jit_solution(14700389223053144849)
XLA Ops:
  0.6 1.0 compare_select_fusion
  1.6 0.1 pad_add_fusion.pos
  1.7 1.1 %pad_maximum_fusion.all_ref = f32[24,64,128]{2,1,0:T(8,128)S(1)} fusion(f32[8,64,128]{2,1,0:T(8,128)} %param.6, f32[8,64,128]{2,1,0:T(8,128)S(1)} %compare_select_fusion, f32[8,64,128]{2,1,0:T(8,128)} %param.4), kind=kLoop, calls=%fused_computation | loop fusion | flops 393216 | bytes 1572864 | tf_op jit(solution)/shard_map/concatenate | solution.py:679
  2.8 0.8 shard_map.59
  3.6 2.1 %collective-permute-start = (f32[13,64,128]{2,1,0:T(8,128)S(1)}, f32[13,64,128]{2,1,0:T(8,128)S(1)}, u32[]{:S(2)}, u32[]{:S(2)}) collective-permute-start(f32[13,64,128]{2,1,0:T(8,128)S(1)} %get-tuple-element.36), channel_id=1, source_target_pairs={{0,32},{32,0},{64,96},{96,64},{1,33},{33,1},{65,97},{97,65},{2,34}... | collective-permute-start | bytes 1277960 | tf_op jit(solution)/shard_map/ppermute | solution.py:648
  5.7 1.8 %collective-permute-start.1 = (f32[13,64,128]{2,1,0:T(8,128)S(1)}, f32[13,64,128]{2,1,0:T(8,128)S(1)}, u32[]{:S(2)}, u32[]{:S(2)}) collective-permute-start(f32[13,64,128]{2,1,0:T(8,128)S(1)} %get-tuple-element.37), channel_id=1, source_target_pairs={{0,96},{32,64},{64,32},{96,0},{1,97},{33,65},{65,33},{97,1},{2,98}... | collective-permute-start | bytes 1277960 | tf_op jit(solution)/shard_map/ppermute | solution.py:649
  7.5 18.5 %all_to_all.34 = f32[128,1,128]{2,1,0:T(1,128)S(1)} all-to-all(f32[128,1,128]{2,1,0:T(1,128)S(1)} %bitcast.21), channel_id=1, replica_groups=mesh['gx'=4,'gy'=4,'gz'=8] {'gx','gy','gz'}, dimensions={0} | all-to-all | bytes 131072 | tf_op jit(solution)/shard_map/all_to_all | solution.py:654
  26.0 0.0 collective-permute-done.refs_3_.xa_ref
  26.0 0.0 collective-permute-done.1.refs_4_.xb_ref
  26.0 0.6 shard_map.60
  26.6 0.4 collective-permute-start.2
  27.1 1.3 %collective-permute-start.3 = (f32[22,8,128]{2,1,0:T(8,128)S(1)}, f32[22,8,128]{2,1,0:T(8,128)S(1)}, u32[]{:S(2)}, u32[]{:S(2)}) collective-permute-start(f32[22,8,128]{2,1,0:T(8,128)S(1)} %get-tuple-element.42), channel_id=1, source_target_pairs={{0,24},{8,16},{16,8},{24,0},{1,25},{9,17},{17,9},{25,1},{2,26},{10... | collective-permute-start | bytes 270344 | tf_op jit(solution)/shard_map/ppermute | solution.py:649
  28.4 1.3 %shard_map.61 = (f32[2,64,128]{2,1,0:T(8,128)S(1)}, f32[2,64,128]{2,1,0:T(8,128)S(1)}) custom-call(s32[3]{0:T(128)S(1)} %pad_add_fusion.pos, f32[8,64,128]{2,1,0:T(8,128)S(1)} %get-tuple-element.33.refs_0_.r_ref, f32[8,64,128]{2,1,0:T(8,128)S(1)} %get-tuple-element.34.refs_1_.g_in, f32[8,64,128]{2,1,0:T(8,128)S(1)} %get-tuple-element.35.refs_2_.v_in.v_ref, ...), custom_call_target="tpu_custom_call" | custom-call | flops 1000000 | bytes 3000000 | tf_op jit(solution)/shard_map/pallas_call | solution.py:629
  29.7 0.4 collective-permute-done.2.ya_ref
  30.1 1.6 %collective-permute-done.3.yb_ref = f32[22,8,128]{2,1,0:T(8,128)S(1)} collective-permute-done((f32[22,8,128]{2,1,0:T(8,128)S(1)}, f32[22,8,128]{2,1,0:T(8,128)S(1)}, u32[]{:S(2)}, u32[]{:S(2)}) %collective-permute-start.3) | collective-permute-done | bytes 90144 | tf_op jit(solution)/shard_map/ppermute | solution.py:649
  31.6 0.8 shard_map.62
  32.4 2.7 %collective-permute-start.4 = (f32[2,80,128]{2,1,0:T(8,128)S(1)}, f32[2,80,128]{2,1,0:T(8,128)S(1)}, u32[]{:S(2)}, u32[]{:S(2)}) collective-permute-start(f32[2,80,128]{2,1,0:T(8,128)S(1)} %get-tuple-element.45), channel_id=1, source_target_pairs={{0,1},{1,0},{2,3},{3,2},{4,5},{5,4},{6,7},{7,6},{8,9},{9,8},{10,11... | collective-permute-start | bytes 245768 | tf_op jit(solution)/shard_map/ppermute | solution.py:648
  35.2 0.0 collective-permute-start.5
  35.2 0.0 copy-start
  35.2 1.6 %copy-done = f32[64,8192]{1,0:T(8,128)S(1)} copy-done((f32[64,8192]{1,0:T(8,128)S(1)}, f32[64,8192]{1,0:T(8,128)}, u32[]{:S(2)}) %copy-start) | copy-done | bytes 2097176
  36.8 0.3 shard_map.63.amounts_ref
  37.0 0.0 collective-permute-done.4.za_ref
  37.1 2.3 %collective-permute-done.5.zb_ref = f32[2,80,128]{2,1,0:T(8,128)S(1)} collective-permute-done((f32[2,80,128]{2,1,0:T(8,128)S(1)}, f32[2,80,128]{2,1,0:T(8,128)S(1)}, u32[]{:S(2)}, u32[]{:S(2)}) %collective-permute-start.5) | collective-permute-done | bytes 81952 | tf_op jit(solution)/shard_map/ppermute | solution.py:649
  39.3 7.8 %shard_map.64 = (f32[8,64,128]{2,1,0:T(8,128)S(1)}, f32[7,64,128]{2,1,0:T(8,128)S(1)}, f32[7,64,128]{2,1,0:T(8,128)S(1)}, f32[2,10,80,128]{3,2,1,0:T(8,128)S(1)}...) custom-call(s32[3]{0:T(128)S(1)} %pad_add_fusion.pos, ...), custom_call_target="tpu_custom_call" | custom-call | tf_op jit(solution)/shard_map/pallas_call | solution.py:629
  47.2 0.4 collective-permute-start.6
  47.5 0.7 collective-permute-start.7
  48.2 5.1 %collective-permute-done.6.refs_1_.xa_ref = f32[7,64,128]{2,1,0:T(8,128)S(1)} collective-permute-done((f32[7,64,128]{2,1,0:T(8,128)S(1)}, f32[7,64,128]{2,1,0:T(8,128)S(1)}, u32[]{:S(2)}, u32[]{:S(2)}) %collective-permute-start.6) | collective-permute-done | bytes 229408 | tf_op jit(solution)/shard_map/ppermute | solution.py:648
  53.3 1.2 %collective-permute-done.7.refs_2_.xb_ref = f32[7,64,128]{2,1,0:T(8,128)S(1)} collective-permute-done((f32[7,64,128]{2,1,0:T(8,128)S(1)}, f32[7,64,128]{2,1,0:T(8,128)S(1)}, u32[]{:S(2)}, u32[]{:S(2)}) %collective-permute-start.7) | collective-permute-done | bytes 229408 | tf_op jit(solution)/shard_map/ppermute | solution.py:649
  54.6 0.6 shard_map.65
  55.1 0.1 collective-permute-start.8
  55.2 0.8 collective-permute-start.9
  56.0 0.9 shard_map.66
  56.9 1.2 %collective-permute-done.8.ya_ref = f32[13,8,128]{2,1,0:T(8,128)S(1)} collective-permute-done((f32[13,8,128]{2,1,0:T(8,128)S(1)}, f32[13,8,128]{2,1,0:T(8,128)S(1)}, u32[]{:S(2)}, u32[]{:S(2)}) %collective-permute-start.8) | collective-permute-done | bytes 53280 | tf_op jit(solution)/shard_map/ppermute | solution.py:648
  58.2 1.3 %collective-permute-done.9.yb_ref = f32[13,8,128]{2,1,0:T(8,128)S(1)} collective-permute-done((f32[13,8,128]{2,1,0:T(8,128)S(1)}, f32[13,8,128]{2,1,0:T(8,128)S(1)}, u32[]{:S(2)}, u32[]{:S(2)}) %collective-permute-start.9) | collective-permute-done | bytes 53280 | tf_op jit(solution)/shard_map/ppermute | solution.py:649
  59.5 0.7 shard_map.67
  60.2 3.7 %collective-permute-start.10 = (f32[1,80,128]{2,1,0:T(8,128)S(1)}, f32[1,80,128]{2,1,0:T(8,128)S(1)}, u32[]{:S(2)}, u32[]{:S(2)}) collective-permute-start(f32[1,80,128]{2,1,0:T(8,128)S(1)} %get-tuple-element.55), channel_id=1, source_target_pairs={{0,1},{1,0},{2,3},{3,2},{4,5},{5,4},{6,7},{7,6},{8,9},{9,8},{10,11... | collective-permute-start | bytes 122888 | tf_op jit(solution)/shard_map/ppermute | solution.py:648
  63.9 0.0 collective-permute-start.11
  63.9 0.0 copy-start.1
  63.9 0.6 shard_map.68.e_ref
  64.5 0.3 collective-permute-done.10.za_ref
  64.8 2.6 %collective-permute-done.11.zb_ref = f32[1,80,128]{2,1,0:T(8,128)S(1)} collective-permute-done((f32[1,80,128]{2,1,0:T(8,128)S(1)}, f32[1,80,128]{2,1,0:T(8,128)S(1)}, u32[]{:S(2)}, u32[]{:S(2)}) %collective-permute-start.11) | collective-permute-done | bytes 40992 | tf_op jit(solution)/shard_map/ppermute | solution.py:649
  67.3 8.3 %shard_map.69 = (f32[8,64,128]{2,1,0:T(8,128)S(1)}, f32[8,64,128]{2,1,0:T(8,128)S(1)}, f32[8,64,128]{2,1,0:T(8,128)S(1)}, f32[128,384]{1,0:T(8,128)S(1)}) custom-call(s32[3]{0:T(128)S(1)} %pad_add_fusion.pos, f32[8,64,128]{2,1,0:T(8,128)S(1)} %get-tuple-element.48.refs_0_.p_ref, f32[7,64,128]{2,1,0:T(8,128)S(1)} %collective-permute-done.6.refs_1_.xa_ref, ...), custom_call_target="tpu_custom_call" | custom-call | tf_op jit(solution)/shard_map/pallas_call | solution.py:629
  75.6 0.2 copy.7
  75.8 14.8 %all_to_all.35 = f32[128,1,384]{2,1,0:T(1,128)S(1)} all-to-all(f32[128,1,384]{2,1,0:T(1,128)S(1)} %copy.7), channel_id=1, replica_groups=mesh['gx'=4,'gy'=4,'gz'=8] {'gx','gy','gz'}, dimensions={0} | all-to-all | bytes 393216 | tf_op jit(solution)/shard_map/all_to_all | solution.py:654
  90.6 0.0 copy-done.1
  90.6 0.7 shard_map.70
  91.3 13.6 %all_to_all.36 = f32[128,1,128]{2,1,0:T(1,128)S(1)} all-to-all(f32[128,1,128]{2,1,0:T(1,128)S(1)} %bitcast.18), channel_id=1, replica_groups=mesh['gx'=4,'gy'=4,'gz'=8] {'gx','gy','gz'}, dimensions={0} | all-to-all | bytes 131072 | tf_op jit(solution)/shard_map/all_to_all | solution.py:654
  105.0 2.2 %shard_map.71 = (f32[8,64,128]{2,1,0:T(8,128)}, f32[8,64,128]{2,1,0:T(8,128)}) custom-call(s32[3]{0:T(128)S(1)} %pad_add_fusion.pos, f32[128,384]{1,0:T(8,128)S(1)} %bitcast.16, f32[128,128]{1,0:T(8,128)S(1)} %bitcast.17, f32[8,64,128]{2,1,0:T(8,128)S(1)} %get-tuple-element.48.refs_0_.p_ref, f32[8,64,128]{2,1,0:T(8,128)S(1)} %get-tuple-element.61.q_ref, ...), custom_call_target="tpu_custom_call" | custom-call | tf_op jit(solution)/shard_map/pallas_call | solution.py:629
  (1 shorter events, 0.0 us)
Async XLA Ops:
  3.6 22.4 %collective-permute-start = (f32[13,64,128]{2,1,0:T(8,128)S(1)}, f32[13,64,128]{2,1,0:T(8,128)S(1)}, u32[]{:S(2)}, u32[]{:S(2)}) collective-permute-start(f32[13,64,128]{2,1,0:T(8,128)S(1)} %get-tuple-element.36), channel_id=1, source_target_pairs={{0,32},{32,0},{64,96},{96,64},{1,33},{33,1},{65,97},{97,65},{2,34}... | collective-permute-start | bytes 1277960 | tf_op jit(solution)/shard_map/ppermute | solution.py:648
  5.7 20.3 %collective-permute-start.1 = (f32[13,64,128]{2,1,0:T(8,128)S(1)}, f32[13,64,128]{2,1,0:T(8,128)S(1)}, u32[]{:S(2)}, u32[]{:S(2)}) collective-permute-start(f32[13,64,128]{2,1,0:T(8,128)S(1)} %get-tuple-element.37), channel_id=1, source_target_pairs={{0,96},{32,64},{64,32},{96,0},{1,97},{33,65},{65,33},{97,1},{2,98}... | collective-permute-start | bytes 1277960 | tf_op jit(solution)/shard_map/ppermute | solution.py:649
  26.6 3.5 %collective-permute-start.2 = (f32[22,8,128]{2,1,0:T(8,128)S(1)}, f32[22,8,128]{2,1,0:T(8,128)S(1)}, u32[]{:S(2)}, u32[]{:S(2)}) collective-permute-start(f32[22,8,128]{2,1,0:T(8,128)S(1)} %get-tuple-element.41), channel_id=1, source_target_pairs={{0,8},{8,0},{16,24},{24,16},{1,9},{9,1},{17,25},{25,17},{2,10},{10... | collective-permute-start | bytes 270344 | tf_op jit(solution)/shard_map/ppermute | solution.py:648
  27.1 4.6 %collective-permute-start.3 = (f32[22,8,128]{2,1,0:T(8,128)S(1)}, f32[22,8,128]{2,1,0:T(8,128)S(1)}, u32[]{:S(2)}, u32[]{:S(2)}) collective-permute-start(f32[22,8,128]{2,1,0:T(8,128)S(1)} %get-tuple-element.42), channel_id=1, source_target_pairs={{0,24},{8,16},{16,8},{24,0},{1,25},{9,17},{17,9},{25,1},{2,26},{10... | collective-permute-start | bytes 270344 | tf_op jit(solution)/shard_map/ppermute | solution.py:649
  32.4 4.6 %collective-permute-start.4 = (f32[2,80,128]{2,1,0:T(8,128)S(1)}, f32[2,80,128]{2,1,0:T(8,128)S(1)}, u32[]{:S(2)}, u32[]{:S(2)}) collective-permute-start(f32[2,80,128]{2,1,0:T(8,128)S(1)} %get-tuple-element.45), channel_id=1, source_target_pairs={{0,1},{1,0},{2,3},{3,2},{4,5},{5,4},{6,7},{7,6},{8,9},{9,8},{10,11... | collective-permute-start | bytes 245768 | tf_op jit(solution)/shard_map/ppermute | solution.py:648
  35.2 4.2 %collective-permute-start.5 = (f32[2,80,128]{2,1,0:T(8,128)S(1)}, f32[2,80,128]{2,1,0:T(8,128)S(1)}, u32[]{:S(2)}, u32[]{:S(2)}) collective-permute-start(f32[2,80,128]{2,1,0:T(8,128)S(1)} %get-tuple-element.46), channel_id=1, source_target_pairs={{0,7},{1,2},{2,1},{3,4},{4,3},{5,6},{6,5},{7,0},{8,15},{9,10},{10,... | collective-permute-start | bytes 245768 | tf_op jit(solution)/shard_map/ppermute | solution.py:649
  35.2 1.6 %copy-start = (f32[64,8192]{1,0:T(8,128)S(1)}, f32[64,8192]{1,0:T(8,128)}, u32[]{:S(2)}) copy-start(f32[64,8192]{1,0:T(8,128)} %matrix_ref.3) | copy-start | bytes 6291460
  47.2 6.2 %collective-permute-start.6 = (f32[7,64,128]{2,1,0:T(8,128)S(1)}, f32[7,64,128]{2,1,0:T(8,128)S(1)}, u32[]{:S(2)}, u32[]{:S(2)}) collective-permute-start(f32[7,64,128]{2,1,0:T(8,128)S(1)} %get-tuple-element.49), channel_id=1, source_target_pairs={{0,32},{32,0},{64,96},{96,64},{1,33},{33,1},{65,97},{97,65},{2,34}... | collective-permute-start | bytes 688136 | tf_op jit(solution)/shard_map/ppermute | solution.py:648
  47.5 7.0 %collective-permute-start.7 = (f32[7,64,128]{2,1,0:T(8,128)S(1)}, f32[7,64,128]{2,1,0:T(8,128)S(1)}, u32[]{:S(2)}, u32[]{:S(2)}) collective-permute-start(f32[7,64,128]{2,1,0:T(8,128)S(1)} %get-tuple-element.50), channel_id=1, source_target_pairs={{0,96},{32,64},{64,32},{96,0},{1,97},{33,65},{65,33},{97,1},{2,98}... | collective-permute-start | bytes 688136 | tf_op jit(solution)/shard_map/ppermute | solution.py:649
  55.1 3.1 %collective-permute-start.8 = (f32[13,8,128]{2,1,0:T(8,128)S(1)}, f32[13,8,128]{2,1,0:T(8,128)S(1)}, u32[]{:S(2)}, u32[]{:S(2)}) collective-permute-start(f32[13,8,128]{2,1,0:T(8,128)S(1)} %get-tuple-element.51), channel_id=1, source_target_pairs={{0,8},{8,0},{16,24},{24,16},{1,9},{9,1},{17,25},{25,17},{2,10},{10... | collective-permute-start | bytes 159752 | tf_op jit(solution)/shard_map/ppermute | solution.py:648
  55.2 4.3 %collective-permute-start.9 = (f32[13,8,128]{2,1,0:T(8,128)S(1)}, f32[13,8,128]{2,1,0:T(8,128)S(1)}, u32[]{:S(2)}, u32[]{:S(2)}) collective-permute-start(f32[13,8,128]{2,1,0:T(8,128)S(1)} %get-tuple-element.52), channel_id=1, source_target_pairs={{0,24},{8,16},{16,8},{24,0},{1,25},{9,17},{17,9},{25,1},{2,26},{10... | collective-permute-start | bytes 159752 | tf_op jit(solution)/shard_map/ppermute | solution.py:649
  60.2 4.6 %collective-permute-start.10 = (f32[1,80,128]{2,1,0:T(8,128)S(1)}, f32[1,80,128]{2,1,0:T(8,128)S(1)}, u32[]{:S(2)}, u32[]{:S(2)}) collective-permute-start(f32[1,80,128]{2,1,0:T(8,128)S(1)} %get-tuple-element.55), channel_id=1, source_target_pairs={{0,1},{1,0},{2,3},{3,2},{4,5},{5,4},{6,7},{7,6},{8,9},{9,8},{10,11... | collective-permute-start | bytes 122888 | tf_op jit(solution)/shard_map/ppermute | solution.py:648
  63.9 3.4 %collective-permute-start.11 = (f32[1,80,128]{2,1,0:T(8,128)S(1)}, f32[1,80,128]{2,1,0:T(8,128)S(1)}, u32[]{:S(2)}, u32[]{:S(2)}) collective-permute-start(f32[1,80,128]{2,1,0:T(8,128)S(1)} %get-tuple-element.56), channel_id=1, source_target_pairs={{0,7},{1,2},{2,1},{3,4},{4,3},{5,6},{6,5},{7,0},{8,15},{9,10},{10,... | collective-permute-start | bytes 122888 | tf_op jit(solution)/shard_map/ppermute | solution.py:649
  63.9 26.7 %copy-start.1 = (f32[64,8192]{1,0:T(8,128)S(1)}, f32[64,8192]{1,0:T(8,128)}, u32[]{:S(2)}) copy-start(f32[64,8192]{1,0:T(8,128)} %matrix_ref.3) | copy-start | bytes 6291460

commit v6 on v5

--- a/solution.py
+++ b/solution.py
@@ -347,11 +347,13 @@
         ref[i, j] = value
 
 
-def chebyshev(halo, w_ref, rp_ref, a_ref, b_ref):
+def chebyshev(halo, w_ref, rp_ref, a_ref, b_ref, steps=(0, DEG - 1), into=None):
     _, weights = recurrence()
     now, before = a_ref, b_ref
-    for index, (keep, push) in enumerate(weights):
+    for index in range(*steps):
+        keep, push = weights[index]
         halo -= 1
+        out = into.pop(0) if into else before
         for i in range(HX - halo, HX + CX + halo):
             for j in range(ROWS):
                 around = around_strided(lambda i, j: now[i, j], i, j)
@@ -361,9 +363,9 @@
                 new = (1.0 + keep - push) * now[i, j] + push * total
                 if index:
                     new = new - keep * before[i, j]
-                store(before, i, j, new, halo)
-        now, before = before, now
-    return now
+                store(out, i, j, new, halo)
+        now, before = out, now
+    return now, before
 
 
 def smooth_kernel(
@@ -398,7 +400,7 @@
                 scaled = strided(wide_ref, i - HX + H_R, j) * inverse
                 store(rp_ref, i, j, scaled, H_R)
                 store(a_ref, i, j, scaled * first_scale, H_R)
-    result = chebyshev(H_R, w_ref, rp_ref, a_ref, b_ref)
+    result, _ = chebyshev(H_R, w_ref, rp_ref, a_ref, b_ref)
     for j in range(ROWS):
         for x in range(CX):
             nat_ref[x, pl.ds(j, 8, stride=ROWS), :] = result[HX + x, j, :, 0:CZ]
@@ -467,9 +469,9 @@
 
 
 def image_kernel(
-    pos, p_ref, xa_ref, xb_ref, ya_ref, yb_ref, za_ref, zb_ref, w_ref, diag_ref, r_ref, v_ref, e_ref,
-    q_ref, c_ref, y_ref, send_ref,
-    full_ref, plane_ref, rp_ref, a_ref, b_ref,
+    pos, p_ref, xa_ref, xb_ref, ya_ref, yb_ref, za_ref, zb_ref, w_ref, diag_ref,
+    q_ref, rp_ref, a_ref, b_ref,
+    full_ref, plane_ref,
 ):
     planes = padded_planes(p_ref, Pair(pos, 0, xa_ref, xb_ref))
     wide = Wide(planes, PLACES_2[0], pos, ya_ref, yb_ref, za_ref, zb_ref)
@@ -489,19 +491,30 @@
             store(a_ref, i, j, total * first_scale, HX - 1)
             if HX <= i < HX + CX:
                 plane_ref[i - HX, rows, :] = total[:, 0:CZ] * diag_ref[i - HX, j]
-    result = chebyshev(HX - 1, w_ref, rp_ref, a_ref, b_ref)
+    chebyshev(HX - 1, w_ref, rp_ref, a_ref, b_ref, (0, 2))
+    for x in range(CX):
+        q_ref[x] = plane_ref[x, HY : HY + CY]
+
+
+def smooth_image_kernel(
+    w_ref, diag_ref, rp_ref, a_ref, b_ref, p_ref, q_ref, r_ref, v_ref, e_ref,
+    c_ref, y_ref, send_ref,
+    plane_ref, one_ref, two_ref,
+):
+    result, _ = chebyshev(HX - 3, w_ref, rp_ref, a_ref, b_ref, (2, DEG - 1), [one_ref, two_ref])
     for x in range(CX):
         for j in range(ROWS):
             rows = pl.ds(j, 8, stride=ROWS)
             mine, image = image_of(result, w_ref, diag_ref, x, j)
-            plane_ref[CX + x, rows, :] = mine
-            plane_ref[2 * CX + x, rows, :] = image
+            plane_ref[x, rows, :] = mine
+            plane_ref[CX + x, rows, :] = image
     parts = [jnp.zeros((CY, CZ), F32) for _ in range(4)]
     energy = jnp.zeros((CY, CZ), F32)
     curve = jnp.zeros((CY, CZ), F32)
     for x in range(CX):
-        q, c, y = (plane_ref[CX * n + x, HY : HY + CY] for n in range(3))
-        q_ref[x], c_ref[x], y_ref[x] = q, c, y
+        q = q_ref[x]
+        c_ref[x] = plane_ref[x, HY : HY + CY]
+        y_ref[x] = plane_ref[CX + x, HY : HY + CY]
         energy = energy + r_ref[x] * p_ref[x]
         curve = curve + q * p_ref[x]
         parts[x // 2] = parts[x // 2] + v_ref[x] * q
@@ -692,12 +705,12 @@
     own = (p, *swap(xa, xb, "gx"))
     quads = call(product_kernel, (4, 128), scratch=[(16, PY, CZ)], cost=cost(1))(v_wide, w, diag)
     halos = exchange_yz(pos, own)
-    q, c, y, send = call(
-        image_kernel,
-        [block, block, block, (NDEV, 384)],
-        scratch=[tall, (3 * CX, PY, CZ), split, split, split],
-        smem=True,
-    )(pos, *own, *halos, w, diag, r, v, quads)
+    q, scaled, newest, older = call(
+        image_kernel, [block, split, split, split], scratch=[tall, (CX, PY, CZ)], smem=True
+    )(pos, *own, *halos, w, diag)
+    c, y, send = call(
+        smooth_image_kernel, [block, block, (NDEV, 384)], scratch=[(2 * CX, PY, CZ), split, split]
+    )(w, diag, scaled, newest, older, p, q, r, v, quads)
     sums = gather(send)
     send = call(amounts_kernel, (NDEV, 128), scratch=[(NDEV, 128)])(sums, coarse_inverse, p, q, c, y, v, r)
     got = gather(send)

time: 107 us -> 107 us (level)
  waiting for transfers between devices: 16 us -> 17.6 us
  local copies, waits for them, and re-layouts: 1.81 us -> 0.22 us
    unnamed x5 -> x3, local copies, waits for them, and re-layouts: 1.61 us -> 0.02 us
    pallas_call x13 -> x14, Pallas kernels: 25.5 us -> 25.4 us  [run(): pl.pallas_call(kernel, out_shape=[jax.ShapeDtypeStruct(s, F32) for s in o...]
  transfers between devices with their start and end apart: 12 -> 12, of which waited for: 9 -> 10; matrix products, arithmetic and copies ran while one was open for 0% -> 0% of each run, Pallas kernels for 3% -> 3%
where the time goes in v6:
time: 107 us
  blocking collectives  46.9 us (44%)
  Pallas kernels  25.4 us (24%)
  waiting for transfers between devices  17.6 us (16%)
  starting transfers between devices  14 us (13%)
  other arithmetic  2.15 us (2%)
    all_to_all x3, blocking collectives, gather(): return lax.all_to_all(rows, AXES, 0, 0, tiled=True)  46.9 us
    pallas_call x14, Pallas kernels, run(): pl.pallas_call(kernel, out_shape=[jax.ShapeDtypeStruct(s, F32) for s in o...  25.4 us
    ppermute x6, waiting for transfers between devices, swap(): lax.ppermute(b, axis, [(i, (i - 1 if i % 2 == 0 else i + 1) % count) for...  9.89 us
    ppermute x6, starting transfers between devices, swap(): got_a = lax.ppermute(a, axis, [(i, i ^ 1) for i in range(count)])  9.46 us
    ppermute x6, waiting for transfers between devices, swap(): got_a = lax.ppermute(a, axis, [(i, i ^ 1) for i in range(count)])  7.69 us
    ppermute x6, starting transfers between devices, swap(): lax.ppermute(b, axis, [(i, (i - 1 if i % 2 == 0 else i + 1) % count) for...  4.58 us
  transfers between devices with their start and end apart: 12, of which 10 were waited for; matrix products, arithmetic and copies ran while one was open for 0% of the time, Pallas kernels for 3%

profile of v6, /device:TPU:1, one launch (start us, length us, event | category | flops | bytes accessed | tf_op | source)
XLA Modules:
  0.0 107.0 jit_solution(8403231881314112362)
XLA Ops:
  0.6 1.0 compare_select_fusion
  1.6 0.1 pad_add_fusion.pos
  1.7 1.1 %pad_maximum_fusion.all_ref = f32[24,64,128]{2,1,0:T(8,128)S(1)} fusion(f32[8,64,128]{2,1,0:T(8,128)} %param.6, f32[8,64,128]{2,1,0:T(8,128)S(1)} %compare_select_fusion, f32[8,64,128]{2,1,0:T(8,128)} %param.4), kind=kLoop, calls=%fused_computation | loop fusion | flops 393216 | bytes 1572864 | tf_op jit(solution)/shard_map/concatenate | solution.py:692
  2.8 0.8 shard_map.59
  3.6 2.1 %collective-permute-start = (f32[13,64,128]{2,1,0:T(8,128)S(1)}, f32[13,64,128]{2,1,0:T(8,128)S(1)}, u32[]{:S(2)}, u32[]{:S(2)}) collective-permute-start(f32[13,64,128]{2,1,0:T(8,128)S(1)} %get-tuple-element.39), channel_id=1, source_target_pairs={{0,32},{32,0},{64,96},{96,64},{1,33},{33,1},{65,97},{97,65},{2,34}... | collective-permute-start | bytes 1277960 | tf_op jit(solution)/shard_map/ppermute | solution.py:661
  5.7 1.8 %collective-permute-start.1 = (f32[13,64,128]{2,1,0:T(8,128)S(1)}, f32[13,64,128]{2,1,0:T(8,128)S(1)}, u32[]{:S(2)}, u32[]{:S(2)}) collective-permute-start(f32[13,64,128]{2,1,0:T(8,128)S(1)} %get-tuple-element.40), channel_id=1, source_target_pairs={{0,96},{32,64},{64,32},{96,0},{1,97},{33,65},{65,33},{97,1},{2,98}... | collective-permute-start | bytes 1277960 | tf_op jit(solution)/shard_map/ppermute | solution.py:662
  7.5 18.5 %all_to_all.34 = f32[128,1,128]{2,1,0:T(1,128)S(1)} all-to-all(f32[128,1,128]{2,1,0:T(1,128)S(1)} %bitcast.21), channel_id=1, replica_groups=mesh['gx'=4,'gy'=4,'gz'=8] {'gx','gy','gz'}, dimensions={0} | all-to-all | bytes 131072 | tf_op jit(solution)/shard_map/all_to_all | solution.py:667
  26.0 0.0 collective-permute-done.refs_3_.xa_ref
  26.0 0.0 collective-permute-done.1.refs_4_.xb_ref
  26.0 0.0 copy-start
  26.0 0.6 shard_map.60
  26.6 0.4 collective-permute-start.2
  27.1 1.3 %collective-permute-start.3 = (f32[22,8,128]{2,1,0:T(8,128)S(1)}, f32[22,8,128]{2,1,0:T(8,128)S(1)}, u32[]{:S(2)}, u32[]{:S(2)}) collective-permute-start(f32[22,8,128]{2,1,0:T(8,128)S(1)} %get-tuple-element.45), channel_id=1, source_target_pairs={{0,24},{8,16},{16,8},{24,0},{1,25},{9,17},{17,9},{25,1},{2,26},{10... | collective-permute-start | bytes 270344 | tf_op jit(solution)/shard_map/ppermute | solution.py:662
  28.4 1.3 %shard_map.61 = (f32[2,64,128]{2,1,0:T(8,128)S(1)}, f32[2,64,128]{2,1,0:T(8,128)S(1)}) custom-call(s32[3]{0:T(128)S(1)} %pad_add_fusion.pos, f32[8,64,128]{2,1,0:T(8,128)S(1)} %get-tuple-element.36.refs_0_.r_ref, f32[8,64,128]{2,1,0:T(8,128)S(1)} %get-tuple-element.37.refs_1_.g_in, f32[8,64,128]{2,1,0:T(8,128)S(1)} %get-tuple-element.38.refs_2_.v_in.v_ref, ...), custom_call_target="tpu_custom_call" | custom-call | flops 1000000 | bytes 3000000 | tf_op jit(solution)/shard_map/pallas_call | solution.py:642
  29.7 0.4 collective-permute-done.2.ya_ref
  30.1 1.6 %collective-permute-done.3.yb_ref = f32[22,8,128]{2,1,0:T(8,128)S(1)} collective-permute-done((f32[22,8,128]{2,1,0:T(8,128)S(1)}, f32[22,8,128]{2,1,0:T(8,128)S(1)}, u32[]{:S(2)}, u32[]{:S(2)}) %collective-permute-start.3) | collective-permute-done | bytes 90144 | tf_op jit(solution)/shard_map/ppermute | solution.py:662
  31.7 0.8 shard_map.62
  32.4 2.7 %collective-permute-start.4 = (f32[2,80,128]{2,1,0:T(8,128)S(1)}, f32[2,80,128]{2,1,0:T(8,128)S(1)}, u32[]{:S(2)}, u32[]{:S(2)}) collective-permute-start(f32[2,80,128]{2,1,0:T(8,128)S(1)} %get-tuple-element.48), channel_id=1, source_target_pairs={{0,1},{1,0},{2,3},{3,2},{4,5},{5,4},{6,7},{7,6},{8,9},{9,8},{10,11... | collective-permute-start | bytes 245768 | tf_op jit(solution)/shard_map/ppermute | solution.py:661
  35.2 0.0 collective-permute-start.5
  35.2 0.0 copy-done
  35.2 0.3 shard_map.63.amounts_ref
  35.5 0.6 collective-permute-done.4.za_ref
  36.1 3.2 %collective-permute-done.5.zb_ref = f32[2,80,128]{2,1,0:T(8,128)S(1)} collective-permute-done((f32[2,80,128]{2,1,0:T(8,128)S(1)}, f32[2,80,128]{2,1,0:T(8,128)S(1)}, u32[]{:S(2)}, u32[]{:S(2)}) %collective-permute-start.5) | collective-permute-done | bytes 81952 | tf_op jit(solution)/shard_map/ppermute | solution.py:662
  39.3 7.8 %shard_map.64 = (f32[8,64,128]{2,1,0:T(8,128)S(1)}, f32[7,64,128]{2,1,0:T(8,128)S(1)}, f32[7,64,128]{2,1,0:T(8,128)S(1)}, f32[2,10,80,128]{3,2,1,0:T(8,128)S(1)}...) custom-call(s32[3]{0:T(128)S(1)} %pad_add_fusion.pos, ...), custom_call_target="tpu_custom_call" | custom-call | tf_op jit(solution)/shard_map/pallas_call | solution.py:642
  47.2 0.4 collective-permute-start.6
  47.5 0.7 collective-permute-start.7
  48.2 5.1 %collective-permute-done.6.refs_1_.xa_ref = f32[7,64,128]{2,1,0:T(8,128)S(1)} collective-permute-done((f32[7,64,128]{2,1,0:T(8,128)S(1)}, f32[7,64,128]{2,1,0:T(8,128)S(1)}, u32[]{:S(2)}, u32[]{:S(2)}) %collective-permute-start.6) | collective-permute-done | bytes 229408 | tf_op jit(solution)/shard_map/ppermute | solution.py:661
  53.3 1.2 %collective-permute-done.7.refs_2_.xb_ref = f32[7,64,128]{2,1,0:T(8,128)S(1)} collective-permute-done((f32[7,64,128]{2,1,0:T(8,128)S(1)}, f32[7,64,128]{2,1,0:T(8,128)S(1)}, u32[]{:S(2)}, u32[]{:S(2)}) %collective-permute-start.7) | collective-permute-done | bytes 229408 | tf_op jit(solution)/shard_map/ppermute | solution.py:662
  54.6 0.6 shard_map.65
  55.1 0.1 collective-permute-start.8
  55.2 0.8 collective-permute-start.9
  56.0 0.9 shard_map.66
  56.9 1.3 %collective-permute-done.8.ya_ref = f32[13,8,128]{2,1,0:T(8,128)S(1)} collective-permute-done((f32[13,8,128]{2,1,0:T(8,128)S(1)}, f32[13,8,128]{2,1,0:T(8,128)S(1)}, u32[]{:S(2)}, u32[]{:S(2)}) %collective-permute-start.8) | collective-permute-done | bytes 53280 | tf_op jit(solution)/shard_map/ppermute | solution.py:661
  58.2 1.3 %collective-permute-done.9.yb_ref = f32[13,8,128]{2,1,0:T(8,128)S(1)} collective-permute-done((f32[13,8,128]{2,1,0:T(8,128)S(1)}, f32[13,8,128]{2,1,0:T(8,128)S(1)}, u32[]{:S(2)}, u32[]{:S(2)}) %collective-permute-start.9) | collective-permute-done | bytes 53280 | tf_op jit(solution)/shard_map/ppermute | solution.py:662
  59.5 0.7 shard_map.67
  60.2 3.7 %collective-permute-start.10 = (f32[1,80,128]{2,1,0:T(8,128)S(1)}, f32[1,80,128]{2,1,0:T(8,128)S(1)}, u32[]{:S(2)}, u32[]{:S(2)}) collective-permute-start(f32[1,80,128]{2,1,0:T(8,128)S(1)} %get-tuple-element.60), channel_id=1, source_target_pairs={{0,1},{1,0},{2,3},{3,2},{4,5},{5,4},{6,7},{7,6},{8,9},{9,8},{10,11... | collective-permute-start | bytes 122888 | tf_op jit(solution)/shard_map/ppermute | solution.py:661
  63.9 0.0 collective-permute-start.11
  63.9 0.6 shard_map.69.e_ref
  64.5 0.3 collective-permute-done.10.za_ref
  64.8 2.6 %collective-permute-done.11.zb_ref = f32[1,80,128]{2,1,0:T(8,128)S(1)} collective-permute-done((f32[1,80,128]{2,1,0:T(8,128)S(1)}, f32[1,80,128]{2,1,0:T(8,128)S(1)}, u32[]{:S(2)}, u32[]{:S(2)}) %collective-permute-start.11) | collective-permute-done | bytes 40992 | tf_op jit(solution)/shard_map/ppermute | solution.py:662
  67.3 4.9 %shard_map.68 = (f32[8,64,128]{2,1,0:T(8,128)S(1)}, f32[22,10,8,256]{3,2,1,0:T(8,128)S(1)}, f32[22,10,8,256]{3,2,1,0:T(8,128)S(1)}, f32[22,10,8,256]{3,2,1,0:T(8,128)S(1)}) custom-call(s32[3]{0:T(128)S(1)} %pad_add_fusion.pos, f32[8,64,128]{2,1,0:T(8,128)S(1)} %get-tuple-element.53.refs_0_.p_ref, f32[7,64,128]{2,1,0:T(8,128)S(1)} %collective-permute-done.6.refs_1_.xa_ref, ...), custom_call_target="tpu_custom_call" | custom-call | tf_op jit(solution)/shard_map/pallas_call | solution.py:642
  72.2 3.2 %shard_map.70 = (f32[8,64,128]{2,1,0:T(8,128)S(1)}, f32[8,64,128]{2,1,0:T(8,128)S(1)}, f32[128,384]{1,0:T(8,128)S(1)}) custom-call(f32[6,22,10,8,256]{4,3,2,1,0:T(8,128)S(1)} %get-tuple-element.51.w_ref, f32[8,10,8,128]{3,2,1,0:T(8,128)S(1)} %get-tuple-element.52.diag_ref, f32[22,10,8,256]{3,2,1,0:T(8,128)S(1)} %get-tuple-element.62.rp_ref, ...), custom_call_target="tpu_custom_call" | custom-call | tf_op jit(solution)/shard_map/pallas_call | solution.py:642
  75.5 0.2 copy.7
  75.7 14.8 %all_to_all.35 = f32[128,1,384]{2,1,0:T(1,128)S(1)} all-to-all(f32[128,1,384]{2,1,0:T(1,128)S(1)} %copy.7), channel_id=1, replica_groups=mesh['gx'=4,'gy'=4,'gz'=8] {'gx','gy','gz'}, dimensions={0} | all-to-all | bytes 393216 | tf_op jit(solution)/shard_map/all_to_all | solution.py:667
  90.5 0.7 shard_map.71
  91.2 13.6 %all_to_all.36 = f32[128,1,128]{2,1,0:T(1,128)S(1)} all-to-all(f32[128,1,128]{2,1,0:T(1,128)S(1)} %bitcast.18), channel_id=1, replica_groups=mesh['gx'=4,'gy'=4,'gz'=8] {'gx','gy','gz'}, dimensions={0} | all-to-all | bytes 131072 | tf_op jit(solution)/shard_map/all_to_all | solution.py:667
  104.8 2.2 %shard_map.72 = (f32[8,64,128]{2,1,0:T(8,128)}, f32[8,64,128]{2,1,0:T(8,128)}) custom-call(s32[3]{0:T(128)S(1)} %pad_add_fusion.pos, f32[128,384]{1,0:T(8,128)S(1)} %bitcast.16, f32[128,128]{1,0:T(8,128)S(1)} %bitcast.17, f32[8,64,128]{2,1,0:T(8,128)S(1)} %get-tuple-element.53.refs_0_.p_ref, f32[8,64,128]{2,1,0:T(8,128)S(1)} %get-tuple-element.65.q_ref, ...), custom_call_target="tpu_custom_call" | custom-call | tf_op jit(solution)/shard_map/pallas_call | solution.py:642
  (1 shorter events, 0.0 us)
Async XLA Ops:
  3.6 22.4 %collective-permute-start = (f32[13,64,128]{2,1,0:T(8,128)S(1)}, f32[13,64,128]{2,1,0:T(8,128)S(1)}, u32[]{:S(2)}, u32[]{:S(2)}) collective-permute-start(f32[13,64,128]{2,1,0:T(8,128)S(1)} %get-tuple-element.39), channel_id=1, source_target_pairs={{0,32},{32,0},{64,96},{96,64},{1,33},{33,1},{65,97},{97,65},{2,34}... | collective-permute-start | bytes 1277960 | tf_op jit(solution)/shard_map/ppermute | solution.py:661
  5.7 20.3 %collective-permute-start.1 = (f32[13,64,128]{2,1,0:T(8,128)S(1)}, f32[13,64,128]{2,1,0:T(8,128)S(1)}, u32[]{:S(2)}, u32[]{:S(2)}) collective-permute-start(f32[13,64,128]{2,1,0:T(8,128)S(1)} %get-tuple-element.40), channel_id=1, source_target_pairs={{0,96},{32,64},{64,32},{96,0},{1,97},{33,65},{65,33},{97,1},{2,98}... | collective-permute-start | bytes 1277960 | tf_op jit(solution)/shard_map/ppermute | solution.py:662
  26.0 9.1 %copy-start = (f32[64,8192]{1,0:T(8,128)S(1)}, f32[64,8192]{1,0:T(8,128)}, u32[]{:S(2)}) copy-start(f32[64,8192]{1,0:T(8,128)} %matrix_ref.3) | copy-start | bytes 6291460
  26.6 3.5 %collective-permute-start.2 = (f32[22,8,128]{2,1,0:T(8,128)S(1)}, f32[22,8,128]{2,1,0:T(8,128)S(1)}, u32[]{:S(2)}, u32[]{:S(2)}) collective-permute-start(f32[22,8,128]{2,1,0:T(8,128)S(1)} %get-tuple-element.44), channel_id=1, source_target_pairs={{0,8},{8,0},{16,24},{24,16},{1,9},{9,1},{17,25},{25,17},{2,10},{10... | collective-permute-start | bytes 270344 | tf_op jit(solution)/shard_map/ppermute | solution.py:661
  27.1 4.6 %collective-permute-start.3 = (f32[22,8,128]{2,1,0:T(8,128)S(1)}, f32[22,8,128]{2,1,0:T(8,128)S(1)}, u32[]{:S(2)}, u32[]{:S(2)}) collective-permute-start(f32[22,8,128]{2,1,0:T(8,128)S(1)} %get-tuple-element.45), channel_id=1, source_target_pairs={{0,24},{8,16},{16,8},{24,0},{1,25},{9,17},{17,9},{25,1},{2,26},{10... | collective-permute-start | bytes 270344 | tf_op jit(solution)/shard_map/ppermute | solution.py:662
  32.4 3.7 %collective-permute-start.4 = (f32[2,80,128]{2,1,0:T(8,128)S(1)}, f32[2,80,128]{2,1,0:T(8,128)S(1)}, u32[]{:S(2)}, u32[]{:S(2)}) collective-permute-start(f32[2,80,128]{2,1,0:T(8,128)S(1)} %get-tuple-element.48), channel_id=1, source_target_pairs={{0,1},{1,0},{2,3},{3,2},{4,5},{5,4},{6,7},{7,6},{8,9},{9,8},{10,11... | collective-permute-start | bytes 245768 | tf_op jit(solution)/shard_map/ppermute | solution.py:661
  35.2 4.2 %collective-permute-start.5 = (f32[2,80,128]{2,1,0:T(8,128)S(1)}, f32[2,80,128]{2,1,0:T(8,128)S(1)}, u32[]{:S(2)}, u32[]{:S(2)}) collective-permute-start(f32[2,80,128]{2,1,0:T(8,128)S(1)} %get-tuple-element.49), channel_id=1, source_target_pairs={{0,7},{1,2},{2,1},{3,4},{4,3},{5,6},{6,5},{7,0},{8,15},{9,10},{10,... | collective-permute-start | bytes 245768 | tf_op jit(solution)/shard_map/ppermute | solution.py:662
  47.2 6.2 %collective-permute-start.6 = (f32[7,64,128]{2,1,0:T(8,128)S(1)}, f32[7,64,128]{2,1,0:T(8,128)S(1)}, u32[]{:S(2)}, u32[]{:S(2)}) collective-permute-start(f32[7,64,128]{2,1,0:T(8,128)S(1)} %get-tuple-element.54), channel_id=1, source_target_pairs={{0,32},{32,0},{64,96},{96,64},{1,33},{33,1},{65,97},{97,65},{2,34}... | collective-permute-start | bytes 688136 | tf_op jit(solution)/shard_map/ppermute | solution.py:661
  47.5 7.0 %collective-permute-start.7 = (f32[7,64,128]{2,1,0:T(8,128)S(1)}, f32[7,64,128]{2,1,0:T(8,128)S(1)}, u32[]{:S(2)}, u32[]{:S(2)}) collective-permute-start(f32[7,64,128]{2,1,0:T(8,128)S(1)} %get-tuple-element.55), channel_id=1, source_target_pairs={{0,96},{32,64},{64,32},{96,0},{1,97},{33,65},{65,33},{97,1},{2,98}... | collective-permute-start | bytes 688136 | tf_op jit(solution)/shard_map/ppermute | solution.py:662
  55.1 3.1 %collective-permute-start.8 = (f32[13,8,128]{2,1,0:T(8,128)S(1)}, f32[13,8,128]{2,1,0:T(8,128)S(1)}, u32[]{:S(2)}, u32[]{:S(2)}) collective-permute-start(f32[13,8,128]{2,1,0:T(8,128)S(1)} %get-tuple-element.56), channel_id=1, source_target_pairs={{0,8},{8,0},{16,24},{24,16},{1,9},{9,1},{17,25},{25,17},{2,10},{10... | collective-permute-start | bytes 159752 | tf_op jit(solution)/shard_map/ppermute | solution.py:661
  55.2 4.3 %collective-permute-start.9 = (f32[13,8,128]{2,1,0:T(8,128)S(1)}, f32[13,8,128]{2,1,0:T(8,128)S(1)}, u32[]{:S(2)}, u32[]{:S(2)}) collective-permute-start(f32[13,8,128]{2,1,0:T(8,128)S(1)} %get-tuple-element.57), channel_id=1, source_target_pairs={{0,24},{8,16},{16,8},{24,0},{1,25},{9,17},{17,9},{25,1},{2,26},{10... | collective-permute-start | bytes 159752 | tf_op jit(solution)/shard_map/ppermute | solution.py:662
  60.2 4.6 %collective-permute-start.10 = (f32[1,80,128]{2,1,0:T(8,128)S(1)}, f32[1,80,128]{2,1,0:T(8,128)S(1)}, u32[]{:S(2)}, u32[]{:S(2)}) collective-permute-start(f32[1,80,128]{2,1,0:T(8,128)S(1)} %get-tuple-element.60), channel_id=1, source_target_pairs={{0,1},{1,0},{2,3},{3,2},{4,5},{5,4},{6,7},{7,6},{8,9},{9,8},{10,11... | collective-permute-start | bytes 122888 | tf_op jit(solution)/shard_map/ppermute | solution.py:661
  63.9 3.4 %collective-permute-start.11 = (f32[1,80,128]{2,1,0:T(8,128)S(1)}, f32[1,80,128]{2,1,0:T(8,128)S(1)}, u32[]{:S(2)}, u32[]{:S(2)}) collective-permute-start(f32[1,80,128]{2,1,0:T(8,128)S(1)} %get-tuple-element.61), channel_id=1, source_target_pairs={{0,7},{1,2},{2,1},{3,4},{4,3},{5,6},{6,5},{7,0},{8,15},{9,10},{10,... | collective-permute-start | bytes 122888 | tf_op jit(solution)/shard_map/ppermute | solution.py:662
